TPU v7x, 256 devices: a whole 4x4x8 slice. The times are simulated.
256 devices in a mesh: seq: 32 (over z, x), batch: 8 (over y, core).
Axes of the slice: x: 4, y: 4, z: 8, core: 2. Of those that a mesh axis runs over, the one named last changes fastest.
Arguments:
- inputs: bfloat16 [16, 2048, 256], P('batch', 'seq'), may hold values from -6 to 6
- w_in: bfloat16 [256, 192], replicated, may hold values from -0.375 to 0.375
- u_rec: float32 [64, 192], replicated, may hold values from -0.375 to 0.375
- timescale: float32 [64], replicated, may hold values from 4 to 16384
- other_bias: float32 [3, 64], replicated, may hold values from -3 to 3
- h_init: float32 [64, 16], P(None, 'batch'), may hold values from -6 to 6
- cotangent: float32 [64, 16, 2048], P(None, 'batch', 'seq'), may hold values from -0.0625 to 0.0625
Outputs:
- states: float32 [64, 16, 2048], P(None, 'batch', 'seq')
- grad_in: float32 [256, 192], replicated
- grad_rec: float32 [64, 192], replicated
- grad_timescale: float32 [64], replicated
- grad_other: float32 [3, 64], replicated
All inputs are finite; a program needn't handle non-finite values.
Results may differ from a plain program's by a relative error of at most 0.00045.
Values sent between devices are 32-bit elements; how exact they have to be, the bound alone decides.
No kernel may reach another device: no remote copies, remote signals or barrier semaphores. Data moves between devices by JAX's collectives and lax.ppermute only.
A program may use at most 128 MiB of HBM per device.

v0:
```python
import functools

import jax
import jax.numpy as jnp
from jax import lax
from jax.experimental import pallas as pl
from jax.experimental.pallas import tpu as pltpu
from jax.sharding import PartitionSpec as P

NEWTON = 3
H = 64
LANES = 128
CHUNKS = 8
STEPS = 8
COLS = H + 1
ROWS = COLS * CHUNKS
BLOCK = 13
MAP = 40
PART = 200
F32 = jnp.float32
BF16 = jnp.bfloat16
VMEM = pltpu.VMEM
SMEM = pltpu.SMEM


def split(value):
    high = value.astype(BF16)
    return high, (value - high.astype(F32)).astype(BF16)


def mm(left, right):
    return jnp.dot(left, right, preferred_element_type=F32)


def mm_nt(left, right):
    return lax.dot_general(left, right, (((1,), (1,)), ((), ())), preferred_element_type=F32)


def mm_tn(left, right):
    return lax.dot_general(left, right, (((0,), (0,)), ((), ())), preferred_element_type=F32)


def left3(value):
    high, low = split(value)
    return jnp.concatenate([high, low, high], axis=1)


def right3(value):
    high, low = split(value)
    return jnp.concatenate([high, high, low], axis=0)


def lane_low(shape):
    return lax.broadcasted_iota(jnp.int32, shape, 1) < H


def swap_halves(value):
    return jnp.concatenate([value[:, H:], value[:, :H]], axis=1)


def doubled(value, half):
    low = lane_low(value.shape)
    other = swap_halves(value)
    return jnp.where(low, value, other) if half == 0 else jnp.where(low, other, value)


def right_doubled(matrix):
    high, low = split(matrix)
    return jnp.concatenate([high, low, high, low], axis=0)


def left_doubled(value):
    high, low = split(value)
    return jnp.concatenate([high, low], axis=1)


def block_diagonal(matrix):
    low = lane_low(matrix.shape)
    return jnp.concatenate([jnp.where(low, matrix, 0.0), jnp.where(low, 0.0, matrix)], axis=0)


def weights_kernel(u_ref, scale_ref, other_ref, w3_ref, uth_ref, utl_ref, ud_ref, bias_ref):
    zero = jnp.zeros((H, H), F32)
    for g in range(3):
        block = u_ref[:, g * H : (g + 1) * H]
        ud_ref[g] = jnp.concatenate([block, block], axis=1)
        diag = jnp.concatenate(
            [jnp.concatenate([block, zero], axis=1), jnp.concatenate([zero, block], axis=1)], axis=0
        )
        at = slice(g * LANES, (g + 1) * LANES)
        high, low = split(diag)
        w3_ref[0:LANES, at] = high
        w3_ref[LANES : 2 * LANES, at] = high
        w3_ref[2 * LANES : 3 * LANES, at] = low
        high, low = split(diag.T)
        uth_ref[at, :] = high
        utl_ref[at, :] = low
    rows = [jnp.log(scale_ref[...]), other_ref[0:1, :], other_ref[1:2, :], other_ref[2:3, :]]
    rows = [jnp.concatenate([row, row], axis=1) for row in rows]
    bias_ref[...] = jnp.concatenate(rows + [jnp.zeros((4, LANES), F32)], axis=0)


def pack_kernel(where_ref, x_ref, cot_ref, h_ref, out_ref):
    odd = where_ref[0]
    zero = jnp.zeros((H, H), F32)
    for m in range(2):
        first = odd == m
        x = jnp.where(first, x_ref[0].astype(F32), x_ref[1].astype(F32))
        out_ref[m, 0:64, :] = x[:, :LANES]
        out_ref[m, 64:128, :] = x[:, LANES:]
        cot = jnp.where(first, cot_ref[0], cot_ref[1])
        low = jnp.concatenate([cot, zero], axis=1)
        high = jnp.concatenate([zero, cot], axis=1)
        out_ref[m, 128:192, :] = jnp.where(odd == 0, low, high)
        start = jnp.where(first, h_ref[0:1, :], h_ref[1:2, :])
        start = jnp.concatenate([start, start], axis=1)
        out_ref[m, 192:200, :] = jnp.broadcast_to(start, (8, LANES))


def coefficients(prev, x3, bias, w3):
    mixed = mm(left3(prev), w3)
    mz, mr, mn = mixed[:, :LANES], mixed[:, LANES : 2 * LANES], mixed[:, 2 * LANES :]
    update = jax.nn.sigmoid(x3[0] + mz)
    reset = jax.nn.sigmoid(x3[1] + mr)
    recur = mn + bias[3:4, :]
    cand = jnp.tanh(x3[2] + reset * recur)
    fresh = (1.0 - update) * cand + update * prev
    slope = (1.0 - update) * (1.0 - cand * cand)
    cz = (prev - cand) * update * (1.0 - update)
    cr = slope * recur * reset * (1.0 - reset)
    cn = slope * reset
    offset = fresh - (update * prev + cz * mz + cr * mr + cn * mn)
    return update, cz, cr, cn, slope, offset


def scan_maps(coef, w3_ref, ud_ref, maps_ref):
    update, cz, cr, cn, _, offset = coef
    shape = (BLOCK, CHUNKS, LANES)
    for j in range(STEPS):
        at = slice(j * CHUNKS, (j + 1) * CHUNKS)
        up_j, cz_j, cr_j, cn_j = (a[at][None] for a in (update, cz, cr, cn))
        for b in range(COLS // BLOCK):
            rows = slice(b * BLOCK * CHUNKS, (b + 1) * BLOCK * CHUNKS)
            last = b == COLS // BLOCK - 1
            if j == 0:
                real = BLOCK - 1 if last else BLOCK
                cols = slice(b * BLOCK, b * BLOCK + real)
                k = lax.broadcasted_iota(jnp.int32, (real, CHUNKS, LANES), 0) + b * BLOCK
                lane = lax.broadcasted_iota(jnp.int32, (real, CHUNKS, LANES), 2) % H
                new = jnp.where(k == lane, up_j, 0.0)
                for c, g in ((cz_j, 0), (cr_j, 1), (cn_j, 2)):
                    new = new + c * ud_ref[g, cols, :][:, None, :]
                if last:
                    new = jnp.concatenate([new, offset[at][None]], axis=0)
            else:
                old = maps_ref[j - 1, rows, :]
                prod = mm(left3(old), w3_ref[...]).reshape(BLOCK, CHUNKS, 3 * LANES)
                new = (
                    up_j * old.reshape(shape)
                    + cz_j * prod[..., :LANES]
                    + cr_j * prod[..., LANES : 2 * LANES]
                    + cn_j * prod[..., 2 * LANES :]
                )
                if last:
                    new = jnp.concatenate([new[: BLOCK - 1], new[BLOCK - 1 :] + offset[at][None]], axis=0)
            maps_ref[j, rows, :] = new.reshape(BLOCK * CHUNKS, LANES)


def chunk_matrix(maps_ref, c):
    return maps_ref[STEPS - 1, pl.ds(c, H, stride=CHUNKS), :]


def chain_chunks(maps_ref, prefix_ref):
    row = lax.broadcasted_iota(jnp.int32, (72, LANES), 0)
    total = None
    for c in range(CHUNKS):
        matrix = chunk_matrix(maps_ref, c)
        vector = maps_ref[STEPS - 1, H * CHUNKS + c : H * CHUNKS + c + 1, :]
        if c == 0:
            total = jnp.concatenate([matrix, vector, jnp.zeros((7, LANES), F32)], axis=0)
        else:
            total = mm(left3(total), right3(block_diagonal(matrix)))
            total = total + jnp.where(row == H, vector, 0.0)
        prefix_ref[c] = total
    return total


def join_halves(total):
    row = lax.broadcasted_iota(jnp.int32, (72, LANES), 0)
    second = doubled(total, 1)
    both = mm(left_doubled(doubled(total, 0)), right_doubled(second[:H]))
    return both + jnp.where(row == H, second, 0.0)


def send_map(total, out_ref):
    low = lane_low((H // 2, LANES))
    packed = jnp.where(low, total[: H // 2], total[H // 2 : H])
    for z in range(out_ref.shape[0]):
        out_ref[z, : H // 2, :] = packed
        out_ref[z, H // 2 :, :] = total[H:]


def unpack_map(packed):
    body = packed[: H // 2]
    other = swap_halves(body)
    low = lane_low(body.shape)
    matrix = jnp.concatenate([jnp.where(low, body, other), jnp.where(low, other, body)], axis=0)
    return matrix, packed[H // 2 : H // 2 + 1]


def apply_row(state, matrix, vector):
    return mm(left_doubled(state), right_doubled(matrix)) + vector


def enter_device(where_ref, own_ref, other_ref, start, reverse):
    core, mine = where_ref[1], where_ref[2]
    planes = own_ref.shape[0]
    state = start
    order = list(range(2 * planes))
    for n in reversed(order) if reverse else order:
        z, kappa = n // 2, n % 2
        packed = jnp.where(core == kappa, own_ref[z], other_ref[z])
        fresh = apply_row(state, *unpack_map(packed))
        reached = (mine < n) if reverse else (mine > n)
        state = jnp.where(reached, fresh, state)
    return state


def spread(rows, count):
    k = lax.broadcasted_iota(jnp.int32, (count,) + rows.shape, 0)
    lane = lax.broadcasted_iota(jnp.int32, (count,) + rows.shape, 2) % H
    picked = jnp.where(k == lane, rows[None], 0.0).reshape(count * rows.shape[0], LANES)
    one = (
        lax.broadcasted_iota(jnp.int32, (LANES, LANES), 0) // H
        == lax.broadcasted_iota(jnp.int32, (LANES, LANES), 1) // H
    )
    one = jnp.where(one, 1.0, 0.0).astype(BF16)
    high, low = split(picked)
    rest = (picked - high.astype(F32) - low.astype(F32)).astype(BF16)
    return mm(jnp.concatenate([high, low, rest], axis=1), jnp.concatenate([one, one, one], axis=0))


def enter_chunks(state, prefix_ref):
    low = lane_low((CHUNKS, LANES))
    ends = prefix_ref[CHUNKS - 1]
    first = doubled(ends, 0)
    middle = apply_row(state, first[:H], first[H : H + 1])
    halves = jnp.where(low, state, middle)
    column = spread(halves[0:1], H)
    row = lax.broadcasted_iota(jnp.int32, (CHUNKS, LANES), 0)
    entering = halves
    for c in range(1, CHUNKS):
        before = prefix_ref[c - 1]
        value = jnp.sum(before[:H] * column, axis=0, keepdims=True) + before[H : H + 1]
        entering = jnp.where(row == c, value, entering)
    return entering


def trajectory(entering, maps_ref, spread_ref):
    spread_ref[...] = spread(entering, H)
    states = [maps_ref[j, H * CHUNKS :, :] for j in range(STEPS)]
    for b in range(0, H * CHUNKS, 64):
        factor = spread_ref[b : b + 64, :].reshape(8, CHUNKS, LANES)
        for j in range(STEPS):
            block = maps_ref[j, b : b + 64, :].reshape(8, CHUNKS, LANES)
            states[j] = states[j] + jnp.sum(block * factor, axis=0)
    return states


def phase(prev, x3_ref, bias_ref, w3_ref, ud_ref, maps_ref, prefix_ref, out_ref):
    coef = coefficients(prev, x3_ref, bias_ref[...], w3_ref[...])
    scan_maps(coef, w3_ref, ud_ref, maps_ref)
    total = chain_chunks(maps_ref, prefix_ref)
    send_map(join_halves(total), out_ref)


def first_kernel(
    where_ref, a_ref, b_ref, w_ref, w3_ref, ud_ref, bias_ref,
    x3_ref, xin_ref, cot_ref, start_ref, maps_ref, prefix_ref, out_ref,
):
    odd, mine = where_ref[0], where_ref[2]
    pieces = []
    for v in range(2):
        for j in range(STEPS):
            rows = [
                jnp.where(odd == v, a_ref[pl.ds(o + j, 8, stride=8), :], b_ref[pl.ds(o + j, 8, stride=8), :])
                for o in (0, 64)
            ]
            pieces.append(jnp.concatenate(rows, axis=1))
    xin = jnp.concatenate(pieces, axis=0).astype(BF16)
    xin_ref[...] = xin
    cot_ref[...] = jnp.concatenate(
        [a_ref[pl.ds(128 + j, 8, stride=8), :] + b_ref[pl.ds(128 + j, 8, stride=8), :] for j in range(STEPS)],
        axis=0,
    )
    start = a_ref[192:200, :]
    start_ref[...] = start
    flat = mm(xin, w_ref[...])
    bias = bias_ref[...]
    for g in range(3):
        cols = slice(g * H, (g + 1) * H)
        x3_ref[g] = jnp.concatenate([flat[:64, cols], flat[64:, cols]], axis=1) + bias[g : g + 1, :]
    row = lax.broadcasted_iota(jnp.int32, (64, LANES), 0)
    lane = lax.broadcasted_iota(jnp.int32, (64, LANES), 1)
    here = (row == 0) & (lane < H) & (mine == 0)
    prev = jnp.where(here, start[0:1, :], 0.0)
    phase(prev, x3_ref, bias_ref, w3_ref, ud_ref, maps_ref, prefix_ref, out_ref)


def next_kernel(
    where_ref, own_ref, other_ref, start_ref, x3_ref, bias_ref, w3_ref, ud_ref, old_ref, before_ref,
    maps_ref, prefix_ref, out_ref, spread_ref,
):
    state = enter_device(where_ref, own_ref, other_ref, start_ref[...], False)
    entering = enter_chunks(state, before_ref)
    states = trajectory(entering, old_ref, spread_ref)
    prev = jnp.concatenate([entering] + states[:-1], axis=0)
    phase(prev, x3_ref, bias_ref, w3_ref, ud_ref, maps_ref, prefix_ref, out_ref)


def half_sums(value):
    row = lax.broadcasted_iota(jnp.int32, (8, LANES), 0)
    low = lane_low((8, LANES))
    pick = jnp.where((row == 0) & low, 1.0, 0.0) + jnp.where((row == 1) & ~low, 1.0, 0.0)
    pick = pick.astype(BF16)
    return mm_nt(jnp.concatenate([pick, pick], axis=1), left_doubled(value))


def turn_kernel(
    where_ref, own_ref, other_ref, start_ref, x3_ref, bias_ref, w3_ref, ud_ref, old_ref, before_ref, cot_ref,
    states_ref, coef_ref, chunk_ref, vector_ref, half_ref, out_ref, spread_ref, maps_ref, prefix_ref, acc_ref,
):
    state = enter_device(where_ref, own_ref, other_ref, start_ref[...], False)
    entering = enter_chunks(state, before_ref)
    states = trajectory(entering, old_ref, spread_ref)
    for j in range(STEPS):
        states_ref[pl.ds(j, CHUNKS, stride=STEPS), :] = states[j]
    prev = jnp.concatenate([entering] + states[:-1], axis=0)
    coef = coefficients(prev, x3_ref, bias_ref[...], w3_ref[...])
    coef_ref[0] = prev
    for n in range(5):
        coef_ref[n + 1] = coef[n]
    scan_maps(coef, w3_ref, ud_ref, maps_ref)
    total = chain_chunks(maps_ref, prefix_ref)
    for b in range(0, H * CHUNKS, 64):
        acc = jnp.zeros((8, CHUNKS, LANES), F32)
        for j in range(STEPS):
            block = maps_ref[j, b : b + 64, :].reshape(8, CHUNKS, LANES)
            acc = acc + block * cot_ref[j * CHUNKS : (j + 1) * CHUNKS, :][None]
        acc_ref[b : b + 64, :] = acc.reshape(64, LANES)
    vectors = []
    for c in range(CHUNKS):
        chunk_ref[c] = chunk_matrix(maps_ref, c)
        sums = half_sums(acc_ref[pl.ds(c, H, stride=CHUNKS), :])
        vectors.append(jnp.concatenate([sums[0:1], sums[1:2]], axis=1))
    vector_ref[...] = jnp.concatenate(vectors, axis=0)
    whole = jnp.zeros((H, LANES), F32)
    for c in range(1, CHUNKS):
        whole = whole + prefix_ref[c - 1][:H] * vectors[c]
    sums = half_sums(whole)
    ends = jnp.concatenate([sums[0:1], sums[1:2]], axis=1) + vectors[0]
    tail = doubled(ends, 1)
    low = lane_low((H, LANES))
    sums = half_sums(jnp.where(low, total[:H], 0.0) * tail)
    left = ends[:, :H] + sums[0:1]
    both = join_halves(total)
    square = jnp.transpose(both[:H])[:H]
    flipped = jnp.concatenate([square, square], axis=1)
    pad = jnp.zeros((7, LANES), F32)
    send_map(jnp.concatenate([flipped, jnp.concatenate([left, left], axis=1), pad], axis=0), out_ref)
    later = jnp.transpose(total[:H])[H:]
    half_ref[...] = jnp.concatenate([jnp.concatenate([later, later], axis=1), tail, pad], axis=0)


def gradient_kernel(
    where_ref, own_ref, other_ref, coef_ref, chunk_ref, vector_ref, half_ref, cot_ref, uth_ref, utl_ref,
    xin_ref, bias_ref, scale_ref, out_ref,
):
    low = lane_low((CHUNKS, LANES))
    row = lax.broadcasted_iota(jnp.int32, (CHUNKS, LANES), 0)
    right = enter_device(where_ref, own_ref, other_ref, jnp.zeros((CHUNKS, LANES), F32), True)
    half = half_ref[...]
    middle = apply_row(right, half[:H], half[H : H + 1])
    value = jnp.where(low, middle, right)
    passed = value
    for c in reversed(range(1, CHUNKS)):
        high, low_part = split(block_diagonal(chunk_ref[c]))
        value = mm_nt(left3(value), jnp.concatenate([high, high, low_part], axis=1)) + vector_ref[c : c + 1, :]
        passed = jnp.where(row < c, value, passed)
    dz, dr, dn, ds = [None] * STEPS, [None] * STEPS, [None] * STEPS, [None] * STEPS
    for j in reversed(range(STEPS)):
        at = slice(j * CHUNKS, (j + 1) * CHUNKS)
        lam = cot_ref[at, :] + passed
        dz[j], dr[j], dn[j] = coef_ref[2, at, :] * lam, coef_ref[3, at, :] * lam, coef_ref[4, at, :] * lam
        ds[j] = coef_ref[5, at, :] * lam
        if j > 0:
            high, low_part = split(jnp.concatenate([dz[j], dr[j], dn[j]], axis=1))
            both = mm(jnp.concatenate([high, low_part], axis=0), uth_ref[...])
            pulled = both[:CHUNKS] + both[CHUNKS:] + mm(high, utl_ref[...])
            passed = coef_ref[1, at, :] * lam + pulled
    dz, dr, dn, ds = (jnp.concatenate(part, axis=0) for part in (dz, dr, dn, ds))

    def stacked(value):
        return jnp.concatenate([value[:, :H], value[:, H:]], axis=0)

    sz, sr, sn, ss = (stacked(part) for part in (dz, dr, dn, ds))
    zero = jnp.zeros((2 * 64, H), F32)
    high, low_part = split(jnp.concatenate([sz, sr, ss, zero], axis=1))
    xin = xin_ref[...]
    grad_in = mm_tn(jnp.concatenate([xin, xin], axis=0), jnp.concatenate([high, low_part], axis=0))
    high, low_part = split(jnp.concatenate([sz, sr, sn, zero], axis=1))
    prev_high, prev_low = split(stacked(coef_ref[0]))
    grad_rec = mm_tn(
        jnp.concatenate([prev_high, prev_low, prev_high], axis=0),
        jnp.concatenate([high, high, low_part], axis=0),
    )
    out_ref[0:256, :] = grad_in[:, :LANES]
    rest = grad_in[:, LANES:]
    out_ref[256:384, :] = jnp.concatenate([rest[:128, :H], rest[128:, :H]], axis=1)
    out_ref[384:448, :] = grad_rec[:, :LANES]
    rest = grad_rec[:, LANES:]
    out_ref[448:480, :] = jnp.concatenate([rest[:32, :H], rest[32:, :H]], axis=1)
    sums = [jnp.sum(part, axis=0, keepdims=True) for part in (sz, sr, ss, sn)]
    scale = sums[0] / scale_ref[...]
    tail = jnp.concatenate(
        [jnp.concatenate([scale, sums[1]], axis=1), jnp.concatenate([sums[2], sums[3]], axis=1)], axis=0
    )
    out_ref[480:512, :] = jnp.concatenate([tail, jnp.zeros((30, LANES), F32)], axis=0)


def unpack_kernel(where_ref, own_ref, other_ref, in_ref, rec_ref, scale_ref, bias_ref):
    first = where_ref[1] == 0
    own = own_ref[...].reshape(256, LANES)
    other = other_ref[...].reshape(256, LANES)
    top, bottom = jnp.where(first, own, other), jnp.where(first, other, own)
    in_ref[:, :LANES] = top
    in_ref[0:128, LANES:] = bottom[:128, :H]
    in_ref[128:, LANES:] = bottom[:128, H:]
    rec_ref[:, :LANES] = bottom[128:192]
    rec_ref[0:32, LANES:] = bottom[192:224, :H]
    rec_ref[32:, LANES:] = bottom[192:224, H:]
    scale_ref[...] = bottom[224:225, :H]
    bias_ref[...] = jnp.concatenate([bottom[224:225, H:], bottom[225:226, :H], bottom[225:226, H:]], axis=0)


def call(kernel, outs, kinds, *operands, scratch=()):
    specs = [pl.BlockSpec(memory_space=SMEM if kind == "s" else VMEM) for kind in kinds]
    return pl.pallas_call(
        kernel,
        out_shape=[jax.ShapeDtypeStruct(*out) for out in outs],
        in_specs=specs,
        out_specs=[pl.BlockSpec(memory_space=VMEM)] * len(outs),
        scratch_shapes=list(scratch),
        compiler_params=pltpu.CompilerParams(vmem_limit_bytes=48 * 1024 * 1024),
    )(*operands)


def local(planes, width, ys, inputs, w_in, u_rec, timescale, other_bias, h_init, cotangent):
    place, part = lax.axis_index("seq"), lax.axis_index("batch")
    z, x, core = place // width, place % width, part % 2
    where = jnp.stack([x % 2, core, z * 2 + core]).astype(jnp.int32)

    def at(z, x, y, core):
        return (z * width + x) * (2 * ys) + y * 2 + core

    there, back = [], []
    for m in range(2):
        pairs = [
            (at(z, x, y, c), at(z, 2 * c + ((x % 2) ^ m), y, x // 2))
            for z in range(planes) for x in range(width) for y in range(ys) for c in range(2)
        ]
        there.append(pairs)
        back.append([(b, a) for a, b in pairs])
    along_x = [[z * width + x for x in range(width)] for z in range(planes)]
    along_z = [[z * width + x for z in range(planes)] for x in range(width)]
    along_y = [[y * 2 + c for y in range(ys)] for c in range(2)]
    cores = [(b, b ^ 1) for b in range(2 * ys)]
    axes = ("seq", "batch")

    def exchange(value):
        own = lax.all_to_all(value, "seq", 0, 0, axis_index_groups=along_z, tiled=True)
        return own, lax.ppermute(own, "batch", cores)

    w3, uth, utl, ud, bias = call(
        weights_kernel,
        [((384, 384), BF16), ((384, LANES), BF16), ((384, LANES), BF16), ((3, H, LANES), F32), ((8, LANES), F32)],
        "vvv", u_rec, timescale[None, :], other_bias,
    )
    (packed,) = call(
        pack_kernel, [((2, PART, LANES), F32)], "svvv",
        where, inputs, jnp.transpose(cotangent, (1, 2, 0)), h_init.T,
    )
    one = lax.ppermute(packed[0], axes, there[0])
    two = lax.ppermute(packed[1], axes, there[1])
    maps_t, prefix_t, send_t = ((STEPS, ROWS, LANES), F32), ((CHUNKS, 72, LANES), F32), ((planes, MAP, LANES), F32)
    x3, xin, cot, start, maps, prefix, send = call(
        first_kernel,
        [((3, 64, LANES), F32), ((128, 256), BF16), ((64, LANES), F32), ((8, LANES), F32), maps_t, prefix_t, send_t],
        "svvvvvv", where, one, two, w_in, w3, ud, bias,
    )
    spread_s = pltpu.VMEM((H * CHUNKS, LANES), F32)
    for _ in range(NEWTON - 1):
        own, other = exchange(send)
        maps, prefix, send = call(
            next_kernel, [maps_t, prefix_t, send_t], "svvvvvvvvv",
            where, own, other, start, x3, bias, w3, ud, maps, prefix, scratch=[spread_s],
        )
    own, other = exchange(send)
    states, coef, chunk, vector, half, send = call(
        turn_kernel,
        [((64, LANES), F32), ((6, 64, LANES), F32), ((CHUNKS, H, LANES), F32), ((8, LANES), F32), ((72, LANES), F32), send_t],
        "svvvvvvvvvv", where, own, other, start, x3, bias, w3, ud, maps, prefix, cot,
        scratch=[spread_s, pltpu.VMEM(*maps_t), pltpu.VMEM(*prefix_t), pltpu.VMEM((H * CHUNKS, LANES), F32)],
    )
    own, other = exchange(send)
    (grads,) = call(
        gradient_kernel, [((512, LANES), F32)], "svvvvvvvvvvvv",
        where, own, other, coef, chunk, vector, half, cot, uth, utl, xin, bias, timescale[None, :],
    )
    odd = x % 2
    low, high = states[:, :H], states[:, H:]
    even = odd == 0
    home = [
        lax.ppermute(jnp.where(even == (m == 0), low, high), axes, back[m]) for m in range(2)
    ]
    first, second = jnp.where(even, home[0], home[1]), jnp.where(even, home[1], home[0])
    traj = jnp.transpose(jnp.stack([first, second]), (2, 0, 1))

    halves = grads.reshape(2, 256, LANES)
    mine = jnp.where(core == 0, halves[0], halves[1])
    send = jnp.where(core == 0, halves[1], halves[0])
    part = mine + lax.ppermute(send, "batch", cores)
    part = lax.all_to_all(part.reshape(width, -1, LANES), "seq", 0, 0, axis_index_groups=along_x, tiled=True).sum(0)

    def everyone(value, axis, groups):
        wide = jnp.broadcast_to(value[None], (len(groups[0]),) + value.shape)
        return lax.all_to_all(wide, axis, 0, 0, axis_index_groups=groups, tiled=True)

    part = everyone(part, "batch", along_y).sum(0)
    part = everyone(part, "seq", along_z).sum(0)
    part = everyone(part, "seq", along_x)
    other = lax.ppermute(part, "batch", cores)
    grad_in, grad_rec, grad_scale, grad_other = call(
        unpack_kernel, [((256, 192), F32), ((H, 192), F32), ((1, H), F32), ((3, H), F32)], "svv", where, part, other,
    )
    return traj, grad_in, grad_rec, grad_scale[0], grad_other


def solution(mesh):
    width = 4
    planes = mesh.shape["seq"] // width
    ys = mesh.shape["batch"] // 2
    return jax.shard_map(
        functools.partial(local, planes, width, ys),
        mesh=mesh,
        in_specs=(P("batch", "seq", None), P(), P(), P(), P(), P(None, "batch"), P(None, "batch", "seq")),
        out_specs=(P(None, "batch", "seq"), P(), P(), P(), P()),
        check_vma=False,
    )
```

profile of v0, /device:TPU:1, one launch (start us, length us, event | category | flops | bytes accessed | tf_op | source)
XLA Modules:
  0.0 159.4 jit_solution(6636738783737335012)
XLA Ops:
  0.7 0.9 copy.16
  1.6 0.1 pad_add_fusion.where_ref
  1.7 0.0 copy-start.1
  1.7 0.8 copy-done.1
  2.5 0.0 copy-start.5
  2.5 0.7 copy-done.5
  3.2 0.6 shard_map.110
  3.9 6.0 %collective-permute-start = (f32[200,128]{1,0:T(8,128)S(1)}, f32[200,128]{1,0:T(8,128)S(1)}, u32[]{:S(2)}, u32[]{:S(2)}) collective-permute-start(f32[200,128]{1,0:T(8,128)S(1)} %get-tuple-element.72), channel_id=1, source_target_pairs={{0,0},{1,16},{2,2},{3,18},{4,4},{5,20},{6,6},{7,22},{8,8},{9,24},{... | collective-permute-start | bytes 307208 | tf_op jit(solution)/shard_map/ppermute | solution.py:493
  9.9 0.7 collective-permute-start.1
  10.6 1.0 copy.17.w_ref
  11.6 0.0 copy-start
  11.6 0.8 copy-done
  12.4 0.0 copy-start.2
  12.4 0.7 copy-done.2
  13.1 0.0 copy-start.4
  13.1 0.7 copy-done.4
  13.7 0.2 shard_map.111
  14.0 0.0 collective-permute-done.a_ref
  14.0 1.3 collective-permute-done.1.b_ref
  15.3 4.3 %shard_map.112 = (f32[3,64,128]{2,1,0:T(8,128)S(1)}, bf16[128,256]{1,0:T(8,128)(2,1)S(1)}, f32[64,128]{1,0:T(8,128)S(1)}, f32[8,128]{1,0:T(8,128)S(1)}, f32[8,52...) custom-call(s32[3]{0:T(128)S(1)} %pad_add_fusion.where_ref, ...), custom_call_target="tpu_custom_call" | custom-call | tf_op jit(solution)/shard_map/pallas_call | solution.py:448
  19.6 16.3 %all_to_all.40.own_ref = f32[8,40,128]{2,1,0:T(8,128)S(1)} all-to-all(f32[8,40,128]{2,1,0:T(8,128)S(1)} %get-tuple-element.36), channel_id=1, replica_groups={{0,32,64,96,128,160,192,224},{8,40,72,104,136,168,200,232},{16,48,80,11..., dimensions={0} | all-to-all | bytes 327680 | tf_op jit(solution)/shard_map/all_to_all | solution.py:481
  35.9 0.0 collective-permute-start.2
  35.9 1.4 collective-permute-done.2.other_ref
  37.3 7.0 %shard_map.113 = (f32[8,520,128]{2,1,0:T(8,128)S(1)}, f32[8,72,128]{2,1,0:T(8,128)S(1)}, f32[8,40,128]{2,1,0:T(8,128)S(1)}) custom-call(s32[3]{0:T(128)S(1)} %pad_add_fusion.where_ref, f32[8,40,128]{2,1,0:T(8,128)S(1)} %all_to_all.40.own_ref, f32[8,40,128]{2,1,0:T(8,128)S(1)} %collective-permute-done.2.other_ref, f32[8,128]{1,0:T(8,128)S(1)} %get-tuple-element.37.start_ref, ...), custom_call_target="tpu_custom_call" | custom-call | tf_op jit(solution)/shard_map/pallas_call | solution.py:448
  44.3 12.5 %all_to_all.41.own_ref = f32[8,40,128]{2,1,0:T(8,128)S(1)} all-to-all(f32[8,40,128]{2,1,0:T(8,128)S(1)} %get-tuple-element.41), channel_id=1, replica_groups={{0,32,64,96,128,160,192,224},{8,40,72,104,136,168,200,232},{16,48,80,11..., dimensions={0} | all-to-all | bytes 327680 | tf_op jit(solution)/shard_map/all_to_all | solution.py:481
  56.8 0.6 collective-permute-start.3
  57.4 1.0 collective-permute-done.3.other_ref
  58.4 7.0 %shard_map.114 = (f32[8,520,128]{2,1,0:T(8,128)S(1)}, f32[8,72,128]{2,1,0:T(8,128)S(1)}, f32[8,40,128]{2,1,0:T(8,128)S(1)}) custom-call(s32[3]{0:T(128)S(1)} %pad_add_fusion.where_ref, f32[8,40,128]{2,1,0:T(8,128)S(1)} %all_to_all.41.own_ref, f32[8,40,128]{2,1,0:T(8,128)S(1)} %collective-permute-done.3.other_ref, f32[8,128]{1,0:T(8,128)S(1)} %get-tuple-element.37.start_ref, ...), custom_call_target="tpu_custom_call" | custom-call | tf_op jit(solution)/shard_map/pallas_call | solution.py:448
  65.5 0.0 copy-start.3
  65.5 11.5 %all_to_all.42.own_ref = f32[8,40,128]{2,1,0:T(8,128)S(1)} all-to-all(f32[8,40,128]{2,1,0:T(8,128)S(1)} %get-tuple-element.44), channel_id=1, replica_groups={{0,32,64,96,128,160,192,224},{8,40,72,104,136,168,200,232},{16,48,80,11..., dimensions={0} | all-to-all | bytes 327680 | tf_op jit(solution)/shard_map/all_to_all | solution.py:481
  77.0 1.6 collective-permute-start.4
  78.6 1.0 collective-permute-done.4.other_ref
  79.6 7.6 %shard_map.115 = (f32[64,128]{1,0:T(8,128)S(1)}, f32[6,64,128]{2,1,0:T(8,128)S(1)}, f32[8,64,128]{2,1,0:T(8,128)S(1)}, f32[8,128]{1,0:T(8,128)S(1)}, f32[72,128]{1,0:T(8,128)S(1)}, /*index=5*/f32[8,40,128]{2,1,0:T(8,128)S(1)}) custom-call(s32[3]{0:T(128)S(1)} %pad_add_fusion.where_ref, f32[8,40,128]{2,1,0:T(8,128)S(1)} %all_to_all.42.own_ref, ...), custom_call_target="tpu_custom_call" | custom-call | tf_op jit(solution)/shard_map/pallas_call | solution.py:448
  87.3 11.5 %all_to_all.43.own_ref = f32[8,40,128]{2,1,0:T(8,128)S(1)} all-to-all(f32[8,40,128]{2,1,0:T(8,128)S(1)} %get-tuple-element.49), channel_id=1, replica_groups={{0,32,64,96,128,160,192,224},{8,40,72,104,136,168,200,232},{16,48,80,11..., dimensions={0} | all-to-all | bytes 327680 | tf_op jit(solution)/shard_map/all_to_all | solution.py:481
  98.8 1.6 collective-permute-start.7
  100.4 1.0 collective-permute-done.7.other_ref
  101.4 0.0 copy-done.3
  101.4 5.2 %shard_map.116 = f32[512,128]{1,0:T(8,128)S(1)} custom-call(s32[3]{0:T(128)S(1)} %pad_add_fusion.where_ref, f32[8,40,128]{2,1,0:T(8,128)S(1)} %all_to_all.43.own_ref, f32[8,40,128]{2,1,0:T(8,128)S(1)} %collective-permute-done.7.other_ref, f32[6,64,128]{2,1,0:T(8,128)S(1)} %get-tuple-element.50.coef_ref, f32[8,64,128]{2,1,0:T(8,128)S(1)} %get-tuple-element.51.chunk_ref, ...), custom_call_target="tpu_custom_call" | custom-call | tf_op jit(solution)/shard_map/pallas_call | solution.py:448
  106.7 0.5 collective-permute-start.8
  107.1 1.0 collective-permute-done.8
  108.1 8.1 %all_to_all.44 = f32[4,64,128]{2,1,0:T(8,128)S(1)} all-to-all(f32[4,64,128]{2,1,0:T(8,128)S(1)} %bitcast.22), channel_id=1, replica_groups={{0,8,16,24},{32,40,48,56},{64,72,80,88},{96,104,112,120},{128,136,144,1..., dimensions={0} | all-to-all | bytes 262144 | tf_op jit(solution)/shard_map/all_to_all | solution.py:533
  116.3 8.8 %all_to_all.45 = f32[4,64,128]{2,1,0:T(8,128)S(1)} all-to-all(f32[4,64,128]{2,1,0:T(8,128)S(1)} %broadcast_in_dim.9), channel_id=1, replica_groups={{0,2,4,6},{1,3,5,7},{8,10,12,14},{9,11,13,15},{16,18,20,22},{17,19,21,2..., dimensions={0} | all-to-all | bytes 262144 | tf_op jit(solution)/shard_map/all_to_all | solution.py:537
  125.1 0.7 broadcast_in_dim.10
  125.8 3.4 %all-to-all-start.6 = ((f32[8,64,128]{2,1,0:T(8,128)}), f32[8,64,128]{2,1,0:T(8,128)S(1)}, u32[]{:S(2)}, u32[]{:S(2)}) async-start(f32[8,64,128]{2,1,0:T(8,128)} %broadcast_in_dim.10), calls=%async_computation.6 | async-start | bytes 524288 | tf_op jit(solution)/shard_map/all_to_all | solution.py:537
  129.3 9.3 %all-to-all-done.6 = f32[8,64,128]{2,1,0:T(8,128)S(1)} async-done(((f32[8,64,128]{2,1,0:T(8,128)}), f32[8,64,128]{2,1,0:T(8,128)S(1)}, u32[]{:S(2)}, u32[]{:S(2)}) %all-to-all-start.6) | async-done | bytes 262176 | tf_op jit(solution)/shard_map/all_to_all | solution.py:537
  138.6 0.7 broadcast_in_dim.11
  139.3 3.3 %all-to-all-start.7 = ((f32[4,64,128]{2,1,0:T(8,128)}), f32[4,64,128]{2,1,0:T(8,128)S(1)}, u32[]{:S(2)}, u32[]{:S(2)}) async-start(f32[4,64,128]{2,1,0:T(8,128)} %broadcast_in_dim.11), calls=%async_computation.7 | async-start | bytes 262144 | tf_op jit(solution)/shard_map/all_to_all | solution.py:537
  142.6 0.1 slice_select_fusion.2
  142.7 9.3 %collective-permute-start.5 = (f32[64,64]{1,0:T(8,128)S(1)}, f32[64,64]{1,0:T(8,128)S(1)}, u32[]{:S(2)}, u32[]{:S(2)}) collective-permute-start(f32[64,64]{1,0:T(8,128)S(1)} %get-tuple-element.75), channel_id=1, source_target_pairs={{0,0},{16,1},{2,2},{18,3},{4,4},{20,5},{6,6},{22,7},{8,8},{24,9},{... | collective-permute-start | bytes 49160 | tf_op jit(solution)/shard_map/ppermute | solution.py:524
  152.0 0.1 collective-permute-start.6
  152.1 0.0 all-to-all-done.7.own_ref
  152.1 0.7 collective-permute-start.9
  152.8 0.7 collective-permute-done.5
  153.6 3.1 %collective-permute-done.6 = f32[64,64]{1,0:T(8,128)S(1)} collective-permute-done((f32[64,64]{1,0:T(8,128)S(1)}, f32[64,64]{1,0:T(8,128)S(1)}, u32[]{:S(2)}, u32[]{:S(2)}) %collective-permute-start.6) | collective-permute-done | bytes 16416 | tf_op jit(solution)/shard_map/ppermute | solution.py:524
  156.6 0.7 copy.18
  157.4 0.0 collective-permute-done.9.other_ref
  157.4 1.3 shard_map.117
  158.6 0.8 copy.19
  (9 shorter events, 0.1 us)
Async XLA Ops:
  1.7 0.8 copy-start.1
  2.5 0.7 copy-start.5
  3.9 10.1 %collective-permute-start = (f32[200,128]{1,0:T(8,128)S(1)}, f32[200,128]{1,0:T(8,128)S(1)}, u32[]{:S(2)}, u32[]{:S(2)}) collective-permute-start(f32[200,128]{1,0:T(8,128)S(1)} %get-tuple-element.72), channel_id=1, source_target_pairs={{0,0},{1,16},{2,2},{3,18},{4,4},{5,20},{6,6},{7,22},{8,8},{9,24},{... | collective-permute-start | bytes 307208 | tf_op jit(solution)/shard_map/ppermute | solution.py:493
  9.9 5.4 %collective-permute-start.1 = (f32[200,128]{1,0:T(8,128)S(1)}, f32[200,128]{1,0:T(8,128)S(1)}, u32[]{:S(2)}, u32[]{:S(2)}) collective-permute-start(f32[200,128]{1,0:T(8,128)S(1)} %get-tuple-element.71), channel_id=1, source_target_pairs={{0,8},{1,24},{2,10},{3,26},{4,12},{5,28},{6,14},{7,30},{8,0},{9,16... | collective-permute-start | bytes 307208 | tf_op jit(solution)/shard_map/ppermute | solution.py:494
  11.6 0.8 copy-start
  12.4 0.7 copy-start.2
  13.1 0.7 copy-start.4
  35.9 1.4 collective-permute-start.2
  56.8 1.6 %collective-permute-start.3 = (f32[8,40,128]{2,1,0:T(8,128)S(1)}, f32[8,40,128]{2,1,0:T(8,128)S(1)}, u32[]{:S(2)}, u32[]{:S(2)}) collective-permute-start(f32[8,40,128]{2,1,0:T(8,128)S(1)} %all_to_all.41.own_ref), channel_id=1, source_target_pairs={{0,1},{1,0},{2,3},{3,2},{4,5},{5,4},{6,7},{7,6},{8,9},{9,8},{10,11... | collective-permute-start | bytes 491528 | tf_op jit(solution)/shard_map/ppermute | solution.py:482
  65.5 35.9 %copy-start.3 = (f32[64]{0:T(128)S(1)}, f32[64]{0:T(128)}, u32[]{:S(2)}) copy-start(f32[64]{0:T(128)} %param.10) | copy-start | bytes 772
  77.0 2.6 %collective-permute-start.4 = (f32[8,40,128]{2,1,0:T(8,128)S(1)}, f32[8,40,128]{2,1,0:T(8,128)S(1)}, u32[]{:S(2)}, u32[]{:S(2)}) collective-permute-start(f32[8,40,128]{2,1,0:T(8,128)S(1)} %all_to_all.42.own_ref), channel_id=1, source_target_pairs={{0,1},{1,0},{2,3},{3,2},{4,5},{5,4},{6,7},{7,6},{8,9},{9,8},{10,11... | collective-permute-start | bytes 491528 | tf_op jit(solution)/shard_map/ppermute | solution.py:482
  98.8 2.6 %collective-permute-start.7 = (f32[8,40,128]{2,1,0:T(8,128)S(1)}, f32[8,40,128]{2,1,0:T(8,128)S(1)}, u32[]{:S(2)}, u32[]{:S(2)}) collective-permute-start(f32[8,40,128]{2,1,0:T(8,128)S(1)} %all_to_all.43.own_ref), channel_id=1, source_target_pairs={{0,1},{1,0},{2,3},{3,2},{4,5},{5,4},{6,7},{7,6},{8,9},{9,8},{10,11... | collective-permute-start | bytes 491528 | tf_op jit(solution)/shard_map/ppermute | solution.py:482
  106.7 1.4 collective-permute-start.8
  125.8 12.8 %all-to-all-start.6 = ((f32[8,64,128]{2,1,0:T(8,128)}), f32[8,64,128]{2,1,0:T(8,128)S(1)}, u32[]{:S(2)}, u32[]{:S(2)}) async-start(f32[8,64,128]{2,1,0:T(8,128)} %broadcast_in_dim.10), calls=%async_computation.6 | async-start | bytes 524288 | tf_op jit(solution)/shard_map/all_to_all | solution.py:537
  139.3 12.8 %all-to-all-start.7 = ((f32[4,64,128]{2,1,0:T(8,128)}), f32[4,64,128]{2,1,0:T(8,128)S(1)}, u32[]{:S(2)}, u32[]{:S(2)}) async-start(f32[4,64,128]{2,1,0:T(8,128)} %broadcast_in_dim.11), calls=%async_computation.7 | async-start | bytes 262144 | tf_op jit(solution)/shard_map/all_to_all | solution.py:537
  142.7 10.9 %collective-permute-start.5 = (f32[64,64]{1,0:T(8,128)S(1)}, f32[64,64]{1,0:T(8,128)S(1)}, u32[]{:S(2)}, u32[]{:S(2)}) collective-permute-start(f32[64,64]{1,0:T(8,128)S(1)} %get-tuple-element.75), channel_id=1, source_target_pairs={{0,0},{16,1},{2,2},{18,3},{4,4},{20,5},{6,6},{22,7},{8,8},{24,9},{... | collective-permute-start | bytes 49160 | tf_op jit(solution)/shard_map/ppermute | solution.py:524
  152.0 4.6 %collective-permute-start.6 = (f32[64,64]{1,0:T(8,128)S(1)}, f32[64,64]{1,0:T(8,128)S(1)}, u32[]{:S(2)}, u32[]{:S(2)}) collective-permute-start(f32[64,64]{1,0:T(8,128)S(1)} %get-tuple-element.76), channel_id=1, source_target_pairs={{8,0},{24,1},{10,2},{26,3},{12,4},{28,5},{14,6},{30,7},{0,8},{16,9... | collective-permute-start | bytes 49160 | tf_op jit(solution)/shard_map/ppermute | solution.py:524
  152.1 5.3 %collective-permute-start.9 = (f32[4,64,128]{2,1,0:T(8,128)S(1)}, f32[4,64,128]{2,1,0:T(8,128)S(1)}, u32[]{:S(2)}, u32[]{:S(2)}) collective-permute-start(f32[4,64,128]{2,1,0:T(8,128)S(1)} %all-to-all-done.7.own_ref), channel_id=1, source_target_pairs={{0,1},{1,0},{2,3},{3,2},{4,5},{5,4},{6,7},{7,6},{8,9},{9,8},{10,11... | collective-permute-start | bytes 393224 | tf_op jit(solution)/shard_map/ppermute | solution.py:542
where the time goes:
time: 160 us; the launch traced here: 159 us
  blocking collectives  68.8 us (43%)
  Pallas kernels  33.3 us (21%)
  starting transfers between devices  27.7 us (17%)
  waiting for transfers between devices  19.9 us (12%)
  local copies, waits for them, and re-layouts  8.52 us (5%)
    all_to_all x4, blocking collectives, exchange(): lax.all_to_all(value, 'seq', 0, 0, axis_index_groups=along_z, tiled=True)  51.9 us
    pallas_call x8, Pallas kernels, call(): pl.pallas_call(kernel, out_shape=[jax.ShapeDtypeStruct(*out) for out in o...  33.3 us
    ppermute x2, starting transfers between devices, local(): lax.ppermute(jnp.where(even == (m == 0), low, high), axes, back[m])  9.35 us
    all_to_all x2, waiting for transfers between devices, everyone(): lax.all_to_all(wide, axis, 0, 0, axis_index_groups=groups, tiled=True)  9.34 us
    all_to_all x1, blocking collectives, everyone(): lax.all_to_all(wide, axis, 0, 0, axis_index_groups=groups, tiled=True)  8.81 us
    all_to_all x1, blocking collectives, local(): lax.all_to_all(part.reshape(width, -1, LANES), 'seq', 0, 0, axis_index_gr...  8.14 us
    unnamed x16, local copies, waits for them, and re-layouts  7.11 us
    all_to_all x2, starting transfers between devices, everyone(): lax.all_to_all(wide, axis, 0, 0, axis_index_groups=groups, tiled=True)  6.74 us
  transfers between devices with their start and end apart: 12, of which 9 were waited for; matrix products, arithmetic and copies ran while one was open for 1% of the time, Pallas kernels for 0%

commit v1 on v0

--- a/solution.py
+++ b/solution.py
@@ -55,7 +55,7 @@
 
 
 def swap_halves(value):
-    return jnp.concatenate([value[:, H:], value[:, :H]], axis=1)
+    return pltpu.roll(value, H, axis=1)
 
 
 def doubled(value, half):
@@ -79,7 +79,19 @@
     return jnp.concatenate([jnp.where(low, matrix, 0.0), jnp.where(low, 0.0, matrix)], axis=0)
 
 
-def weights_kernel(u_ref, scale_ref, other_ref, w3_ref, uth_ref, utl_ref, ud_ref, bias_ref):
+def fetch(sources, targets, sems):
+    copies = [pltpu.make_async_copy(a, b, sems.at[n]) for n, (a, b) in enumerate(zip(sources, targets))]
+    for copy in copies:
+        copy.start()
+    for copy in copies:
+        copy.wait()
+
+
+def weights_kernel(
+    u_hbm, scale_hbm, other_hbm, w_hbm, w3_ref, ws_ref, uth_ref, utl_ref, ud_ref, bias_ref, w_ref,
+    u_ref, scale_ref, other_ref, sems,
+):
+    fetch((u_hbm, scale_hbm, other_hbm, w_hbm), (u_ref, scale_ref, other_ref, w_ref), sems)
     zero = jnp.zeros((H, H), F32)
     for g in range(3):
         block = u_ref[:, g * H : (g + 1) * H]
@@ -92,29 +104,41 @@
         w3_ref[0:LANES, at] = high
         w3_ref[LANES : 2 * LANES, at] = high
         w3_ref[2 * LANES : 3 * LANES, at] = low
+        ws_ref[0:LANES, at] = high
+        ws_ref[LANES : 2 * LANES, at] = high
+        ws_ref[2 * LANES : 3 * LANES, at] = low
+        if g == 2:
+            ws_ref[0:LANES, 3 * LANES :] = low
+            ws_ref[LANES : 2 * LANES, 3 * LANES :] = low
+            ws_ref[2 * LANES : 3 * LANES, 3 * LANES :] = low
         high, low = split(diag.T)
         uth_ref[at, :] = high
         utl_ref[at, :] = low
-    rows = [jnp.log(scale_ref[...]), other_ref[0:1, :], other_ref[1:2, :], other_ref[2:3, :]]
+    scale = scale_ref[...]
+    rows = [jnp.log(scale), other_ref[0:1, :], other_ref[1:2, :], other_ref[2:3, :], scale]
     rows = [jnp.concatenate([row, row], axis=1) for row in rows]
-    bias_ref[...] = jnp.concatenate(rows + [jnp.zeros((4, LANES), F32)], axis=0)
-
-
-def pack_kernel(where_ref, x_ref, cot_ref, h_ref, out_ref):
+    bias_ref[...] = jnp.concatenate(rows + [jnp.zeros((3, LANES), F32)], axis=0)
+
+
+def pack_kernel(where_ref, x_hbm, cot_hbm, h_hbm, one_ref, two_ref, x_ref, cot_ref, h_ref, sems):
+    fetch((x_hbm, cot_hbm, h_hbm), (x_ref, cot_ref, h_ref), sems)
     odd = where_ref[0]
     zero = jnp.zeros((H, H), F32)
-    for m in range(2):
+    cots = []
+    for e in range(2):
+        cots.append(jnp.transpose(jnp.concatenate([cot_ref[:, e, :], zero], axis=1))[:H])
+    for m, out_ref in enumerate((one_ref, two_ref)):
         first = odd == m
         x = jnp.where(first, x_ref[0].astype(F32), x_ref[1].astype(F32))
-        out_ref[m, 0:64, :] = x[:, :LANES]
-        out_ref[m, 64:128, :] = x[:, LANES:]
-        cot = jnp.where(first, cot_ref[0], cot_ref[1])
+        out_ref[0:64, :] = x[:, :LANES]
+        out_ref[64:128, :] = x[:, LANES:]
+        cot = jnp.where(first, cots[0], cots[1])
         low = jnp.concatenate([cot, zero], axis=1)
         high = jnp.concatenate([zero, cot], axis=1)
-        out_ref[m, 128:192, :] = jnp.where(odd == 0, low, high)
+        out_ref[128:192, :] = jnp.where(odd == 0, low, high)
         start = jnp.where(first, h_ref[0:1, :], h_ref[1:2, :])
         start = jnp.concatenate([start, start], axis=1)
-        out_ref[m, 192:200, :] = jnp.broadcast_to(start, (8, LANES))
+        out_ref[192:200, :] = jnp.broadcast_to(start, (8, LANES))
 
 
 def coefficients(prev, x3, bias, w3):
@@ -133,7 +157,15 @@
     return update, cz, cr, cn, slope, offset
 
 
-def scan_maps(coef, w3_ref, ud_ref, maps_ref):
+def gate_products(rows, ws_ref):
+    high, low = split(rows)
+    pair = jnp.concatenate([high, low], axis=1)
+    both = mm(jnp.concatenate([pair, high], axis=1), ws_ref[:, : 2 * LANES])
+    last = mm(pair, ws_ref[: 2 * LANES, 2 * LANES :])
+    return both[:, :LANES], both[:, LANES:], last[:, :LANES] + last[:, LANES:]
+
+
+def scan_maps(coef, ws_ref, ud_ref, maps_ref):
     update, cz, cr, cn, _, offset = coef
     shape = (BLOCK, CHUNKS, LANES)
     for j in range(STEPS):
@@ -154,13 +186,8 @@
                     new = jnp.concatenate([new, offset[at][None]], axis=0)
             else:
                 old = maps_ref[j - 1, rows, :]
-                prod = mm(left3(old), w3_ref[...]).reshape(BLOCK, CHUNKS, 3 * LANES)
-                new = (
-                    up_j * old.reshape(shape)
-                    + cz_j * prod[..., :LANES]
-                    + cr_j * prod[..., LANES : 2 * LANES]
-                    + cn_j * prod[..., 2 * LANES :]
-                )
+                mz, mr, mn = (part.reshape(shape) for part in gate_products(old, ws_ref))
+                new = up_j * old.reshape(shape) + cz_j * mz + cr_j * mr + cn_j * mn
                 if last:
                     new = jnp.concatenate([new[: BLOCK - 1], new[BLOCK - 1 :] + offset[at][None]], axis=0)
             maps_ref[j, rows, :] = new.reshape(BLOCK * CHUNKS, LANES)
@@ -192,20 +219,29 @@
     return both + jnp.where(row == H, second, 0.0)
 
 
-def send_map(total, out_ref):
+def send_map(total, flipped, where_ref, out_ref):
     low = lane_low((H // 2, LANES))
-    packed = jnp.where(low, total[: H // 2], total[H // 2 : H])
+    matrix = jnp.where(where_ref[1] == 0, flipped, total[:H])
+    packed = jnp.where(low, matrix[: H // 2], matrix[H // 2 :])
     for z in range(out_ref.shape[0]):
         out_ref[z, : H // 2, :] = packed
         out_ref[z, H // 2 :, :] = total[H:]
 
 
-def unpack_map(packed):
+def flip(matrix):
+    square = jnp.transpose(matrix)[:H]
+    return jnp.concatenate([square, square], axis=1)
+
+
+def unpack_map(packed, whole):
     body = packed[: H // 2]
     other = swap_halves(body)
     low = lane_low(body.shape)
-    matrix = jnp.concatenate([jnp.where(low, body, other), jnp.where(low, other, body)], axis=0)
-    return matrix, packed[H // 2 : H // 2 + 1]
+    if whole:
+        parts = [jnp.where(low, body, other), jnp.where(low, other, body)]
+    else:
+        parts = [jnp.where(low, body, 0.0), jnp.where(low, other, 0.0)]
+    return jnp.concatenate(parts, axis=0), packed[H // 2 : H // 2 + 1]
 
 
 def apply_row(state, matrix, vector):
@@ -215,15 +251,27 @@
 def enter_device(where_ref, own_ref, other_ref, start, reverse):
     core, mine = where_ref[1], where_ref[2]
     planes = own_ref.shape[0]
-    state = start
+    row = lax.broadcasted_iota(jnp.int32, (H, LANES), 0)
+    lane = lax.broadcasted_iota(jnp.int32, (H, LANES), 1)
+    eye = jnp.where(row == lane, 1.0, 0.0)
+    eyes = jnp.where(row == lane % H, 1.0, 0.0)
+    state = start[0:1]
     order = list(range(2 * planes))
     for n in reversed(order) if reverse else order:
         z, kappa = n // 2, n % 2
+        reached = (mine < n) if reverse else (mine > n)
         packed = jnp.where(core == kappa, own_ref[z], other_ref[z])
-        fresh = apply_row(state, *unpack_map(packed))
-        reached = (mine < n) if reverse else (mine > n)
-        state = jnp.where(reached, fresh, state)
-    return state
+        to_column = kappa == (1 if reverse else 0)
+        matrix, vector = unpack_map(packed, not to_column)
+        vector = jnp.where(reached, vector, 0.0)
+        if to_column:
+            matrix = jnp.where(reached, matrix, eye)
+            summed = jnp.sum(matrix * state + eye * vector, axis=1, keepdims=True)
+            state = jnp.broadcast_to(summed, (H, LANES))
+        else:
+            matrix = jnp.where(reached, matrix, eyes)
+            state = jnp.sum(matrix * state, axis=0, keepdims=True) + vector
+    return jnp.broadcast_to(state, (CHUNKS, LANES))
 
 
 def spread(rows, count):
@@ -267,15 +315,16 @@
     return states
 
 
-def phase(prev, x3_ref, bias_ref, w3_ref, ud_ref, maps_ref, prefix_ref, out_ref):
+def phase(where_ref, prev, x3_ref, bias_ref, w3_ref, ws_ref, ud_ref, maps_ref, prefix_ref, out_ref):
     coef = coefficients(prev, x3_ref, bias_ref[...], w3_ref[...])
-    scan_maps(coef, w3_ref, ud_ref, maps_ref)
+    scan_maps(coef, ws_ref, ud_ref, maps_ref)
     total = chain_chunks(maps_ref, prefix_ref)
-    send_map(join_halves(total), out_ref)
+    total = join_halves(total)
+    send_map(total, flip(total[:H]), where_ref, out_ref)
 
 
 def first_kernel(
-    where_ref, a_ref, b_ref, w_ref, w3_ref, ud_ref, bias_ref,
+    where_ref, a_ref, b_ref, w_ref, w3_ref, ws_ref, ud_ref, bias_ref,
     x3_ref, xin_ref, cot_ref, start_ref, maps_ref, prefix_ref, out_ref,
 ):
     odd, mine = where_ref[0], where_ref[2]
@@ -295,7 +344,7 @@
     )
     start = a_ref[192:200, :]
     start_ref[...] = start
-    flat = mm(xin, w_ref[...])
+    flat = mm_nt(xin, w_ref[...])
     bias = bias_ref[...]
     for g in range(3):
         cols = slice(g * H, (g + 1) * H)
@@ -304,18 +353,18 @@
     lane = lax.broadcasted_iota(jnp.int32, (64, LANES), 1)
     here = (row == 0) & (lane < H) & (mine == 0)
     prev = jnp.where(here, start[0:1, :], 0.0)
-    phase(prev, x3_ref, bias_ref, w3_ref, ud_ref, maps_ref, prefix_ref, out_ref)
+    phase(where_ref, prev, x3_ref, bias_ref, w3_ref, ws_ref, ud_ref, maps_ref, prefix_ref, out_ref)
 
 
 def next_kernel(
-    where_ref, own_ref, other_ref, start_ref, x3_ref, bias_ref, w3_ref, ud_ref, old_ref, before_ref,
+    where_ref, own_ref, other_ref, start_ref, x3_ref, bias_ref, w3_ref, ws_ref, ud_ref, old_ref, before_ref,
     maps_ref, prefix_ref, out_ref, spread_ref,
 ):
     state = enter_device(where_ref, own_ref, other_ref, start_ref[...], False)
     entering = enter_chunks(state, before_ref)
     states = trajectory(entering, old_ref, spread_ref)
     prev = jnp.concatenate([entering] + states[:-1], axis=0)
-    phase(prev, x3_ref, bias_ref, w3_ref, ud_ref, maps_ref, prefix_ref, out_ref)
+    phase(where_ref, prev, x3_ref, bias_ref, w3_ref, ws_ref, ud_ref, maps_ref, prefix_ref, out_ref)
 
 
 def half_sums(value):
@@ -327,8 +376,9 @@
 
 
 def turn_kernel(
-    where_ref, own_ref, other_ref, start_ref, x3_ref, bias_ref, w3_ref, ud_ref, old_ref, before_ref, cot_ref,
-    states_ref, coef_ref, chunk_ref, vector_ref, half_ref, out_ref, spread_ref, maps_ref, prefix_ref, acc_ref,
+    where_ref, own_ref, other_ref, start_ref, x3_ref, bias_ref, w3_ref, ws_ref, ud_ref, old_ref, before_ref, cot_ref,
+    states_ref, coef_ref, chunk_ref, vector_ref, half_ref, out_ref,
+    spread_ref, maps_ref, prefix_ref, acc_ref,
 ):
     state = enter_device(where_ref, own_ref, other_ref, start_ref[...], False)
     entering = enter_chunks(state, before_ref)
@@ -340,7 +390,7 @@
     coef_ref[0] = prev
     for n in range(5):
         coef_ref[n + 1] = coef[n]
-    scan_maps(coef, w3_ref, ud_ref, maps_ref)
+    scan_maps(coef, ws_ref, ud_ref, maps_ref)
     total = chain_chunks(maps_ref, prefix_ref)
     for b in range(0, H * CHUNKS, 64):
         acc = jnp.zeros((8, CHUNKS, LANES), F32)
@@ -364,17 +414,15 @@
     sums = half_sums(jnp.where(low, total[:H], 0.0) * tail)
     left = ends[:, :H] + sums[0:1]
     both = join_halves(total)
-    square = jnp.transpose(both[:H])[:H]
-    flipped = jnp.concatenate([square, square], axis=1)
     pad = jnp.zeros((7, LANES), F32)
-    send_map(jnp.concatenate([flipped, jnp.concatenate([left, left], axis=1), pad], axis=0), out_ref)
-    later = jnp.transpose(total[:H])[H:]
-    half_ref[...] = jnp.concatenate([jnp.concatenate([later, later], axis=1), tail, pad], axis=0)
+    left = jnp.concatenate([left, left], axis=1)
+    send_map(jnp.concatenate([both[:H], left, pad], axis=0), flip(both[:H]), where_ref, out_ref)
+    half_ref[...] = jnp.concatenate([flip(doubled(total[:H], 1)), tail, pad], axis=0)
 
 
 def gradient_kernel(
     where_ref, own_ref, other_ref, coef_ref, chunk_ref, vector_ref, half_ref, cot_ref, uth_ref, utl_ref,
-    xin_ref, bias_ref, scale_ref, out_ref,
+    xin_ref, bias_ref, states_ref, across_ref, keep_ref, give_ref, home_ref, full_ref,
 ):
     low = lane_low((CHUNKS, LANES))
     row = lax.broadcasted_iota(jnp.int32, (CHUNKS, LANES), 0)
@@ -407,73 +455,100 @@
     zero = jnp.zeros((2 * 64, H), F32)
     high, low_part = split(jnp.concatenate([sz, sr, ss, zero], axis=1))
     xin = xin_ref[...]
-    grad_in = mm_tn(jnp.concatenate([xin, xin], axis=0), jnp.concatenate([high, low_part], axis=0))
+    grad_in = mm_tn(jnp.concatenate([high, low_part], axis=0), jnp.concatenate([xin, xin], axis=0))
     high, low_part = split(jnp.concatenate([sz, sr, sn, zero], axis=1))
     prev_high, prev_low = split(stacked(coef_ref[0]))
     grad_rec = mm_tn(
         jnp.concatenate([prev_high, prev_low, prev_high], axis=0),
         jnp.concatenate([high, high, low_part], axis=0),
     )
-    out_ref[0:256, :] = grad_in[:, :LANES]
-    rest = grad_in[:, LANES:]
-    out_ref[256:384, :] = jnp.concatenate([rest[:128, :H], rest[128:, :H]], axis=1)
-    out_ref[384:448, :] = grad_rec[:, :LANES]
+    full_ref[0:192, :] = grad_in[:192, :LANES]
+    full_ref[192:384, :] = grad_in[:192, LANES:]
+    full_ref[384:448, :] = grad_rec[:, :LANES]
     rest = grad_rec[:, LANES:]
-    out_ref[448:480, :] = jnp.concatenate([rest[:32, :H], rest[32:, :H]], axis=1)
+    full_ref[448:480, :] = jnp.concatenate([rest[:32, :H], rest[32:, :H]], axis=1)
     sums = [jnp.sum(part, axis=0, keepdims=True) for part in (sz, sr, ss, sn)]
-    scale = sums[0] / scale_ref[...]
+    scale = sums[0] / bias_ref[4:5, :H]
     tail = jnp.concatenate(
         [jnp.concatenate([scale, sums[1]], axis=1), jnp.concatenate([sums[2], sums[3]], axis=1)], axis=0
     )
-    out_ref[480:512, :] = jnp.concatenate([tail, jnp.zeros((30, LANES), F32)], axis=0)
-
-
-def unpack_kernel(where_ref, own_ref, other_ref, in_ref, rec_ref, scale_ref, bias_ref):
-    first = where_ref[1] == 0
-    own = own_ref[...].reshape(256, LANES)
-    other = other_ref[...].reshape(256, LANES)
-    top, bottom = jnp.where(first, own, other), jnp.where(first, other, own)
-    in_ref[:, :LANES] = top
-    in_ref[0:128, LANES:] = bottom[:128, :H]
-    in_ref[128:, LANES:] = bottom[:128, H:]
-    rec_ref[:, :LANES] = bottom[128:192]
-    rec_ref[0:32, LANES:] = bottom[192:224, :H]
-    rec_ref[32:, LANES:] = bottom[192:224, H:]
-    scale_ref[...] = bottom[224:225, :H]
-    bias_ref[...] = jnp.concatenate([bottom[224:225, H:], bottom[225:226, :H], bottom[225:226, H:]], axis=0)
+    full_ref[480:512, :] = jnp.concatenate([tail, jnp.zeros((30, LANES), F32)], axis=0)
+    core, x = where_ref[1], where_ref[3]
+    for d in range(4):
+        part = lax.rem(x + d, 4)
+        rows = slice(d * 64, (d + 1) * 64)
+        keep_ref[rows, :] = full_ref[pl.ds(pl.multiple_of((core * 4 + part) * 64, 64), 64), :]
+        give_ref[rows, :] = full_ref[pl.ds(pl.multiple_of(((1 - core) * 4 + part) * 64, 64), 64), :]
+    for d in range(4):
+        part = lax.rem(x + d, 4)
+        whole = jnp.where(part // 2 == core, states_ref[...], across_ref[...])
+        block = jnp.where(lax.rem(part, 2) == 0, whole, swap_halves(whole))
+        home_ref[d] = jnp.where(lane_low((32, LANES)), block[:32], swap_halves(block[32:]))
+
+
+def unpack_kernel(
+    where_ref, one_ref, two_ref, three_ref, both_ref, home_ref, early0_ref, early1_ref, early2_ref,
+    in_ref, rec_ref, scale_ref, bias_ref, traj_ref, full_ref,
+):
+    core, x = where_ref[1], where_ref[3]
+    pieces = (both_ref, one_ref, two_ref, three_ref)
+    early = (early0_ref, early1_ref, early2_ref)
+    blocks = [home_ref[0]] + [ref[64:96, :] for ref in early]
+    for e in range(2):
+        where = lax.rem(x + 4 - 2 * core - e, 4)
+        block = blocks[0]
+        for d in range(1, 4):
+            block = jnp.where(where == d, blocks[d], block)
+        block = jnp.concatenate([block, swap_halves(block)], axis=0)
+        traj_ref[:, e, :] = jnp.transpose(block)[:H]
+    for d in range(4):
+        part = lax.rem(x + 4 - d, 4)
+        for core in range(2):
+            full_ref[pl.ds(pl.multiple_of((core * 4 + part) * 64, 64), 64), :] = pieces[d][core]
+    in_ref[:, :LANES] = full_ref[0:192, :]
+    in_ref[:, LANES:] = full_ref[192:384, :]
+    rec_ref[:, :LANES] = full_ref[384:448, :]
+    rec_ref[0:32, LANES:] = full_ref[448:480, :H]
+    rec_ref[32:, LANES:] = full_ref[448:480, H:]
+    one, two = full_ref[480:481, :], full_ref[481:482, :]
+    scale_ref[...] = one[:, :H]
+    bias_ref[...] = jnp.concatenate([one[:, H:], two[:, :H], two[:, H:]], axis=0)
 
 
 def call(kernel, outs, kinds, *operands, scratch=()):
-    specs = [pl.BlockSpec(memory_space=SMEM if kind == "s" else VMEM) for kind in kinds]
+    spaces = {"s": SMEM, "v": VMEM, "h": pltpu.HBM}
+    specs = [pl.BlockSpec(memory_space=spaces[kind]) for kind in kinds]
     return pl.pallas_call(
         kernel,
         out_shape=[jax.ShapeDtypeStruct(*out) for out in outs],
         in_specs=specs,
         out_specs=[pl.BlockSpec(memory_space=VMEM)] * len(outs),
         scratch_shapes=list(scratch),
-        compiler_params=pltpu.CompilerParams(vmem_limit_bytes=48 * 1024 * 1024),
+        compiler_params=pltpu.CompilerParams(vmem_limit_bytes=16 * 1024 * 1024),
     )(*operands)
 
 
 def local(planes, width, ys, inputs, w_in, u_rec, timescale, other_bias, h_init, cotangent):
     place, part = lax.axis_index("seq"), lax.axis_index("batch")
     z, x, core = place // width, place % width, part % 2
-    where = jnp.stack([x % 2, core, z * 2 + core]).astype(jnp.int32)
+    where = jnp.stack([x % 2, core, z * 2 + core, x]).astype(jnp.int32)
 
     def at(z, x, y, core):
         return (z * width + x) * (2 * ys) + y * 2 + core
 
-    there, back = [], []
+    there = []
     for m in range(2):
         pairs = [
             (at(z, x, y, c), at(z, 2 * c + ((x % 2) ^ m), y, x // 2))
             for z in range(planes) for x in range(width) for y in range(ys) for c in range(2)
         ]
         there.append(pairs)
-        back.append([(b, a) for a, b in pairs])
-    along_x = [[z * width + x for x in range(width)] for z in range(planes)]
+    step_x = [
+        [(z * width + x, z * width + (x + d) % width) for z in range(planes) for x in range(width)]
+        for d in range(1, width)
+    ]
     along_z = [[z * width + x for z in range(planes)] for x in range(width)]
-    along_y = [[y * 2 + c for y in range(ys)] for c in range(2)]
+    step_y = [[(b, (b + 2 * d) % (2 * ys)) for b in range(2 * ys)] for d in range(1, ys)]
     cores = [(b, b ^ 1) for b in range(2 * ys)]
     axes = ("seq", "batch")
 
@@ -481,69 +556,77 @@
         own = lax.all_to_all(value, "seq", 0, 0, axis_index_groups=along_z, tiled=True)
         return own, lax.ppermute(own, "batch", cores)
 
-    w3, uth, utl, ud, bias = call(
+    sems = pltpu.SemaphoreType.DMA((4,))
+    one, two = call(
+        pack_kernel, [((PART, LANES), F32)] * 2, "shhh", where, inputs, cotangent, h_init.T,
+        scratch=[
+            pltpu.VMEM(inputs.shape, BF16), pltpu.VMEM(cotangent.shape, F32), pltpu.VMEM((2, H), F32), sems
+        ],
+    )
+    one = lax.ppermute(one, axes, there[0])
+    two = lax.ppermute(two, axes, there[1])
+    w3, ws, uth, utl, ud, bias, w = call(
         weights_kernel,
-        [((384, 384), BF16), ((384, LANES), BF16), ((384, LANES), BF16), ((3, H, LANES), F32), ((8, LANES), F32)],
-        "vvv", u_rec, timescale[None, :], other_bias,
-    )
-    (packed,) = call(
-        pack_kernel, [((2, PART, LANES), F32)], "svvv",
-        where, inputs, jnp.transpose(cotangent, (1, 2, 0)), h_init.T,
-    )
-    one = lax.ppermute(packed[0], axes, there[0])
-    two = lax.ppermute(packed[1], axes, there[1])
+        [
+            ((384, 384), BF16), ((384, 512), BF16), ((384, LANES), BF16), ((384, LANES), BF16),
+            ((3, H, LANES), F32), ((8, LANES), F32), ((192, 256), BF16),
+        ],
+        "hhhh", u_rec, timescale[None, :], other_bias, w_in.T,
+        scratch=[pltpu.VMEM((H, 192), F32), pltpu.VMEM((1, H), F32), pltpu.VMEM((3, H), F32), sems],
+    )
     maps_t, prefix_t, send_t = ((STEPS, ROWS, LANES), F32), ((CHUNKS, 72, LANES), F32), ((planes, MAP, LANES), F32)
     x3, xin, cot, start, maps, prefix, send = call(
         first_kernel,
         [((3, 64, LANES), F32), ((128, 256), BF16), ((64, LANES), F32), ((8, LANES), F32), maps_t, prefix_t, send_t],
-        "svvvvvv", where, one, two, w_in, w3, ud, bias,
+        "svvvvvvv", where, one, two, w, w3, ws, ud, bias,
     )
     spread_s = pltpu.VMEM((H * CHUNKS, LANES), F32)
     for _ in range(NEWTON - 1):
         own, other = exchange(send)
         maps, prefix, send = call(
-            next_kernel, [maps_t, prefix_t, send_t], "svvvvvvvvv",
-            where, own, other, start, x3, bias, w3, ud, maps, prefix, scratch=[spread_s],
+            next_kernel, [maps_t, prefix_t, send_t], "svvvvvvvvvv",
+            where, own, other, start, x3, bias, w3, ws, ud, maps, prefix, scratch=[spread_s],
         )
     own, other = exchange(send)
     states, coef, chunk, vector, half, send = call(
         turn_kernel,
-        [((64, LANES), F32), ((6, 64, LANES), F32), ((CHUNKS, H, LANES), F32), ((8, LANES), F32), ((72, LANES), F32), send_t],
-        "svvvvvvvvvv", where, own, other, start, x3, bias, w3, ud, maps, prefix, cot,
-        scratch=[spread_s, pltpu.VMEM(*maps_t), pltpu.VMEM(*prefix_t), pltpu.VMEM((H * CHUNKS, LANES), F32)],
-    )
+        [
+            ((64, LANES), F32), ((6, 64, LANES), F32), ((CHUNKS, H, LANES), F32),
+            ((8, LANES), F32), ((72, LANES), F32), send_t,
+        ],
+        "svvvvvvvvvvv", where, own, other, start, x3, bias, w3, ws, ud, maps, prefix, cot,
+        scratch=[
+            spread_s, pltpu.VMEM(*maps_t), pltpu.VMEM(*prefix_t),
+            pltpu.VMEM((H * CHUNKS, LANES), F32),
+        ],
+    )
+    across = lax.ppermute(states, "batch", cores)
     own, other = exchange(send)
-    (grads,) = call(
-        gradient_kernel, [((512, LANES), F32)], "svvvvvvvvvvvv",
-        where, own, other, coef, chunk, vector, half, cot, uth, utl, xin, bias, timescale[None, :],
-    )
-    odd = x % 2
-    low, high = states[:, :H], states[:, H:]
-    even = odd == 0
-    home = [
-        lax.ppermute(jnp.where(even == (m == 0), low, high), axes, back[m]) for m in range(2)
-    ]
-    first, second = jnp.where(even, home[0], home[1]), jnp.where(even, home[1], home[0])
-    traj = jnp.transpose(jnp.stack([first, second]), (2, 0, 1))
-
-    halves = grads.reshape(2, 256, LANES)
-    mine = jnp.where(core == 0, halves[0], halves[1])
-    send = jnp.where(core == 0, halves[1], halves[0])
-    part = mine + lax.ppermute(send, "batch", cores)
-    part = lax.all_to_all(part.reshape(width, -1, LANES), "seq", 0, 0, axis_index_groups=along_x, tiled=True).sum(0)
-
-    def everyone(value, axis, groups):
-        wide = jnp.broadcast_to(value[None], (len(groups[0]),) + value.shape)
-        return lax.all_to_all(wide, axis, 0, 0, axis_index_groups=groups, tiled=True)
-
-    part = everyone(part, "batch", along_y).sum(0)
-    part = everyone(part, "seq", along_z).sum(0)
-    part = everyone(part, "seq", along_x)
+    keep, give, home = call(
+        gradient_kernel, [((256, LANES), F32), ((256, LANES), F32), ((4, 32, LANES), F32)], "svvvvvvvvvvvvv",
+        where, own, other, coef, chunk, vector, half, cot, uth, utl, xin, bias, states, across,
+        scratch=[pltpu.VMEM((512, LANES), F32)],
+    )
+
+    def around(values, axis, pairs):
+        return [lax.ppermute(value, axis, pair) for value, pair in zip(values, pairs)]
+
+    parts = (keep + lax.ppermute(give, "batch", cores)).reshape(width, -1, LANES)
+    early = around([jnp.concatenate([parts[d], home[d]], axis=0) for d in range(1, width)], "seq", step_x)
+    part = parts[0] + sum(piece[:64] for piece in early)
+    part = part + sum(around([part] * (ys - 1), "batch", step_y))
+    wide = jnp.broadcast_to(part[None], (planes,) + part.shape)
+    part = lax.all_to_all(wide, "seq", 0, 0, axis_index_groups=along_z, tiled=True).sum(0)
     other = lax.ppermute(part, "batch", cores)
-    grad_in, grad_rec, grad_scale, grad_other = call(
-        unpack_kernel, [((256, 192), F32), ((H, 192), F32), ((1, H), F32), ((3, H), F32)], "svv", where, part, other,
-    )
-    return traj, grad_in, grad_rec, grad_scale[0], grad_other
+    first = core == 0
+    both = jnp.stack([jnp.where(first, part, other), jnp.where(first, other, part)])
+    rest = around([both] * (width - 1), "seq", step_x)
+    grad_in, grad_rec, grad_scale, grad_other, traj = call(
+        unpack_kernel,
+        [((192, 256), F32), ((H, 192), F32), ((1, H), F32), ((3, H), F32), ((H, 2, 64), F32)], "svvvvvvvv",
+        where, *rest, both, home, *early, scratch=[pltpu.VMEM((512, LANES), F32)],
+    )
+    return traj, grad_in.T, grad_rec, grad_scale[0], grad_other
 
 
 def solution(mesh):

time: 160 us -> 143 us (0.89)
  Pallas kernels: 33.3 us -> 28 us
  blocking collectives: 68.8 us -> 63.7 us
  starting transfers between devices: 27.7 us -> 24.4 us
  local copies, waits for them, and re-layouts: 8.52 us -> 5.46 us
    all_to_all x2 -> x0, waiting for transfers between devices: 9.34 us -> none  [everyone(): lax.all_to_all(wide, axis, 0, 0, axis_index_groups=groups, tiled=True)]
    ppermute x5 -> x13, waiting for transfers between devices: 6.09 us -> 15.2 us  [the longest x9 11.6 us: around(): lax.ppermute(value, axis, pair)]
    all_to_all x2 -> x0, starting transfers between devices: 6.74 us -> none  [everyone(): lax.all_to_all(wide, axis, 0, 0, axis_index_groups=groups, tiled=True)]
    pallas_call x8, Pallas kernels: 33.3 us -> 28 us  [call(): pl.pallas_call(kernel, out_shape=[jax.ShapeDtypeStruct(*out) for out in o...]
    all_to_all x2 -> x1, blocking collectives: 17 us -> 11.9 us  [local(): lax.all_to_all(wide, 'seq', 0, 0, axis_index_groups=along_z, tiled=True)]
    ppermute x1, starting transfers between devices: 0.75 us -> 4.22 us  [local(): other = lax.ppermute(part, 'batch', cores)]
    unnamed x16 -> x14, local copies, waits for them, and re-layouts: 7.11 us -> 5.43 us
    ppermute x5 -> x13, starting transfers between devices: 16.5 us -> 16.5 us  [the longest x9 9.45 us: around(): lax.ppermute(value, axis, pair)]
  transfers between devices with their start and end apart: 12 -> 18, of which waited for: 9 -> 15; matrix products, arithmetic and copies ran while one was open for 1% -> 0% of each run, Pallas kernels for 0% -> 0%
where the time goes in v1:
time: 143 us; the launch traced here: 142 us
  blocking collectives  63.7 us (45%)
  Pallas kernels  28 us (20%)
  starting transfers between devices  24.4 us (17%)
  waiting for transfers between devices  19.5 us (14%)
  local copies, waits for them, and re-layouts  5.46 us (4%)
    all_to_all x4, blocking collectives, exchange(): lax.all_to_all(value, 'seq', 0, 0, axis_index_groups=along_z, tiled=True)  51.9 us
    pallas_call x8, Pallas kernels, call(): pl.pallas_call(kernel, out_shape=[jax.ShapeDtypeStruct(*out) for out in o...  28 us
    all_to_all x1, blocking collectives, local(): lax.all_to_all(wide, 'seq', 0, 0, axis_index_groups=along_z, tiled=True)  11.9 us
    ppermute x9, waiting for transfers between devices, around(): lax.ppermute(value, axis, pair)  11.6 us
    ppermute x9, starting transfers between devices, around(): lax.ppermute(value, axis, pair)  9.45 us
    ppermute x1, starting transfers between devices, local(): one = lax.ppermute(one, axes, there[0])  6.04 us
    unnamed x14, local copies, waits for them, and re-layouts  5.43 us
    ppermute x1, starting transfers between devices, local(): other = lax.ppermute(part, 'batch', cores)  4.22 us
  transfers between devices with their start and end apart: 18, of which 15 were waited for; matrix products, arithmetic and copies ran while one was open for 0% of the time, Pallas kernels for 0%

profile of v1, /device:TPU:1, one launch (start us, length us, event | category | flops | bytes accessed | tf_op | source)
XLA Modules:
  0.0 142.1 jit_solution(11015322383867505992)
XLA Ops:
  0.7 0.1 pad_add_fusion.where_ref
  0.8 0.0 copy-start.1
  0.8 0.8 copy-done.1
  1.6 0.0 copy-start.2
  1.6 0.8 copy-done.2
  2.4 0.0 copy-start.5
  2.4 0.7 copy-done.5
  3.1 0.9 shard_map.110
  4.1 6.0 %collective-permute-start = (f32[200,128]{1,0:T(8,128)S(1)}, f32[200,128]{1,0:T(8,128)S(1)}, u32[]{:S(2)}, u32[]{:S(2)}) collective-permute-start(f32[200,128]{1,0:T(8,128)S(1)} %get-tuple-element.41), channel_id=1, source_target_pairs={{0,0},{1,16},{2,2},{3,18},{4,4},{5,20},{6,6},{7,22},{8,8},{9,24},{... | collective-permute-start | bytes 307208 | tf_op jit(solution)/shard_map/ppermute | solution.py:566
  10.1 0.7 collective-permute-start.1
  10.8 0.0 copy-start
  10.8 0.9 copy-done
  11.7 0.0 copy-start.3
  11.7 0.8 copy-done.3
  12.5 0.0 copy-start.4
  12.5 0.7 copy-done.4
  13.2 0.0 copy-start.6
  13.2 0.7 copy-done.6
  13.8 0.4 shard_map.111
  14.3 0.0 collective-permute-done.a_ref
  14.3 1.2 collective-permute-done.1.b_ref
  15.5 4.0 %shard_map.112 = (f32[3,64,128]{2,1,0:T(8,128)S(1)}, bf16[128,256]{1,0:T(8,128)(2,1)S(1)}, f32[64,128]{1,0:T(8,128)S(1)}, f32[8,128]{1,0:T(8,128)S(1)}, f32[8,52...) custom-call(s32[4]{0:T(128)S(1)} %pad_add_fusion.where_ref, ...), custom_call_target="tpu_custom_call" | custom-call | tf_op jit(solution)/shard_map/pallas_call | solution.py:521
  19.5 16.3 %all_to_all.25.own_ref = f32[8,40,128]{2,1,0:T(8,128)S(1)} all-to-all(f32[8,40,128]{2,1,0:T(8,128)S(1)} %get-tuple-element.48), channel_id=1, replica_groups={{0,32,64,96,128,160,192,224},{8,40,72,104,136,168,200,232},{16,48,80,11..., dimensions={0} | all-to-all | bytes 327680 | tf_op jit(solution)/shard_map/all_to_all | solution.py:556
  35.8 0.0 collective-permute-start.2
  35.8 1.4 collective-permute-done.2.other_ref
  37.2 5.6 %shard_map.113 = (f32[8,520,128]{2,1,0:T(8,128)S(1)}, f32[8,72,128]{2,1,0:T(8,128)S(1)}, f32[8,40,128]{2,1,0:T(8,128)S(1)}) custom-call(s32[4]{0:T(128)S(1)} %pad_add_fusion.where_ref, f32[8,40,128]{2,1,0:T(8,128)S(1)} %all_to_all.25.own_ref, f32[8,40,128]{2,1,0:T(8,128)S(1)} %collective-permute-done.2.other_ref, f32[8,128]{1,0:T(8,128)S(1)} %get-tuple-element.49.start_ref, ...), custom_call_target="tpu_custom_call" | custom-call | tf_op jit(solution)/shard_map/pallas_call | solution.py:521
  42.8 12.5 %all_to_all.26.own_ref = f32[8,40,128]{2,1,0:T(8,128)S(1)} all-to-all(f32[8,40,128]{2,1,0:T(8,128)S(1)} %get-tuple-element.53), channel_id=1, replica_groups={{0,32,64,96,128,160,192,224},{8,40,72,104,136,168,200,232},{16,48,80,11..., dimensions={0} | all-to-all | bytes 327680 | tf_op jit(solution)/shard_map/all_to_all | solution.py:556
  55.3 0.6 collective-permute-start.3
  55.9 1.0 collective-permute-done.3.other_ref
  56.9 5.6 %shard_map.114 = (f32[8,520,128]{2,1,0:T(8,128)S(1)}, f32[8,72,128]{2,1,0:T(8,128)S(1)}, f32[8,40,128]{2,1,0:T(8,128)S(1)}) custom-call(s32[4]{0:T(128)S(1)} %pad_add_fusion.where_ref, f32[8,40,128]{2,1,0:T(8,128)S(1)} %all_to_all.26.own_ref, f32[8,40,128]{2,1,0:T(8,128)S(1)} %collective-permute-done.3.other_ref, f32[8,128]{1,0:T(8,128)S(1)} %get-tuple-element.49.start_ref, ...), custom_call_target="tpu_custom_call" | custom-call | tf_op jit(solution)/shard_map/pallas_call | solution.py:521
  62.5 11.5 %all_to_all.27.own_ref = f32[8,40,128]{2,1,0:T(8,128)S(1)} all-to-all(f32[8,40,128]{2,1,0:T(8,128)S(1)} %get-tuple-element.56), channel_id=1, replica_groups={{0,32,64,96,128,160,192,224},{8,40,72,104,136,168,200,232},{16,48,80,11..., dimensions={0} | all-to-all | bytes 327680 | tf_op jit(solution)/shard_map/all_to_all | solution.py:556
  74.0 1.6 %collective-permute-start.4 = (f32[8,40,128]{2,1,0:T(8,128)S(1)}, f32[8,40,128]{2,1,0:T(8,128)S(1)}, u32[]{:S(2)}, u32[]{:S(2)}) collective-permute-start(f32[8,40,128]{2,1,0:T(8,128)S(1)} %all_to_all.27.own_ref), channel_id=1, source_target_pairs={{0,1},{1,0},{2,3},{3,2},{4,5},{5,4},{6,7},{7,6},{8,9},{9,8},{10,11... | collective-permute-start | bytes 491528 | tf_op jit(solution)/shard_map/ppermute | solution.py:557
  75.6 1.0 collective-permute-done.4.other_ref
  76.6 6.1 %shard_map.115 = (f32[64,128]{1,0:T(8,128)S(1)}, f32[6,64,128]{2,1,0:T(8,128)S(1)}, f32[8,64,128]{2,1,0:T(8,128)S(1)}, f32[8,128]{1,0:T(8,128)S(1)}, f32[72,128]{1,0:T(8,128)S(1)}, /*index=5*/f32[8,40,128]{2,1,0:T(8,128)S(1)}) custom-call(s32[4]{0:T(128)S(1)} %pad_add_fusion.where_ref, f32[8,40,128]{2,1,0:T(8,128)S(1)} %all_to_all.27.own_ref, ...), custom_call_target="tpu_custom_call" | custom-call | tf_op jit(solution)/shard_map/pallas_call | solution.py:521
  82.7 11.5 %all_to_all.28.own_ref = f32[8,40,128]{2,1,0:T(8,128)S(1)} all-to-all(f32[8,40,128]{2,1,0:T(8,128)S(1)} %get-tuple-element.60), channel_id=1, replica_groups={{0,32,64,96,128,160,192,224},{8,40,72,104,136,168,200,232},{16,48,80,11..., dimensions={0} | all-to-all | bytes 327680 | tf_op jit(solution)/shard_map/all_to_all | solution.py:556
  94.3 1.6 %collective-permute-start.5 = (f32[8,40,128]{2,1,0:T(8,128)S(1)}, f32[8,40,128]{2,1,0:T(8,128)S(1)}, u32[]{:S(2)}, u32[]{:S(2)}) collective-permute-start(f32[8,40,128]{2,1,0:T(8,128)S(1)} %all_to_all.28.own_ref), channel_id=1, source_target_pairs={{0,1},{1,0},{2,3},{3,2},{4,5},{5,4},{6,7},{7,6},{8,9},{9,8},{10,11... | collective-permute-start | bytes 491528 | tf_op jit(solution)/shard_map/ppermute | solution.py:557
  95.8 0.0 collective-permute-start.6
  95.8 1.2 collective-permute-done.6.across_ref
  97.0 0.0 collective-permute-done.5.other_ref
  97.0 4.0 %shard_map.116 = (f32[256,128]{1,0:T(8,128)S(1)}, f32[256,128]{1,0:T(8,128)S(1)}, f32[4,32,128]{2,1,0:T(8,128)S(1)}) custom-call(s32[4]{0:T(128)S(1)} %pad_add_fusion.where_ref, f32[8,40,128]{2,1,0:T(8,128)S(1)} %all_to_all.28.own_ref, f32[8,40,128]{2,1,0:T(8,128)S(1)} %collective-permute-done.5.other_ref, f32[6,64,128]{2,1,0:T(8,128)S(1)} %get-tuple-element.61.coef_ref, ...), custom_call_target="tpu_custom_call" | custom-call | tf_op jit(solution)/shard_map/pallas_call | solution.py:521
  101.1 0.3 collective-permute-start.7
  101.4 1.1 collective-permute-done.7
  102.5 1.9 %collective-permute-start.9 = (f32[96,128]{1,0:T(8,128)S(1)}, f32[96,128]{1,0:T(8,128)S(1)}, u32[]{:S(2)}, u32[]{:S(2)}) collective-permute-start(f32[96,128]{1,0:T(8,128)S(1)} %pad_maximum_fusion.2), channel_id=1, source_target_pairs={{0,16},{8,24},{16,0},{24,8},{32,48},{40,56},{48,32},{56,40},{64,80... | collective-permute-start | bytes 147464 | tf_op jit(solution)/shard_map/ppermute | solution.py:612
  104.4 0.7 collective-permute-start.10
  105.1 0.8 collective-permute-start.8
  105.9 1.2 collective-permute-done.9.early1_ref
  107.1 1.0 collective-permute-done.10.early2_ref
  108.1 1.2 collective-permute-done.8.early0_ref
  109.3 2.8 %collective-permute-start.13 = (f32[64,128]{1,0:T(8,128)S(1)}, f32[64,128]{1,0:T(8,128)S(1)}, u32[]{:S(2)}, u32[]{:S(2)}) collective-permute-start(f32[64,128]{1,0:T(8,128)S(1)} %fusion), channel_id=1, source_target_pairs={{0,6},{1,7},{2,0},{3,1},{4,2},{5,3},{6,4},{7,5},{8,14},{9,15},{10,... | collective-permute-start | bytes 98312 | tf_op jit(solution)/shard_map/ppermute | solution.py:612
  112.1 0.3 collective-permute-start.12
  112.4 0.7 collective-permute-start.11
  113.1 0.0 collective-permute-done.13
  113.1 3.3 %collective-permute-done.12 = f32[64,128]{1,0:T(8,128)S(1)} collective-permute-done((f32[64,128]{1,0:T(8,128)S(1)}, f32[64,128]{1,0:T(8,128)S(1)}, u32[]{:S(2)}, u32[]{:S(2)}) %collective-permute-start.12) | collective-permute-done | bytes 32800 | tf_op jit(solution)/shard_map/ppermute | solution.py:612
  116.4 0.3 collective-permute-done.11
  116.7 11.9 %all_to_all.29 = f32[8,64,128]{2,1,0:T(8,128)S(1)} all-to-all(f32[8,64,128]{2,1,0:T(8,128)S(1)} %broadcast_in_dim.10), channel_id=1, replica_groups={{0,32,64,96,128,160,192,224},{8,40,72,104,136,168,200,232},{16,48,80,11..., dimensions={0} | all-to-all | bytes 524288 | tf_op jit(solution)/shard_map/all_to_all | solution.py:619
  128.6 4.2 %collective-permute-start.14 = (f32[64,128]{1,0:T(8,128)S(1)}, f32[64,128]{1,0:T(8,128)S(1)}, u32[]{:S(2)}, u32[]{:S(2)}) collective-permute-start(f32[64,128]{1,0:T(8,128)S(1)} %reduce_sum.9), channel_id=1, source_target_pairs={{0,1},{1,0},{2,3},{3,2},{4,5},{5,4},{6,7},{7,6},{8,9},{9,8},{10,11... | collective-permute-start | bytes 98312 | tf_op jit(solution)/shard_map/ppermute | solution.py:620
  132.8 0.9 collective-permute-done.14
  133.7 0.9 collective-permute-start.17
  134.6 0.8 collective-permute-start.16
  135.4 0.6 collective-permute-start.15
  136.0 0.9 collective-permute-done.17.three_ref
  136.9 2.4 %collective-permute-done.16.two_ref = f32[2,64,128]{2,1,0:T(8,128)S(1)} collective-permute-done((f32[2,64,128]{2,1,0:T(8,128)S(1)}, f32[2,64,128]{2,1,0:T(8,128)S(1)}, u32[]{:S(2)}, u32[]{:S(2)}) %collective-permute-start.16) | collective-permute-done | bytes 65568 | tf_op jit(solution)/shard_map/ppermute | solution.py:612
  139.3 1.4 %collective-permute-done.15.one_ref = f32[2,64,128]{2,1,0:T(8,128)S(1)} collective-permute-done((f32[2,64,128]{2,1,0:T(8,128)S(1)}, f32[2,64,128]{2,1,0:T(8,128)S(1)}, u32[]{:S(2)}, u32[]{:S(2)}) %collective-permute-start.15) | collective-permute-done | bytes 65568 | tf_op jit(solution)/shard_map/ppermute | solution.py:612
  140.7 1.4 shard_map.117
  (12 shorter events, 0.1 us)
Async XLA Ops:
  0.8 0.8 copy-start.1
  1.6 0.8 copy-start.2
  2.4 0.7 copy-start.5
  4.1 10.2 %collective-permute-start = (f32[200,128]{1,0:T(8,128)S(1)}, f32[200,128]{1,0:T(8,128)S(1)}, u32[]{:S(2)}, u32[]{:S(2)}) collective-permute-start(f32[200,128]{1,0:T(8,128)S(1)} %get-tuple-element.41), channel_id=1, source_target_pairs={{0,0},{1,16},{2,2},{3,18},{4,4},{5,20},{6,6},{7,22},{8,8},{9,24},{... | collective-permute-start | bytes 307208 | tf_op jit(solution)/shard_map/ppermute | solution.py:566
  10.1 5.4 %collective-permute-start.1 = (f32[200,128]{1,0:T(8,128)S(1)}, f32[200,128]{1,0:T(8,128)S(1)}, u32[]{:S(2)}, u32[]{:S(2)}) collective-permute-start(f32[200,128]{1,0:T(8,128)S(1)} %get-tuple-element.42), channel_id=1, source_target_pairs={{0,8},{1,24},{2,10},{3,26},{4,12},{5,28},{6,14},{7,30},{8,0},{9,16... | collective-permute-start | bytes 307208 | tf_op jit(solution)/shard_map/ppermute | solution.py:567
  10.8 0.9 copy-start
  11.7 0.8 copy-start.3
  12.5 0.7 copy-start.4
  13.2 0.7 copy-start.6
  35.8 1.4 collective-permute-start.2
  55.3 1.6 %collective-permute-start.3 = (f32[8,40,128]{2,1,0:T(8,128)S(1)}, f32[8,40,128]{2,1,0:T(8,128)S(1)}, u32[]{:S(2)}, u32[]{:S(2)}) collective-permute-start(f32[8,40,128]{2,1,0:T(8,128)S(1)} %all_to_all.26.own_ref), channel_id=1, source_target_pairs={{0,1},{1,0},{2,3},{3,2},{4,5},{5,4},{6,7},{7,6},{8,9},{9,8},{10,11... | collective-permute-start | bytes 491528 | tf_op jit(solution)/shard_map/ppermute | solution.py:557
  74.0 2.6 %collective-permute-start.4 = (f32[8,40,128]{2,1,0:T(8,128)S(1)}, f32[8,40,128]{2,1,0:T(8,128)S(1)}, u32[]{:S(2)}, u32[]{:S(2)}) collective-permute-start(f32[8,40,128]{2,1,0:T(8,128)S(1)} %all_to_all.27.own_ref), channel_id=1, source_target_pairs={{0,1},{1,0},{2,3},{3,2},{4,5},{5,4},{6,7},{7,6},{8,9},{9,8},{10,11... | collective-permute-start | bytes 491528 | tf_op jit(solution)/shard_map/ppermute | solution.py:557
  94.3 2.8 %collective-permute-start.5 = (f32[8,40,128]{2,1,0:T(8,128)S(1)}, f32[8,40,128]{2,1,0:T(8,128)S(1)}, u32[]{:S(2)}, u32[]{:S(2)}) collective-permute-start(f32[8,40,128]{2,1,0:T(8,128)S(1)} %all_to_all.28.own_ref), channel_id=1, source_target_pairs={{0,1},{1,0},{2,3},{3,2},{4,5},{5,4},{6,7},{7,6},{8,9},{9,8},{10,11... | collective-permute-start | bytes 491528 | tf_op jit(solution)/shard_map/ppermute | solution.py:557
  95.8 1.2 collective-permute-start.6
  101.1 1.4 %collective-permute-start.7 = (f32[256,128]{1,0:T(8,128)S(1)}, f32[256,128]{1,0:T(8,128)S(1)}, u32[]{:S(2)}, u32[]{:S(2)}) collective-permute-start(f32[256,128]{1,0:T(8,128)S(1)} %get-tuple-element.70), channel_id=1, source_target_pairs={{0,1},{1,0},{2,3},{3,2},{4,5},{5,4},{6,7},{7,6},{8,9},{9,8},{10,11... | collective-permute-start | bytes 393224 | tf_op jit(solution)/shard_map/ppermute | solution.py:614
  102.5 4.5 %collective-permute-start.9 = (f32[96,128]{1,0:T(8,128)S(1)}, f32[96,128]{1,0:T(8,128)S(1)}, u32[]{:S(2)}, u32[]{:S(2)}) collective-permute-start(f32[96,128]{1,0:T(8,128)S(1)} %pad_maximum_fusion.2), channel_id=1, source_target_pairs={{0,16},{8,24},{16,0},{24,8},{32,48},{40,56},{48,32},{56,40},{64,80... | collective-permute-start | bytes 147464 | tf_op jit(solution)/shard_map/ppermute | solution.py:612
  104.4 3.6 %collective-permute-start.10 = (f32[96,128]{1,0:T(8,128)S(1)}, f32[96,128]{1,0:T(8,128)S(1)}, u32[]{:S(2)}, u32[]{:S(2)}) collective-permute-start(f32[96,128]{1,0:T(8,128)S(1)} %pad_maximum_fusion.3), channel_id=1, source_target_pairs={{0,24},{8,0},{16,8},{24,16},{32,56},{40,32},{48,40},{56,48},{64,88... | collective-permute-start | bytes 147464 | tf_op jit(solution)/shard_map/ppermute | solution.py:612
  105.1 4.2 %collective-permute-start.8 = (f32[96,128]{1,0:T(8,128)S(1)}, f32[96,128]{1,0:T(8,128)S(1)}, u32[]{:S(2)}, u32[]{:S(2)}) collective-permute-start(f32[96,128]{1,0:T(8,128)S(1)} %pad_maximum_fusion.1), channel_id=1, source_target_pairs={{0,8},{8,16},{16,24},{24,0},{32,40},{40,48},{48,56},{56,32},{64,72... | collective-permute-start | bytes 147464 | tf_op jit(solution)/shard_map/ppermute | solution.py:612
  109.3 3.8 %collective-permute-start.13 = (f32[64,128]{1,0:T(8,128)S(1)}, f32[64,128]{1,0:T(8,128)S(1)}, u32[]{:S(2)}, u32[]{:S(2)}) collective-permute-start(f32[64,128]{1,0:T(8,128)S(1)} %fusion), channel_id=1, source_target_pairs={{0,6},{1,7},{2,0},{3,1},{4,2},{5,3},{6,4},{7,5},{8,14},{9,15},{10,... | collective-permute-start | bytes 98312 | tf_op jit(solution)/shard_map/ppermute | solution.py:612
  112.1 4.3 %collective-permute-start.12 = (f32[64,128]{1,0:T(8,128)S(1)}, f32[64,128]{1,0:T(8,128)S(1)}, u32[]{:S(2)}, u32[]{:S(2)}) collective-permute-start(f32[64,128]{1,0:T(8,128)S(1)} %fusion), channel_id=1, source_target_pairs={{0,4},{1,5},{2,6},{3,7},{4,0},{5,1},{6,2},{7,3},{8,12},{9,13},{10,... | collective-permute-start | bytes 98312 | tf_op jit(solution)/shard_map/ppermute | solution.py:612
  112.4 4.3 %collective-permute-start.11 = (f32[64,128]{1,0:T(8,128)S(1)}, f32[64,128]{1,0:T(8,128)S(1)}, u32[]{:S(2)}, u32[]{:S(2)}) collective-permute-start(f32[64,128]{1,0:T(8,128)S(1)} %fusion), channel_id=1, source_target_pairs={{0,2},{1,3},{2,4},{3,5},{4,6},{5,7},{6,0},{7,1},{8,10},{9,11},{10,... | collective-permute-start | bytes 98312 | tf_op jit(solution)/shard_map/ppermute | solution.py:612
  128.6 5.1 %collective-permute-start.14 = (f32[64,128]{1,0:T(8,128)S(1)}, f32[64,128]{1,0:T(8,128)S(1)}, u32[]{:S(2)}, u32[]{:S(2)}) collective-permute-start(f32[64,128]{1,0:T(8,128)S(1)} %reduce_sum.9), channel_id=1, source_target_pairs={{0,1},{1,0},{2,3},{3,2},{4,5},{5,4},{6,7},{7,6},{8,9},{9,8},{10,11... | collective-permute-start | bytes 98312 | tf_op jit(solution)/shard_map/ppermute | solution.py:620
  133.7 3.2 %collective-permute-start.17 = (f32[2,64,128]{2,1,0:T(8,128)S(1)}, f32[2,64,128]{2,1,0:T(8,128)S(1)}, u32[]{:S(2)}, u32[]{:S(2)}) collective-permute-start(f32[2,64,128]{2,1,0:T(8,128)S(1)} %pad_maximum_fusion.both_ref), channel_id=1, source_target_pairs={{0,24},{8,0},{16,8},{24,16},{32,56},{40,32},{48,40},{56,48},{64,88... | collective-permute-start | bytes 196616 | tf_op jit(solution)/shard_map/ppermute | solution.py:612
  134.6 4.6 %collective-permute-start.16 = (f32[2,64,128]{2,1,0:T(8,128)S(1)}, f32[2,64,128]{2,1,0:T(8,128)S(1)}, u32[]{:S(2)}, u32[]{:S(2)}) collective-permute-start(f32[2,64,128]{2,1,0:T(8,128)S(1)} %pad_maximum_fusion.both_ref), channel_id=1, source_target_pairs={{0,16},{8,24},{16,0},{24,8},{32,48},{40,56},{48,32},{56,40},{64,80... | collective-permute-start | bytes 196616 | tf_op jit(solution)/shard_map/ppermute | solution.py:612
  135.4 5.3 %collective-permute-start.15 = (f32[2,64,128]{2,1,0:T(8,128)S(1)}, f32[2,64,128]{2,1,0:T(8,128)S(1)}, u32[]{:S(2)}, u32[]{:S(2)}) collective-permute-start(f32[2,64,128]{2,1,0:T(8,128)S(1)} %pad_maximum_fusion.both_ref), channel_id=1, source_target_pairs={{0,8},{8,16},{16,24},{24,0},{32,40},{40,48},{48,56},{56,32},{64,72... | collective-permute-start | bytes 196616 | tf_op jit(solution)/shard_map/ppermute | solution.py:612

commit v2 on v1

--- a/solution.py
+++ b/solution.py
@@ -16,7 +16,7 @@
 ROWS = COLS * CHUNKS
 BLOCK = 13
 MAP = 40
-PART = 200
+PART = 168
 F32 = jnp.float32
 BF16 = jnp.bfloat16
 VMEM = pltpu.VMEM
@@ -133,12 +133,10 @@
         out_ref[0:64, :] = x[:, :LANES]
         out_ref[64:128, :] = x[:, LANES:]
         cot = jnp.where(first, cots[0], cots[1])
-        low = jnp.concatenate([cot, zero], axis=1)
-        high = jnp.concatenate([zero, cot], axis=1)
-        out_ref[128:192, :] = jnp.where(odd == 0, low, high)
+        out_ref[128:160, :] = jnp.concatenate([cot[:32], cot[32:]], axis=1)
         start = jnp.where(first, h_ref[0:1, :], h_ref[1:2, :])
         start = jnp.concatenate([start, start], axis=1)
-        out_ref[192:200, :] = jnp.broadcast_to(start, (8, LANES))
+        out_ref[160:168, :] = jnp.broadcast_to(start, (8, LANES))
 
 
 def coefficients(prev, x3, bias, w3):
@@ -197,19 +195,51 @@
     return maps_ref[STEPS - 1, pl.ds(c, H, stride=CHUNKS), :]
 
 
-def chain_chunks(maps_ref, prefix_ref):
+def chunk_vector(maps_ref, c):
+    return maps_ref[STEPS - 1, H * CHUNKS + c : H * CHUNKS + c + 1, :]
+
+
+def compose(earlier, later):
     row = lax.broadcasted_iota(jnp.int32, (72, LANES), 0)
-    total = None
-    for c in range(CHUNKS):
-        matrix = chunk_matrix(maps_ref, c)
-        vector = maps_ref[STEPS - 1, H * CHUNKS + c : H * CHUNKS + c + 1, :]
-        if c == 0:
-            total = jnp.concatenate([matrix, vector, jnp.zeros((7, LANES), F32)], axis=0)
-        else:
-            total = mm(left3(total), right3(block_diagonal(matrix)))
-            total = total + jnp.where(row == H, vector, 0.0)
-        prefix_ref[c] = total
-    return total
+    both = mm(left3(earlier), right3(block_diagonal(later[:H])))
+    return both + jnp.where(row == H, later[H : H + 1], 0.0)
+
+
+def compose_chunks(maps_ref):
+    pad = jnp.zeros((7, LANES), F32)
+    parts = [
+        jnp.concatenate([chunk_matrix(maps_ref, c), chunk_vector(maps_ref, c), pad], axis=0) for c in range(CHUNKS)
+    ]
+    while len(parts) > 1:
+        parts = [compose(a, b) for a, b in zip(parts[::2], parts[1::2])]
+    return parts[0]
+
+
+def flip_halves(matrix):
+    turned = jnp.transpose(matrix)
+    return jnp.concatenate([turned[:H], turned[H:]], axis=1)
+
+
+def diagonal(rows):
+    row = lax.broadcasted_iota(jnp.int32, (H, LANES), 0)
+    lane = lax.broadcasted_iota(jnp.int32, (H, LANES), 1) % H
+    return jnp.where(row == lane, rows, 0.0)
+
+
+def to_column(row, matrix, vector):
+    low = lane_low(matrix.shape)
+    prod = matrix * row + diagonal(vector)
+    first = jnp.sum(jnp.where(low, prod, 0.0), axis=1, keepdims=True)
+    second = jnp.sum(jnp.where(low, 0.0, prod), axis=1, keepdims=True)
+    return jnp.where(low, first, second)
+
+
+def to_row(column, matrix, vector):
+    return jnp.sum(column * matrix, axis=0, keepdims=True) + vector
+
+
+def as_row(column):
+    return jnp.sum(diagonal(column), axis=0, keepdims=True)
 
 
 def join_halves(total):
@@ -288,19 +318,27 @@
     return mm(jnp.concatenate([high, low, rest], axis=1), jnp.concatenate([one, one, one], axis=0))
 
 
-def enter_chunks(state, prefix_ref):
+def store_chunks(maps_ref, chunk_ref, flipped):
+    for c in range(CHUNKS):
+        matrix = chunk_matrix(maps_ref, c)
+        chunk_ref[c] = flip_halves(matrix) if c % 2 == flipped else matrix
+
+
+def enter_chunks(state, maps_ref, chunk_ref, ends_ref):
     low = lane_low((CHUNKS, LANES))
-    ends = prefix_ref[CHUNKS - 1]
-    first = doubled(ends, 0)
+    first = doubled(ends_ref[...], 0)
     middle = apply_row(state, first[:H], first[H : H + 1])
-    halves = jnp.where(low, state, middle)
-    column = spread(halves[0:1], H)
+    entering = jnp.where(low, state, middle)
     row = lax.broadcasted_iota(jnp.int32, (CHUNKS, LANES), 0)
-    entering = halves
-    for c in range(1, CHUNKS):
-        before = prefix_ref[c - 1]
-        value = jnp.sum(before[:H] * column, axis=0, keepdims=True) + before[H : H + 1]
-        entering = jnp.where(row == c, value, entering)
+    value = entering[0:1]
+    for c in range(CHUNKS - 1):
+        vector = chunk_vector(maps_ref, c)
+        if c % 2 == 0:
+            column = to_column(value, chunk_ref[c], vector)
+            value = as_row(column)
+        else:
+            value = to_row(column, chunk_ref[c], vector)
+        entering = jnp.where(row == c + 1, value, entering)
     return entering
 
 
@@ -315,17 +353,19 @@
     return states
 
 
-def phase(where_ref, prev, x3_ref, bias_ref, w3_ref, ws_ref, ud_ref, maps_ref, prefix_ref, out_ref):
+def phase(where_ref, prev, x3_ref, bias_ref, w3_ref, ws_ref, ud_ref, maps_ref, chunk_ref, ends_ref, out_ref):
     coef = coefficients(prev, x3_ref, bias_ref[...], w3_ref[...])
     scan_maps(coef, ws_ref, ud_ref, maps_ref)
-    total = chain_chunks(maps_ref, prefix_ref)
+    total = compose_chunks(maps_ref)
+    store_chunks(maps_ref, chunk_ref, 0)
+    ends_ref[...] = total
     total = join_halves(total)
     send_map(total, flip(total[:H]), where_ref, out_ref)
 
 
 def first_kernel(
     where_ref, a_ref, b_ref, w_ref, w3_ref, ws_ref, ud_ref, bias_ref,
-    x3_ref, xin_ref, cot_ref, start_ref, maps_ref, prefix_ref, out_ref,
+    x3_ref, xin_ref, cot_ref, start_ref, maps_ref, chunk_ref, ends_ref, out_ref, natural_ref,
 ):
     odd, mine = where_ref[0], where_ref[2]
     pieces = []
@@ -338,11 +378,12 @@
             pieces.append(jnp.concatenate(rows, axis=1))
     xin = jnp.concatenate(pieces, axis=0).astype(BF16)
     xin_ref[...] = xin
-    cot_ref[...] = jnp.concatenate(
-        [a_ref[pl.ds(128 + j, 8, stride=8), :] + b_ref[pl.ds(128 + j, 8, stride=8), :] for j in range(STEPS)],
-        axis=0,
-    )
-    start = a_ref[192:200, :]
+    cots = [jnp.where(odd == v, a_ref[128:160, :], b_ref[128:160, :]) for v in range(2)]
+    low = lane_low((32, LANES))
+    natural_ref[0:32, :] = jnp.where(low, cots[0], swap_halves(cots[1]))
+    natural_ref[32:64, :] = jnp.where(low, swap_halves(cots[0]), cots[1])
+    cot_ref[...] = jnp.concatenate([natural_ref[pl.ds(j, 8, stride=8), :] for j in range(STEPS)], axis=0)
+    start = a_ref[160:168, :]
     start_ref[...] = start
     flat = mm_nt(xin, w_ref[...])
     bias = bias_ref[...]
@@ -353,18 +394,18 @@
     lane = lax.broadcasted_iota(jnp.int32, (64, LANES), 1)
     here = (row == 0) & (lane < H) & (mine == 0)
     prev = jnp.where(here, start[0:1, :], 0.0)
-    phase(where_ref, prev, x3_ref, bias_ref, w3_ref, ws_ref, ud_ref, maps_ref, prefix_ref, out_ref)
+    phase(where_ref, prev, x3_ref, bias_ref, w3_ref, ws_ref, ud_ref, maps_ref, chunk_ref, ends_ref, out_ref)
 
 
 def next_kernel(
-    where_ref, own_ref, other_ref, start_ref, x3_ref, bias_ref, w3_ref, ws_ref, ud_ref, old_ref, before_ref,
-    maps_ref, prefix_ref, out_ref, spread_ref,
+    where_ref, own_ref, other_ref, start_ref, x3_ref, bias_ref, w3_ref, ws_ref, ud_ref, old_ref, pieces_ref, before_ref,
+    maps_ref, chunk_ref, ends_ref, out_ref, spread_ref,
 ):
     state = enter_device(where_ref, own_ref, other_ref, start_ref[...], False)
-    entering = enter_chunks(state, before_ref)
+    entering = enter_chunks(state, old_ref, pieces_ref, before_ref)
     states = trajectory(entering, old_ref, spread_ref)
     prev = jnp.concatenate([entering] + states[:-1], axis=0)
-    phase(where_ref, prev, x3_ref, bias_ref, w3_ref, ws_ref, ud_ref, maps_ref, prefix_ref, out_ref)
+    phase(where_ref, prev, x3_ref, bias_ref, w3_ref, ws_ref, ud_ref, maps_ref, chunk_ref, ends_ref, out_ref)
 
 
 def half_sums(value):
@@ -376,12 +417,12 @@
 
 
 def turn_kernel(
-    where_ref, own_ref, other_ref, start_ref, x3_ref, bias_ref, w3_ref, ws_ref, ud_ref, old_ref, before_ref, cot_ref,
+    where_ref, own_ref, other_ref, start_ref, x3_ref, bias_ref, w3_ref, ws_ref, ud_ref, old_ref, pieces_ref, before_ref, cot_ref,
     states_ref, coef_ref, chunk_ref, vector_ref, half_ref, out_ref,
-    spread_ref, maps_ref, prefix_ref, acc_ref,
+    spread_ref, maps_ref, acc_ref,
 ):
     state = enter_device(where_ref, own_ref, other_ref, start_ref[...], False)
-    entering = enter_chunks(state, before_ref)
+    entering = enter_chunks(state, old_ref, pieces_ref, before_ref)
     states = trajectory(entering, old_ref, spread_ref)
     for j in range(STEPS):
         states_ref[pl.ds(j, CHUNKS, stride=STEPS), :] = states[j]
@@ -391,7 +432,8 @@
     for n in range(5):
         coef_ref[n + 1] = coef[n]
     scan_maps(coef, ws_ref, ud_ref, maps_ref)
-    total = chain_chunks(maps_ref, prefix_ref)
+    total = compose_chunks(maps_ref)
+    store_chunks(maps_ref, chunk_ref, 0)
     for b in range(0, H * CHUNKS, 64):
         acc = jnp.zeros((8, CHUNKS, LANES), F32)
         for j in range(STEPS):
@@ -400,15 +442,15 @@
         acc_ref[b : b + 64, :] = acc.reshape(64, LANES)
     vectors = []
     for c in range(CHUNKS):
-        chunk_ref[c] = chunk_matrix(maps_ref, c)
         sums = half_sums(acc_ref[pl.ds(c, H, stride=CHUNKS), :])
         vectors.append(jnp.concatenate([sums[0:1], sums[1:2]], axis=1))
     vector_ref[...] = jnp.concatenate(vectors, axis=0)
-    whole = jnp.zeros((H, LANES), F32)
-    for c in range(1, CHUNKS):
-        whole = whole + prefix_ref[c - 1][:H] * vectors[c]
-    sums = half_sums(whole)
-    ends = jnp.concatenate([sums[0:1], sums[1:2]], axis=1) + vectors[0]
+    ends = jnp.zeros((1, LANES), F32)
+    for c in reversed(range(CHUNKS)):
+        if c % 2 == 1:
+            column = to_column(ends, chunk_ref[c], vectors[c])
+        else:
+            ends = to_row(column, chunk_ref[c], vectors[c])
     tail = doubled(ends, 1)
     low = lane_low((H, LANES))
     sums = half_sums(jnp.where(low, total[:H], 0.0) * tail)
@@ -429,11 +471,15 @@
     right = enter_device(where_ref, own_ref, other_ref, jnp.zeros((CHUNKS, LANES), F32), True)
     half = half_ref[...]
     middle = apply_row(right, half[:H], half[H : H + 1])
-    value = jnp.where(low, middle, right)
-    passed = value
+    passed = jnp.where(low, middle, right)
+    value = passed[0:1]
     for c in reversed(range(1, CHUNKS)):
-        high, low_part = split(block_diagonal(chunk_ref[c]))
-        value = mm_nt(left3(value), jnp.concatenate([high, high, low_part], axis=1)) + vector_ref[c : c + 1, :]
+        vector = vector_ref[c : c + 1, :]
+        if c % 2 == 1:
+            column = to_column(value, chunk_ref[c], vector)
+            value = as_row(column)
+        else:
+            value = to_row(column, chunk_ref[c], vector)
         passed = jnp.where(row < c, value, passed)
     dz, dr, dn, ds = [None] * STEPS, [None] * STEPS, [None] * STEPS, [None] * STEPS
     for j in reversed(range(STEPS)):
@@ -486,14 +532,9 @@
         home_ref[d] = jnp.where(lane_low((32, LANES)), block[:32], swap_halves(block[32:]))
 
 
-def unpack_kernel(
-    where_ref, one_ref, two_ref, three_ref, both_ref, home_ref, early0_ref, early1_ref, early2_ref,
-    in_ref, rec_ref, scale_ref, bias_ref, traj_ref, full_ref,
-):
+def home_kernel(where_ref, home_ref, one_ref, two_ref, three_ref, traj_ref):
     core, x = where_ref[1], where_ref[3]
-    pieces = (both_ref, one_ref, two_ref, three_ref)
-    early = (early0_ref, early1_ref, early2_ref)
-    blocks = [home_ref[0]] + [ref[64:96, :] for ref in early]
+    blocks = [home_ref[0]] + [ref[64:96, :] for ref in (one_ref, two_ref, three_ref)]
     for e in range(2):
         where = lax.rem(x + 4 - 2 * core - e, 4)
         block = blocks[0]
@@ -501,6 +542,13 @@
             block = jnp.where(where == d, blocks[d], block)
         block = jnp.concatenate([block, swap_halves(block)], axis=0)
         traj_ref[:, e, :] = jnp.transpose(block)[:H]
+
+
+def unpack_kernel(
+    where_ref, one_ref, two_ref, three_ref, both_ref, in_ref, rec_ref, scale_ref, bias_ref, full_ref
+):
+    x = where_ref[3]
+    pieces = (both_ref, one_ref, two_ref, three_ref)
     for d in range(4):
         part = lax.rem(x + 4 - d, 4)
         for core in range(2):
@@ -518,6 +566,10 @@
 def call(kernel, outs, kinds, *operands, scratch=()):
     spaces = {"s": SMEM, "v": VMEM, "h": pltpu.HBM}
     specs = [pl.BlockSpec(memory_space=spaces[kind]) for kind in kinds]
+    operands = [
+        pltpu.with_memory_space_constraint(operand, pltpu.HBM) if kind == "h" else operand
+        for kind, operand in zip(kinds, operands)
+    ]
     return pl.pallas_call(
         kernel,
         out_shape=[jax.ShapeDtypeStruct(*out) for out in outs],
@@ -574,29 +626,31 @@
         "hhhh", u_rec, timescale[None, :], other_bias, w_in.T,
         scratch=[pltpu.VMEM((H, 192), F32), pltpu.VMEM((1, H), F32), pltpu.VMEM((3, H), F32), sems],
     )
-    maps_t, prefix_t, send_t = ((STEPS, ROWS, LANES), F32), ((CHUNKS, 72, LANES), F32), ((planes, MAP, LANES), F32)
-    x3, xin, cot, start, maps, prefix, send = call(
+    maps_t, chunk_t = ((STEPS, ROWS, LANES), F32), ((CHUNKS, H, LANES), F32)
+    ends_t, send_t = ((72, LANES), F32), ((planes, MAP, LANES), F32)
+    x3, xin, cot, start, maps, chunk, ends, send = call(
         first_kernel,
-        [((3, 64, LANES), F32), ((128, 256), BF16), ((64, LANES), F32), ((8, LANES), F32), maps_t, prefix_t, send_t],
+        [((3, 64, LANES), F32), ((128, 256), BF16), ((64, LANES), F32), ((8, LANES), F32), maps_t, chunk_t, ends_t, send_t],
         "svvvvvvv", where, one, two, w, w3, ws, ud, bias,
+        scratch=[pltpu.VMEM((64, LANES), F32)],
     )
     spread_s = pltpu.VMEM((H * CHUNKS, LANES), F32)
     for _ in range(NEWTON - 1):
         own, other = exchange(send)
-        maps, prefix, send = call(
-            next_kernel, [maps_t, prefix_t, send_t], "svvvvvvvvvv",
-            where, own, other, start, x3, bias, w3, ws, ud, maps, prefix, scratch=[spread_s],
+        maps, chunk, ends, send = call(
+            next_kernel, [maps_t, chunk_t, ends_t, send_t], "svvvvvvvvvvv",
+            where, own, other, start, x3, bias, w3, ws, ud, maps, chunk, ends, scratch=[spread_s],
         )
     own, other = exchange(send)
     states, coef, chunk, vector, half, send = call(
         turn_kernel,
         [
-            ((64, LANES), F32), ((6, 64, LANES), F32), ((CHUNKS, H, LANES), F32),
+            ((64, LANES), F32), ((6, 64, LANES), F32), chunk_t,
             ((8, LANES), F32), ((72, LANES), F32), send_t,
         ],
-        "svvvvvvvvvvv", where, own, other, start, x3, bias, w3, ws, ud, maps, prefix, cot,
+        "svvvvvvvvvvvv", where, own, other, start, x3, bias, w3, ws, ud, maps, chunk, ends, cot,
         scratch=[
-            spread_s, pltpu.VMEM(*maps_t), pltpu.VMEM(*prefix_t),
+            spread_s, pltpu.VMEM(*maps_t),
             pltpu.VMEM((H * CHUNKS, LANES), F32),
         ],
     )
@@ -621,10 +675,11 @@
     first = core == 0
     both = jnp.stack([jnp.where(first, part, other), jnp.where(first, other, part)])
     rest = around([both] * (width - 1), "seq", step_x)
-    grad_in, grad_rec, grad_scale, grad_other, traj = call(
+    (traj,) = call(home_kernel, [((H, 2, 64), F32)], "svvvv", where, home, *early)
+    grad_in, grad_rec, grad_scale, grad_other = call(
         unpack_kernel,
-        [((192, 256), F32), ((H, 192), F32), ((1, H), F32), ((3, H), F32), ((H, 2, 64), F32)], "svvvvvvvv",
-        where, *rest, both, home, *early, scratch=[pltpu.VMEM((512, LANES), F32)],
+        [((192, 256), F32), ((H, 192), F32), ((1, H), F32), ((3, H), F32)], "svvvv",
+        where, *rest, both, scratch=[pltpu.VMEM((512, LANES), F32)],
     )
     return traj, grad_in.T, grad_rec, grad_scale[0], grad_other
 

time: 143 us -> 140 us (0.979)
  local copies, waits for them, and re-layouts: 5.46 us -> 0.03 us
    unnamed x14 -> x0, local copies, waits for them, and re-layouts: 5.43 us -> none
    ppermute x1, waiting for transfers between devices: 1.21 us -> 3.05 us  [local(): two = lax.ppermute(two, axes, there[1])]
    pallas_call x8 -> x9, Pallas kernels: 28 us -> 29.2 us  [call(): pl.pallas_call(kernel, out_shape=[jax.ShapeDtypeStruct(*out) for out in o...]
  transfers between devices with their start and end apart: 18 -> 18, of which waited for: 15 -> 15; matrix products, arithmetic and copies ran while one was open for 0% -> 0% of each run, Pallas kernels for 0% -> 2%
where the time goes in v2:
time: 140 us; the launch traced here: 139 us
  blocking collectives  63.7 us (46%)
  Pallas kernels  29.2 us (21%)
  starting transfers between devices  24.8 us (18%)
  waiting for transfers between devices  20.5 us (15%)
    all_to_all x4, blocking collectives, exchange(): lax.all_to_all(value, 'seq', 0, 0, axis_index_groups=along_z, tiled=True)  51.9 us
    pallas_call x9, Pallas kernels, call(): pl.pallas_call(kernel, out_shape=[jax.ShapeDtypeStruct(*out) for out in o...  29.2 us
    all_to_all x1, blocking collectives, local(): lax.all_to_all(wide, 'seq', 0, 0, axis_index_groups=along_z, tiled=True)  11.8 us
    ppermute x9, waiting for transfers between devices, around(): lax.ppermute(value, axis, pair)  10.5 us
    ppermute x9, starting transfers between devices, around(): lax.ppermute(value, axis, pair)  9.89 us
    ppermute x1, starting transfers between devices, local(): one = lax.ppermute(one, axes, there[0])  6.04 us
    ppermute x1, starting transfers between devices, local(): other = lax.ppermute(part, 'batch', cores)  4.17 us
    ppermute x4, starting transfers between devices, exchange(): return (own, lax.ppermute(own, 'batch', cores))  3.73 us
  transfers between devices with their start and end apart: 18, of which 15 were waited for; matrix products, arithmetic and copies ran while one was open for 0% of the time, Pallas kernels for 2%

profile of v2, /device:TPU:1, one launch (start us, length us, event | category | flops | bytes accessed | tf_op | source)
XLA Modules:
  0.0 139.2 jit_solution(395063780219161965)
XLA Ops:
  0.7 0.1 pad_add_fusion.where_ref
  0.8 1.6 %shard_map.110 = (f32[168,128]{1,0:T(8,128)S(1)}, f32[168,128]{1,0:T(8,128)S(1)}) custom-call(s32[4]{0:T(128)S(1)} %pad_add_fusion.where_ref, bf16[2,64,256]{2,1,0:T(8,128)(2,1)} %x_hbm.1, f32[64,2,64]{2,1,0:T(2,128)} %cot_hbm.1, f32[2,64]{1,0:T(2,128)} %bitcast.20), custom_call_target="tpu_custom_call" | custom-call | tf_op jit(solution)/shard_map/pallas_call | solution.py:573
  2.4 6.0 %collective-permute-start = (f32[168,128]{1,0:T(8,128)S(1)}, f32[168,128]{1,0:T(8,128)S(1)}, u32[]{:S(2)}, u32[]{:S(2)}) collective-permute-start(f32[168,128]{1,0:T(8,128)S(1)} %get-tuple-element.43), channel_id=1, source_target_pairs={{0,0},{1,16},{2,2},{3,18},{4,4},{5,20},{6,6},{7,22},{8,8},{9,24},{... | collective-permute-start | bytes 258056 | tf_op jit(solution)/shard_map/ppermute | solution.py:618
  8.4 0.7 collective-permute-start.1
  9.1 1.2 shard_map.111
  10.3 0.3 collective-permute-done.a_ref
  10.6 3.1 %collective-permute-done.1.b_ref = f32[168,128]{1,0:T(8,128)S(1)} collective-permute-done((f32[168,128]{1,0:T(8,128)S(1)}, f32[168,128]{1,0:T(8,128)S(1)}, u32[]{:S(2)}, u32[]{:S(2)}) %collective-permute-start.1) | collective-permute-done | bytes 86048 | tf_op jit(solution)/shard_map/ppermute | solution.py:619
  13.6 3.7 %shard_map.112 = (f32[3,64,128]{2,1,0:T(8,128)S(1)}, bf16[128,256]{1,0:T(8,128)(2,1)S(1)}, f32[64,128]{1,0:T(8,128)S(1)}, f32[8,128]{1,0:T(8,128)S(1)}, f32[8,52...) custom-call(s32[4]{0:T(128)S(1)} %pad_add_fusion.where_ref, ...), custom_call_target="tpu_custom_call" | custom-call | tf_op jit(solution)/shard_map/pallas_call | solution.py:573
  17.3 16.3 %all_to_all.25.own_ref = f32[8,40,128]{2,1,0:T(8,128)S(1)} all-to-all(f32[8,40,128]{2,1,0:T(8,128)S(1)} %get-tuple-element.50), channel_id=1, replica_groups={{0,32,64,96,128,160,192,224},{8,40,72,104,136,168,200,232},{16,48,80,11..., dimensions={0} | all-to-all | bytes 327680 | tf_op jit(solution)/shard_map/all_to_all | solution.py:608
  33.6 0.0 collective-permute-start.2
  33.6 1.4 collective-permute-done.2.other_ref
  35.0 5.3 %shard_map.113 = (f32[8,520,128]{2,1,0:T(8,128)S(1)}, f32[8,64,128]{2,1,0:T(8,128)S(1)}, f32[72,128]{1,0:T(8,128)S(1)}, f32[8,40,128]{2,1,0:T(8,128)S(1)}) custom-call(s32[4]{0:T(128)S(1)} %pad_add_fusion.where_ref, f32[8,40,128]{2,1,0:T(8,128)S(1)} %all_to_all.25.own_ref, f32[8,40,128]{2,1,0:T(8,128)S(1)} %collective-permute-done.2.other_ref, ...), custom_call_target="tpu_custom_call" | custom-call | tf_op jit(solution)/shard_map/pallas_call | solution.py:573
  40.3 12.5 %all_to_all.26.own_ref = f32[8,40,128]{2,1,0:T(8,128)S(1)} all-to-all(f32[8,40,128]{2,1,0:T(8,128)S(1)} %get-tuple-element.56), channel_id=1, replica_groups={{0,32,64,96,128,160,192,224},{8,40,72,104,136,168,200,232},{16,48,80,11..., dimensions={0} | all-to-all | bytes 327680 | tf_op jit(solution)/shard_map/all_to_all | solution.py:608
  52.8 0.6 collective-permute-start.3
  53.4 1.0 collective-permute-done.3.other_ref
  54.5 5.3 %shard_map.114 = (f32[8,520,128]{2,1,0:T(8,128)S(1)}, f32[8,64,128]{2,1,0:T(8,128)S(1)}, f32[72,128]{1,0:T(8,128)S(1)}, f32[8,40,128]{2,1,0:T(8,128)S(1)}) custom-call(s32[4]{0:T(128)S(1)} %pad_add_fusion.where_ref, f32[8,40,128]{2,1,0:T(8,128)S(1)} %all_to_all.26.own_ref, f32[8,40,128]{2,1,0:T(8,128)S(1)} %collective-permute-done.3.other_ref, ...), custom_call_target="tpu_custom_call" | custom-call | tf_op jit(solution)/shard_map/pallas_call | solution.py:573
  59.8 11.5 %all_to_all.27.own_ref = f32[8,40,128]{2,1,0:T(8,128)S(1)} all-to-all(f32[8,40,128]{2,1,0:T(8,128)S(1)} %get-tuple-element.60), channel_id=1, replica_groups={{0,32,64,96,128,160,192,224},{8,40,72,104,136,168,200,232},{16,48,80,11..., dimensions={0} | all-to-all | bytes 327680 | tf_op jit(solution)/shard_map/all_to_all | solution.py:608
  71.3 1.6 %collective-permute-start.4 = (f32[8,40,128]{2,1,0:T(8,128)S(1)}, f32[8,40,128]{2,1,0:T(8,128)S(1)}, u32[]{:S(2)}, u32[]{:S(2)}) collective-permute-start(f32[8,40,128]{2,1,0:T(8,128)S(1)} %all_to_all.27.own_ref), channel_id=1, source_target_pairs={{0,1},{1,0},{2,3},{3,2},{4,5},{5,4},{6,7},{7,6},{8,9},{9,8},{10,11... | collective-permute-start | bytes 491528 | tf_op jit(solution)/shard_map/ppermute | solution.py:609
  72.9 1.0 collective-permute-done.4.other_ref
  73.9 6.1 %shard_map.115 = (f32[64,128]{1,0:T(8,128)S(1)}, f32[6,64,128]{2,1,0:T(8,128)S(1)}, f32[8,64,128]{2,1,0:T(8,128)S(1)}, f32[8,128]{1,0:T(8,128)S(1)}, f32[72,128]{1,0:T(8,128)S(1)}, /*index=5*/f32[8,40,128]{2,1,0:T(8,128)S(1)}) custom-call(s32[4]{0:T(128)S(1)} %pad_add_fusion.where_ref, f32[8,40,128]{2,1,0:T(8,128)S(1)} %all_to_all.27.own_ref, ...), custom_call_target="tpu_custom_call" | custom-call | tf_op jit(solution)/shard_map/pallas_call | solution.py:573
  80.1 11.5 %all_to_all.28.own_ref = f32[8,40,128]{2,1,0:T(8,128)S(1)} all-to-all(f32[8,40,128]{2,1,0:T(8,128)S(1)} %get-tuple-element.65), channel_id=1, replica_groups={{0,32,64,96,128,160,192,224},{8,40,72,104,136,168,200,232},{16,48,80,11..., dimensions={0} | all-to-all | bytes 327680 | tf_op jit(solution)/shard_map/all_to_all | solution.py:608
  91.6 1.6 %collective-permute-start.5 = (f32[8,40,128]{2,1,0:T(8,128)S(1)}, f32[8,40,128]{2,1,0:T(8,128)S(1)}, u32[]{:S(2)}, u32[]{:S(2)}) collective-permute-start(f32[8,40,128]{2,1,0:T(8,128)S(1)} %all_to_all.28.own_ref), channel_id=1, source_target_pairs={{0,1},{1,0},{2,3},{3,2},{4,5},{5,4},{6,7},{7,6},{8,9},{9,8},{10,11... | collective-permute-start | bytes 491528 | tf_op jit(solution)/shard_map/ppermute | solution.py:609
  93.2 0.0 collective-permute-start.6
  93.2 1.2 collective-permute-done.6.across_ref
  94.4 0.0 collective-permute-done.5.other_ref
  94.4 3.3 %shard_map.116 = (f32[256,128]{1,0:T(8,128)S(1)}, f32[256,128]{1,0:T(8,128)S(1)}, f32[4,32,128]{2,1,0:T(8,128)S(1)}) custom-call(s32[4]{0:T(128)S(1)} %pad_add_fusion.where_ref, f32[8,40,128]{2,1,0:T(8,128)S(1)} %all_to_all.28.own_ref, f32[8,40,128]{2,1,0:T(8,128)S(1)} %collective-permute-done.5.other_ref, f32[6,64,128]{2,1,0:T(8,128)S(1)} %get-tuple-element.66.coef_ref, ...), custom_call_target="tpu_custom_call" | custom-call | tf_op jit(solution)/shard_map/pallas_call | solution.py:573
  97.7 0.3 collective-permute-start.7
  98.0 1.1 collective-permute-done.7
  99.2 0.1 collective-permute-start.8
  99.3 3.2 %collective-permute-start.9 = (f32[96,128]{1,0:T(8,128)S(1)}, f32[96,128]{1,0:T(8,128)S(1)}, u32[]{:S(2)}, u32[]{:S(2)}) collective-permute-start(f32[96,128]{1,0:T(8,128)S(1)} %pad_maximum_fusion.2), channel_id=1, source_target_pairs={{0,16},{8,24},{16,0},{24,8},{32,48},{40,56},{48,32},{56,40},{64,80... | collective-permute-start | bytes 147464 | tf_op jit(solution)/shard_map/ppermute | solution.py:666
  102.5 0.4 collective-permute-start.10
  102.9 0.5 collective-permute-done.8.one_ref
  103.4 1.5 %collective-permute-done.9.two_ref = f32[96,128]{1,0:T(8,128)S(1)} collective-permute-done((f32[96,128]{1,0:T(8,128)S(1)}, f32[96,128]{1,0:T(8,128)S(1)}, u32[]{:S(2)}, u32[]{:S(2)}) %collective-permute-start.9) | collective-permute-done | bytes 49184 | tf_op jit(solution)/shard_map/ppermute | solution.py:666
  104.9 0.9 collective-permute-done.10.three_ref
  105.8 2.8 %collective-permute-start.13 = (f32[64,128]{1,0:T(8,128)S(1)}, f32[64,128]{1,0:T(8,128)S(1)}, u32[]{:S(2)}, u32[]{:S(2)}) collective-permute-start(f32[64,128]{1,0:T(8,128)S(1)} %fusion), channel_id=1, source_target_pairs={{0,6},{1,7},{2,0},{3,1},{4,2},{5,3},{6,4},{7,5},{8,14},{9,15},{10,... | collective-permute-start | bytes 98312 | tf_op jit(solution)/shard_map/ppermute | solution.py:666
  108.6 0.3 collective-permute-start.12
  109.0 0.7 collective-permute-start.11
  109.7 0.0 collective-permute-done.13
  109.7 3.3 %collective-permute-done.12 = f32[64,128]{1,0:T(8,128)S(1)} collective-permute-done((f32[64,128]{1,0:T(8,128)S(1)}, f32[64,128]{1,0:T(8,128)S(1)}, u32[]{:S(2)}, u32[]{:S(2)}) %collective-permute-start.12) | collective-permute-done | bytes 32800 | tf_op jit(solution)/shard_map/ppermute | solution.py:666
  112.9 0.3 collective-permute-done.11
  113.3 11.8 %all_to_all.29 = f32[8,64,128]{2,1,0:T(8,128)S(1)} all-to-all(f32[8,64,128]{2,1,0:T(8,128)S(1)} %broadcast_in_dim.10), channel_id=1, replica_groups={{0,32,64,96,128,160,192,224},{8,40,72,104,136,168,200,232},{16,48,80,11..., dimensions={0} | all-to-all | bytes 524288 | tf_op jit(solution)/shard_map/all_to_all | solution.py:673
  125.1 4.2 %collective-permute-start.14 = (f32[64,128]{1,0:T(8,128)S(1)}, f32[64,128]{1,0:T(8,128)S(1)}, u32[]{:S(2)}, u32[]{:S(2)}) collective-permute-start(f32[64,128]{1,0:T(8,128)S(1)} %reduce_sum.9), channel_id=1, source_target_pairs={{0,1},{1,0},{2,3},{3,2},{4,5},{5,4},{6,7},{7,6},{8,9},{9,8},{10,11... | collective-permute-start | bytes 98312 | tf_op jit(solution)/shard_map/ppermute | solution.py:674
  129.3 0.9 collective-permute-done.14
  130.2 1.7 %collective-permute-start.17 = (f32[2,64,128]{2,1,0:T(8,128)S(1)}, f32[2,64,128]{2,1,0:T(8,128)S(1)}, u32[]{:S(2)}, u32[]{:S(2)}) collective-permute-start(f32[2,64,128]{2,1,0:T(8,128)S(1)} %pad_maximum_fusion.both_ref), channel_id=1, source_target_pairs={{0,24},{8,0},{16,8},{24,16},{32,56},{40,32},{48,40},{56,48},{64,88... | collective-permute-start | bytes 196616 | tf_op jit(solution)/shard_map/ppermute | solution.py:666
  131.9 0.2 collective-permute-start.16
  132.1 0.4 collective-permute-start.15
  132.5 1.3 shard_map.117
  133.9 0.0 collective-permute-done.17.three_ref
  133.9 2.7 %collective-permute-done.16.two_ref = f32[2,64,128]{2,1,0:T(8,128)S(1)} collective-permute-done((f32[2,64,128]{2,1,0:T(8,128)S(1)}, f32[2,64,128]{2,1,0:T(8,128)S(1)}, u32[]{:S(2)}, u32[]{:S(2)}) %collective-permute-start.16) | collective-permute-done | bytes 65568 | tf_op jit(solution)/shard_map/ppermute | solution.py:666
  136.6 1.4 collective-permute-done.15.one_ref
  137.9 1.3 shard_map.118
  (12 shorter events, 0.1 us)
Async XLA Ops:
  2.4 8.2 %collective-permute-start = (f32[168,128]{1,0:T(8,128)S(1)}, f32[168,128]{1,0:T(8,128)S(1)}, u32[]{:S(2)}, u32[]{:S(2)}) collective-permute-start(f32[168,128]{1,0:T(8,128)S(1)} %get-tuple-element.43), channel_id=1, source_target_pairs={{0,0},{1,16},{2,2},{3,18},{4,4},{5,20},{6,6},{7,22},{8,8},{9,24},{... | collective-permute-start | bytes 258056 | tf_op jit(solution)/shard_map/ppermute | solution.py:618
  8.4 5.2 %collective-permute-start.1 = (f32[168,128]{1,0:T(8,128)S(1)}, f32[168,128]{1,0:T(8,128)S(1)}, u32[]{:S(2)}, u32[]{:S(2)}) collective-permute-start(f32[168,128]{1,0:T(8,128)S(1)} %get-tuple-element.44), channel_id=1, source_target_pairs={{0,8},{1,24},{2,10},{3,26},{4,12},{5,28},{6,14},{7,30},{8,0},{9,16... | collective-permute-start | bytes 258056 | tf_op jit(solution)/shard_map/ppermute | solution.py:619
  33.6 1.4 %collective-permute-start.2 = (f32[8,40,128]{2,1,0:T(8,128)S(1)}, f32[8,40,128]{2,1,0:T(8,128)S(1)}, u32[]{:S(2)}, u32[]{:S(2)}) collective-permute-start(f32[8,40,128]{2,1,0:T(8,128)S(1)} %all_to_all.25.own_ref), channel_id=1, source_target_pairs={{0,1},{1,0},{2,3},{3,2},{4,5},{5,4},{6,7},{7,6},{8,9},{9,8},{10,11... | collective-permute-start | bytes 491528 | tf_op jit(solution)/shard_map/ppermute | solution.py:609
  52.8 1.6 %collective-permute-start.3 = (f32[8,40,128]{2,1,0:T(8,128)S(1)}, f32[8,40,128]{2,1,0:T(8,128)S(1)}, u32[]{:S(2)}, u32[]{:S(2)}) collective-permute-start(f32[8,40,128]{2,1,0:T(8,128)S(1)} %all_to_all.26.own_ref), channel_id=1, source_target_pairs={{0,1},{1,0},{2,3},{3,2},{4,5},{5,4},{6,7},{7,6},{8,9},{9,8},{10,11... | collective-permute-start | bytes 491528 | tf_op jit(solution)/shard_map/ppermute | solution.py:609
  71.3 2.6 %collective-permute-start.4 = (f32[8,40,128]{2,1,0:T(8,128)S(1)}, f32[8,40,128]{2,1,0:T(8,128)S(1)}, u32[]{:S(2)}, u32[]{:S(2)}) collective-permute-start(f32[8,40,128]{2,1,0:T(8,128)S(1)} %all_to_all.27.own_ref), channel_id=1, source_target_pairs={{0,1},{1,0},{2,3},{3,2},{4,5},{5,4},{6,7},{7,6},{8,9},{9,8},{10,11... | collective-permute-start | bytes 491528 | tf_op jit(solution)/shard_map/ppermute | solution.py:609
  91.6 2.8 %collective-permute-start.5 = (f32[8,40,128]{2,1,0:T(8,128)S(1)}, f32[8,40,128]{2,1,0:T(8,128)S(1)}, u32[]{:S(2)}, u32[]{:S(2)}) collective-permute-start(f32[8,40,128]{2,1,0:T(8,128)S(1)} %all_to_all.28.own_ref), channel_id=1, source_target_pairs={{0,1},{1,0},{2,3},{3,2},{4,5},{5,4},{6,7},{7,6},{8,9},{9,8},{10,11... | collective-permute-start | bytes 491528 | tf_op jit(solution)/shard_map/ppermute | solution.py:609
  93.2 1.2 collective-permute-start.6
  97.7 1.4 %collective-permute-start.7 = (f32[256,128]{1,0:T(8,128)S(1)}, f32[256,128]{1,0:T(8,128)S(1)}, u32[]{:S(2)}, u32[]{:S(2)}) collective-permute-start(f32[256,128]{1,0:T(8,128)S(1)} %get-tuple-element.76), channel_id=1, source_target_pairs={{0,1},{1,0},{2,3},{3,2},{4,5},{5,4},{6,7},{7,6},{8,9},{9,8},{10,11... | collective-permute-start | bytes 393224 | tf_op jit(solution)/shard_map/ppermute | solution.py:668
  99.2 4.2 %collective-permute-start.8 = (f32[96,128]{1,0:T(8,128)S(1)}, f32[96,128]{1,0:T(8,128)S(1)}, u32[]{:S(2)}, u32[]{:S(2)}) collective-permute-start(f32[96,128]{1,0:T(8,128)S(1)} %pad_maximum_fusion.1), channel_id=1, source_target_pairs={{0,8},{8,16},{16,24},{24,0},{32,40},{40,48},{48,56},{56,32},{64,72... | collective-permute-start | bytes 147464 | tf_op jit(solution)/shard_map/ppermute | solution.py:666
  99.3 5.6 %collective-permute-start.9 = (f32[96,128]{1,0:T(8,128)S(1)}, f32[96,128]{1,0:T(8,128)S(1)}, u32[]{:S(2)}, u32[]{:S(2)}) collective-permute-start(f32[96,128]{1,0:T(8,128)S(1)} %pad_maximum_fusion.2), channel_id=1, source_target_pairs={{0,16},{8,24},{16,0},{24,8},{32,48},{40,56},{48,32},{56,40},{64,80... | collective-permute-start | bytes 147464 | tf_op jit(solution)/shard_map/ppermute | solution.py:666
  102.5 3.3 %collective-permute-start.10 = (f32[96,128]{1,0:T(8,128)S(1)}, f32[96,128]{1,0:T(8,128)S(1)}, u32[]{:S(2)}, u32[]{:S(2)}) collective-permute-start(f32[96,128]{1,0:T(8,128)S(1)} %pad_maximum_fusion.3), channel_id=1, source_target_pairs={{0,24},{8,0},{16,8},{24,16},{32,56},{40,32},{48,40},{56,48},{64,88... | collective-permute-start | bytes 147464 | tf_op jit(solution)/shard_map/ppermute | solution.py:666
  105.8 3.9 %collective-permute-start.13 = (f32[64,128]{1,0:T(8,128)S(1)}, f32[64,128]{1,0:T(8,128)S(1)}, u32[]{:S(2)}, u32[]{:S(2)}) collective-permute-start(f32[64,128]{1,0:T(8,128)S(1)} %fusion), channel_id=1, source_target_pairs={{0,6},{1,7},{2,0},{3,1},{4,2},{5,3},{6,4},{7,5},{8,14},{9,15},{10,... | collective-permute-start | bytes 98312 | tf_op jit(solution)/shard_map/ppermute | solution.py:666
  108.6 4.3 %collective-permute-start.12 = (f32[64,128]{1,0:T(8,128)S(1)}, f32[64,128]{1,0:T(8,128)S(1)}, u32[]{:S(2)}, u32[]{:S(2)}) collective-permute-start(f32[64,128]{1,0:T(8,128)S(1)} %fusion), channel_id=1, source_target_pairs={{0,4},{1,5},{2,6},{3,7},{4,0},{5,1},{6,2},{7,3},{8,12},{9,13},{10,... | collective-permute-start | bytes 98312 | tf_op jit(solution)/shard_map/ppermute | solution.py:666
  109.0 4.3 %collective-permute-start.11 = (f32[64,128]{1,0:T(8,128)S(1)}, f32[64,128]{1,0:T(8,128)S(1)}, u32[]{:S(2)}, u32[]{:S(2)}) collective-permute-start(f32[64,128]{1,0:T(8,128)S(1)} %fusion), channel_id=1, source_target_pairs={{0,2},{1,3},{2,4},{3,5},{4,6},{5,7},{6,0},{7,1},{8,10},{9,11},{10,... | collective-permute-start | bytes 98312 | tf_op jit(solution)/shard_map/ppermute | solution.py:666
  125.1 5.0 %collective-permute-start.14 = (f32[64,128]{1,0:T(8,128)S(1)}, f32[64,128]{1,0:T(8,128)S(1)}, u32[]{:S(2)}, u32[]{:S(2)}) collective-permute-start(f32[64,128]{1,0:T(8,128)S(1)} %reduce_sum.9), channel_id=1, source_target_pairs={{0,1},{1,0},{2,3},{3,2},{4,5},{5,4},{6,7},{7,6},{8,9},{9,8},{10,11... | collective-permute-start | bytes 98312 | tf_op jit(solution)/shard_map/ppermute | solution.py:674
  130.2 3.7 %collective-permute-start.17 = (f32[2,64,128]{2,1,0:T(8,128)S(1)}, f32[2,64,128]{2,1,0:T(8,128)S(1)}, u32[]{:S(2)}, u32[]{:S(2)}) collective-permute-start(f32[2,64,128]{2,1,0:T(8,128)S(1)} %pad_maximum_fusion.both_ref), channel_id=1, source_target_pairs={{0,24},{8,0},{16,8},{24,16},{32,56},{40,32},{48,40},{56,48},{64,88... | collective-permute-start | bytes 196616 | tf_op jit(solution)/shard_map/ppermute | solution.py:666
  131.9 4.7 %collective-permute-start.16 = (f32[2,64,128]{2,1,0:T(8,128)S(1)}, f32[2,64,128]{2,1,0:T(8,128)S(1)}, u32[]{:S(2)}, u32[]{:S(2)}) collective-permute-start(f32[2,64,128]{2,1,0:T(8,128)S(1)} %pad_maximum_fusion.both_ref), channel_id=1, source_target_pairs={{0,16},{8,24},{16,0},{24,8},{32,48},{40,56},{48,32},{56,40},{64,80... | collective-permute-start | bytes 196616 | tf_op jit(solution)/shard_map/ppermute | solution.py:666
  132.1 5.9 %collective-permute-start.15 = (f32[2,64,128]{2,1,0:T(8,128)S(1)}, f32[2,64,128]{2,1,0:T(8,128)S(1)}, u32[]{:S(2)}, u32[]{:S(2)}) collective-permute-start(f32[2,64,128]{2,1,0:T(8,128)S(1)} %pad_maximum_fusion.both_ref), channel_id=1, source_target_pairs={{0,8},{8,16},{16,24},{24,0},{32,40},{40,48},{48,56},{56,32},{64,72... | collective-permute-start | bytes 196616 | tf_op jit(solution)/shard_map/ppermute | solution.py:666

commit v3 on v2

--- a/solution.py
+++ b/solution.py
@@ -205,14 +205,15 @@
     return both + jnp.where(row == H, later[H : H + 1], 0.0)
 
 
-def compose_chunks(maps_ref):
+def chunk_levels(maps_ref):
     pad = jnp.zeros((7, LANES), F32)
-    parts = [
+    levels = [[
         jnp.concatenate([chunk_matrix(maps_ref, c), chunk_vector(maps_ref, c), pad], axis=0) for c in range(CHUNKS)
-    ]
-    while len(parts) > 1:
-        parts = [compose(a, b) for a, b in zip(parts[::2], parts[1::2])]
-    return parts[0]
+    ]]
+    while len(levels[-1]) > 1:
+        parts = levels[-1]
+        levels.append([compose(a, b) for a, b in zip(parts[::2], parts[1::2])])
+    return levels
 
 
 def flip_halves(matrix):
@@ -318,28 +319,28 @@
     return mm(jnp.concatenate([high, low, rest], axis=1), jnp.concatenate([one, one, one], axis=0))
 
 
-def store_chunks(maps_ref, chunk_ref, flipped):
-    for c in range(CHUNKS):
-        matrix = chunk_matrix(maps_ref, c)
-        chunk_ref[c] = flip_halves(matrix) if c % 2 == flipped else matrix
-
-
-def enter_chunks(state, maps_ref, chunk_ref, ends_ref):
+def store_chunks(levels, chunk_ref, vector_ref):
+    ones, twos, fours, _ = levels
+    parts = (ones[0], twos[0], fours[0], ones[6], ones[2], ones[4], twos[2])
+    for n, part in enumerate(parts):
+        chunk_ref[n] = flip_halves(part[:H]) if n < 4 else part[:H]
+        vector_ref[n : n + 1, :] = part[H : H + 1]
+
+
+def enter_chunks(state, chunk_ref, vector_ref, ends_ref):
     low = lane_low((CHUNKS, LANES))
     first = doubled(ends_ref[...], 0)
     middle = apply_row(state, first[:H], first[H : H + 1])
     entering = jnp.where(low, state, middle)
-    row = lax.broadcasted_iota(jnp.int32, (CHUNKS, LANES), 0)
-    value = entering[0:1]
-    for c in range(CHUNKS - 1):
-        vector = chunk_vector(maps_ref, c)
-        if c % 2 == 0:
-            column = to_column(value, chunk_ref[c], vector)
-            value = as_row(column)
-        else:
-            value = to_row(column, chunk_ref[c], vector)
-        entering = jnp.where(row == c + 1, value, entering)
-    return entering
+    vectors = vector_ref[...]
+    row = entering[0:1]
+    one, two, four = (to_column(row, chunk_ref[n], vectors[n : n + 1]) for n in range(3))
+    three = to_row(two, chunk_ref[4], vectors[4:5])
+    five = to_row(four, chunk_ref[5], vectors[5:6])
+    six = to_row(four, chunk_ref[6], vectors[6:7])
+    seven = to_column(six, chunk_ref[3], vectors[3:4])
+    rows = [row, as_row(one), as_row(two), three, as_row(four), five, six, as_row(seven)]
+    return jnp.concatenate(rows, axis=0)
 
 
 def trajectory(entering, maps_ref, spread_ref):
@@ -353,11 +354,12 @@
     return states
 
 
-def phase(where_ref, prev, x3_ref, bias_ref, w3_ref, ws_ref, ud_ref, maps_ref, chunk_ref, ends_ref, out_ref):
+def phase(where_ref, prev, x3_ref, bias_ref, w3_ref, ws_ref, ud_ref, maps_ref, chunk_ref, vector_ref, ends_ref, out_ref):
     coef = coefficients(prev, x3_ref, bias_ref[...], w3_ref[...])
     scan_maps(coef, ws_ref, ud_ref, maps_ref)
-    total = compose_chunks(maps_ref)
-    store_chunks(maps_ref, chunk_ref, 0)
+    levels = chunk_levels(maps_ref)
+    store_chunks(levels, chunk_ref, vector_ref)
+    total = levels[-1][0]
     ends_ref[...] = total
     total = join_halves(total)
     send_map(total, flip(total[:H]), where_ref, out_ref)
@@ -365,7 +367,7 @@
 
 def first_kernel(
     where_ref, a_ref, b_ref, w_ref, w3_ref, ws_ref, ud_ref, bias_ref,
-    x3_ref, xin_ref, cot_ref, start_ref, maps_ref, chunk_ref, ends_ref, out_ref, natural_ref,
+    x3_ref, xin_ref, cot_ref, start_ref, maps_ref, chunk_ref, vector_ref, ends_ref, out_ref, natural_ref,
 ):
     odd, mine = where_ref[0], where_ref[2]
     pieces = []
@@ -394,18 +396,18 @@
     lane = lax.broadcasted_iota(jnp.int32, (64, LANES), 1)
     here = (row == 0) & (lane < H) & (mine == 0)
     prev = jnp.where(here, start[0:1, :], 0.0)
-    phase(where_ref, prev, x3_ref, bias_ref, w3_ref, ws_ref, ud_ref, maps_ref, chunk_ref, ends_ref, out_ref)
+    phase(where_ref, prev, x3_ref, bias_ref, w3_ref, ws_ref, ud_ref, maps_ref, chunk_ref, vector_ref, ends_ref, out_ref)
 
 
 def next_kernel(
-    where_ref, own_ref, other_ref, start_ref, x3_ref, bias_ref, w3_ref, ws_ref, ud_ref, old_ref, pieces_ref, before_ref,
-    maps_ref, chunk_ref, ends_ref, out_ref, spread_ref,
+    where_ref, own_ref, other_ref, start_ref, x3_ref, bias_ref, w3_ref, ws_ref, ud_ref, old_ref, pieces_ref, rows_ref, before_ref,
+    maps_ref, chunk_ref, vector_ref, ends_ref, out_ref, spread_ref,
 ):
     state = enter_device(where_ref, own_ref, other_ref, start_ref[...], False)
-    entering = enter_chunks(state, old_ref, pieces_ref, before_ref)
+    entering = enter_chunks(state, pieces_ref, rows_ref, before_ref)
     states = trajectory(entering, old_ref, spread_ref)
     prev = jnp.concatenate([entering] + states[:-1], axis=0)
-    phase(where_ref, prev, x3_ref, bias_ref, w3_ref, ws_ref, ud_ref, maps_ref, chunk_ref, ends_ref, out_ref)
+    phase(where_ref, prev, x3_ref, bias_ref, w3_ref, ws_ref, ud_ref, maps_ref, chunk_ref, vector_ref, ends_ref, out_ref)
 
 
 def half_sums(value):
@@ -417,12 +419,12 @@
 
 
 def turn_kernel(
-    where_ref, own_ref, other_ref, start_ref, x3_ref, bias_ref, w3_ref, ws_ref, ud_ref, old_ref, pieces_ref, before_ref, cot_ref,
+    where_ref, own_ref, other_ref, start_ref, x3_ref, bias_ref, w3_ref, ws_ref, ud_ref, old_ref, pieces_ref, rows_ref, before_ref, cot_ref,
     states_ref, coef_ref, chunk_ref, vector_ref, half_ref, out_ref,
     spread_ref, maps_ref, acc_ref,
 ):
     state = enter_device(where_ref, own_ref, other_ref, start_ref[...], False)
-    entering = enter_chunks(state, old_ref, pieces_ref, before_ref)
+    entering = enter_chunks(state, pieces_ref, rows_ref, before_ref)
     states = trajectory(entering, old_ref, spread_ref)
     for j in range(STEPS):
         states_ref[pl.ds(j, CHUNKS, stride=STEPS), :] = states[j]
@@ -432,8 +434,8 @@
     for n in range(5):
         coef_ref[n + 1] = coef[n]
     scan_maps(coef, ws_ref, ud_ref, maps_ref)
-    total = compose_chunks(maps_ref)
-    store_chunks(maps_ref, chunk_ref, 0)
+    levels = chunk_levels(maps_ref)
+    total = levels[-1][0]
     for b in range(0, H * CHUNKS, 64):
         acc = jnp.zeros((8, CHUNKS, LANES), F32)
         for j in range(STEPS):
@@ -444,13 +446,18 @@
     for c in range(CHUNKS):
         sums = half_sums(acc_ref[pl.ds(c, H, stride=CHUNKS), :])
         vectors.append(jnp.concatenate([sums[0:1], sums[1:2]], axis=1))
-    vector_ref[...] = jnp.concatenate(vectors, axis=0)
-    ends = jnp.zeros((1, LANES), F32)
-    for c in reversed(range(CHUNKS)):
-        if c % 2 == 1:
-            column = to_column(ends, chunk_ref[c], vectors[c])
-        else:
-            ends = to_row(column, chunk_ref[c], vectors[c])
+    ones, twos, fours, _ = [[part[:H] for part in level] for level in levels]
+    flip_23 = flip_halves(twos[1])
+    pairs = [to_column(vectors[2 * n + 1], ones[2 * n], vectors[2 * n]) for n in range(4)]
+    pair_rows = [as_row(pair) for pair in pairs]
+    quad_low = to_row(pairs[1], flip_halves(twos[0]), pair_rows[0])
+    quad_high = to_row(pairs[3], flip_halves(twos[2]), pair_rows[2])
+    ends = as_row(to_column(quad_high, fours[0], quad_low))
+    matrices = (fours[1], twos[3], ones[7], flip_23, flip_halves(ones[5]), flip_halves(ones[3]), ones[1])
+    rows = (quad_high, pair_rows[3], vectors[7], pair_rows[1], vectors[5], vectors[3], vectors[1])
+    for n, (matrix, vector) in enumerate(zip(matrices, rows)):
+        chunk_ref[n] = matrix
+        vector_ref[n : n + 1, :] = vector
     tail = doubled(ends, 1)
     low = lane_low((H, LANES))
     sums = half_sums(jnp.where(low, total[:H], 0.0) * tail)
@@ -467,20 +474,19 @@
     xin_ref, bias_ref, states_ref, across_ref, keep_ref, give_ref, home_ref, full_ref,
 ):
     low = lane_low((CHUNKS, LANES))
-    row = lax.broadcasted_iota(jnp.int32, (CHUNKS, LANES), 0)
     right = enter_device(where_ref, own_ref, other_ref, jnp.zeros((CHUNKS, LANES), F32), True)
     half = half_ref[...]
     middle = apply_row(right, half[:H], half[H : H + 1])
-    passed = jnp.where(low, middle, right)
-    value = passed[0:1]
-    for c in reversed(range(1, CHUNKS)):
-        vector = vector_ref[c : c + 1, :]
-        if c % 2 == 1:
-            column = to_column(value, chunk_ref[c], vector)
-            value = as_row(column)
-        else:
-            value = to_row(column, chunk_ref[c], vector)
-        passed = jnp.where(row < c, value, passed)
+    last = jnp.where(low, middle, right)[0:1]
+    vectors = vector_ref[...]
+    three, five, six = (to_column(last, chunk_ref[n], vectors[n : n + 1]) for n in range(3))
+    one = to_row(three, chunk_ref[3], vectors[3:4])
+    four = to_row(five, chunk_ref[4], vectors[4:5])
+    two = to_row(three, chunk_ref[5], vectors[5:6])
+    zero = to_column(one, chunk_ref[6], vectors[6:7])
+    passed = jnp.concatenate(
+        [as_row(zero), one, two, as_row(three), four, as_row(five), as_row(six), last], axis=0
+    )
     dz, dr, dn, ds = [None] * STEPS, [None] * STEPS, [None] * STEPS, [None] * STEPS
     for j in reversed(range(STEPS)):
         at = slice(j * CHUNKS, (j + 1) * CHUNKS)
@@ -532,7 +538,7 @@
         home_ref[d] = jnp.where(lane_low((32, LANES)), block[:32], swap_halves(block[32:]))
 
 
-def home_kernel(where_ref, home_ref, one_ref, two_ref, three_ref, traj_ref):
+def home_kernel(where_ref, home_ref, two_ref, one_ref, three_ref, traj_ref):
     core, x = where_ref[1], where_ref[3]
     blocks = [home_ref[0]] + [ref[64:96, :] for ref in (one_ref, two_ref, three_ref)]
     for e in range(2):
@@ -545,7 +551,7 @@
 
 
 def unpack_kernel(
-    where_ref, one_ref, two_ref, three_ref, both_ref, in_ref, rec_ref, scale_ref, bias_ref, full_ref
+    where_ref, three_ref, one_ref, two_ref, both_ref, in_ref, rec_ref, scale_ref, bias_ref, full_ref
 ):
     x = where_ref[3]
     pieces = (both_ref, one_ref, two_ref, three_ref)
@@ -595,12 +601,12 @@
             for z in range(planes) for x in range(width) for y in range(ys) for c in range(2)
         ]
         there.append(pairs)
-    step_x = [
-        [(z * width + x, z * width + (x + d) % width) for z in range(planes) for x in range(width)]
+    step_x = {
+        d: [(z * width + x, z * width + (x + d) % width) for z in range(planes) for x in range(width)]
         for d in range(1, width)
-    ]
+    }
     along_z = [[z * width + x for z in range(planes)] for x in range(width)]
-    step_y = [[(b, (b + 2 * d) % (2 * ys)) for b in range(2 * ys)] for d in range(1, ys)]
+    step_y = {d: [(b, (b + 2 * d) % (2 * ys)) for b in range(2 * ys)] for d in range(1, ys)}
     cores = [(b, b ^ 1) for b in range(2 * ys)]
     axes = ("seq", "batch")
 
@@ -627,19 +633,19 @@
         scratch=[pltpu.VMEM((H, 192), F32), pltpu.VMEM((1, H), F32), pltpu.VMEM((3, H), F32), sems],
     )
     maps_t, chunk_t = ((STEPS, ROWS, LANES), F32), ((CHUNKS, H, LANES), F32)
-    ends_t, send_t = ((72, LANES), F32), ((planes, MAP, LANES), F32)
-    x3, xin, cot, start, maps, chunk, ends, send = call(
+    rows_t, ends_t, send_t = ((8, LANES), F32), ((72, LANES), F32), ((planes, MAP, LANES), F32)
+    x3, xin, cot, start, maps, chunk, vector, ends, send = call(
         first_kernel,
-        [((3, 64, LANES), F32), ((128, 256), BF16), ((64, LANES), F32), ((8, LANES), F32), maps_t, chunk_t, ends_t, send_t],
+        [((3, 64, LANES), F32), ((128, 256), BF16), ((64, LANES), F32), ((8, LANES), F32), maps_t, chunk_t, rows_t, ends_t, send_t],
         "svvvvvvv", where, one, two, w, w3, ws, ud, bias,
         scratch=[pltpu.VMEM((64, LANES), F32)],
     )
     spread_s = pltpu.VMEM((H * CHUNKS, LANES), F32)
     for _ in range(NEWTON - 1):
         own, other = exchange(send)
-        maps, chunk, ends, send = call(
-            next_kernel, [maps_t, chunk_t, ends_t, send_t], "svvvvvvvvvvv",
-            where, own, other, start, x3, bias, w3, ws, ud, maps, chunk, ends, scratch=[spread_s],
+        maps, chunk, vector, ends, send = call(
+            next_kernel, [maps_t, chunk_t, rows_t, ends_t, send_t], "svvvvvvvvvvvv",
+            where, own, other, start, x3, bias, w3, ws, ud, maps, chunk, vector, ends, scratch=[spread_s],
         )
     own, other = exchange(send)
     states, coef, chunk, vector, half, send = call(
@@ -648,7 +654,7 @@
             ((64, LANES), F32), ((6, 64, LANES), F32), chunk_t,
             ((8, LANES), F32), ((72, LANES), F32), send_t,
         ],
-        "svvvvvvvvvvvv", where, own, other, start, x3, bias, w3, ws, ud, maps, chunk, ends, cot,
+        "svvvvvvvvvvvvv", where, own, other, start, x3, bias, w3, ws, ud, maps, chunk, vector, ends, cot,
         scratch=[
             spread_s, pltpu.VMEM(*maps_t),
             pltpu.VMEM((H * CHUNKS, LANES), F32),
@@ -662,19 +668,20 @@
         scratch=[pltpu.VMEM((512, LANES), F32)],
     )
 
-    def around(values, axis, pairs):
-        return [lax.ppermute(value, axis, pair) for value, pair in zip(values, pairs)]
+    def around(value_of, axis, steps, order):
+        got = {d: lax.ppermute(value_of(d), axis, steps[d]) for d in order}
+        return [got[d] for d in order]
 
     parts = (keep + lax.ppermute(give, "batch", cores)).reshape(width, -1, LANES)
-    early = around([jnp.concatenate([parts[d], home[d]], axis=0) for d in range(1, width)], "seq", step_x)
+    early = around(lambda d: jnp.concatenate([parts[d], home[d]], axis=0), "seq", step_x, (2, 1, 3))
     part = parts[0] + sum(piece[:64] for piece in early)
-    part = part + sum(around([part] * (ys - 1), "batch", step_y))
+    part = part + sum(around(lambda d: part, "batch", step_y, (3, 1, 2)))
     wide = jnp.broadcast_to(part[None], (planes,) + part.shape)
     part = lax.all_to_all(wide, "seq", 0, 0, axis_index_groups=along_z, tiled=True).sum(0)
     other = lax.ppermute(part, "batch", cores)
     first = core == 0
     both = jnp.stack([jnp.where(first, part, other), jnp.where(first, other, part)])
-    rest = around([both] * (width - 1), "seq", step_x)
+    rest = around(lambda d: both, "seq", step_x, (3, 1, 2))
     (traj,) = call(home_kernel, [((H, 2, 64), F32)], "svvvv", where, home, *early)
     grad_in, grad_rec, grad_scale, grad_other = call(
         unpack_kernel,

time: 140 us -> 137 us (0.979)
  waiting for transfers between devices: 20.5 us -> 14.7 us
  starting transfers between devices: 24.8 us -> 28.7 us
    ppermute x9, waiting for transfers between devices: 10.5 us -> 4.79 us  [around(): got = {d: lax.ppermute(value_of(d), axis, steps[d]) for d in order}]
    ppermute x9, starting transfers between devices: 9.89 us -> 13.8 us  [around(): got = {d: lax.ppermute(value_of(d), axis, steps[d]) for d in order}]
  transfers between devices with their start and end apart: 18 -> 18, of which waited for: 15 -> 13; matrix products, arithmetic and copies ran while one was open for 0% -> 0% of each run, Pallas kernels for 2% -> 2%
where the time goes in v3:
time: 137 us; the launch traced here: 136 us
  blocking collectives  63.7 us (46%)
  starting transfers between devices  28.7 us (21%)
  Pallas kernels  28.2 us (21%)
  waiting for transfers between devices  14.7 us (11%)
    all_to_all x4, blocking collectives, exchange(): lax.all_to_all(value, 'seq', 0, 0, axis_index_groups=along_z, tiled=True)  51.9 us
    pallas_call x9, Pallas kernels, call(): pl.pallas_call(kernel, out_shape=[jax.ShapeDtypeStruct(*out) for out in o...  28.2 us
    ppermute x9, starting transfers between devices, around(): got = {d: lax.ppermute(value_of(d), axis, steps[d]) for d in order}  13.8 us
    all_to_all x1, blocking collectives, local(): lax.all_to_all(wide, 'seq', 0, 0, axis_index_groups=along_z, tiled=True)  11.8 us
    ppermute x1, starting transfers between devices, local(): one = lax.ppermute(one, axes, there[0])  6.04 us
    ppermute x9, waiting for transfers between devices, around(): got = {d: lax.ppermute(value_of(d), axis, steps[d]) for d in order}  4.79 us
    ppermute x1, starting transfers between devices, local(): other = lax.ppermute(part, 'batch', cores)  4.17 us
    ppermute x4, starting transfers between devices, exchange(): return (own, lax.ppermute(own, 'batch', cores))  3.74 us
  transfers between devices with their start and end apart: 18, of which 13 were waited for; matrix products, arithmetic and copies ran while one was open for 0% of the time, Pallas kernels for 2%

profile of v3, /device:TPU:1, one launch (start us, length us, event | category | flops | bytes accessed | tf_op | source)
XLA Modules:
  0.0 136.3 jit_solution(3167812470506588704)
XLA Ops:
  0.7 0.1 pad_add_fusion.where_ref
  0.8 1.6 %shard_map.110 = (f32[168,128]{1,0:T(8,128)S(1)}, f32[168,128]{1,0:T(8,128)S(1)}) custom-call(s32[4]{0:T(128)S(1)} %pad_add_fusion.where_ref, bf16[2,64,256]{2,1,0:T(8,128)(2,1)} %x_hbm.1, f32[64,2,64]{2,1,0:T(2,128)} %cot_hbm.1, f32[2,64]{1,0:T(2,128)} %bitcast.20), custom_call_target="tpu_custom_call" | custom-call | tf_op jit(solution)/shard_map/pallas_call | solution.py:579
  2.4 6.0 %collective-permute-start = (f32[168,128]{1,0:T(8,128)S(1)}, f32[168,128]{1,0:T(8,128)S(1)}, u32[]{:S(2)}, u32[]{:S(2)}) collective-permute-start(f32[168,128]{1,0:T(8,128)S(1)} %get-tuple-element.46), channel_id=1, source_target_pairs={{0,0},{1,16},{2,2},{3,18},{4,4},{5,20},{6,6},{7,22},{8,8},{9,24},{... | collective-permute-start | bytes 258056 | tf_op jit(solution)/shard_map/ppermute | solution.py:624
  8.4 0.7 collective-permute-start.1
  9.1 1.2 shard_map.111
  10.3 0.3 collective-permute-done.a_ref
  10.6 3.1 %collective-permute-done.1.b_ref = f32[168,128]{1,0:T(8,128)S(1)} collective-permute-done((f32[168,128]{1,0:T(8,128)S(1)}, f32[168,128]{1,0:T(8,128)S(1)}, u32[]{:S(2)}, u32[]{:S(2)}) %collective-permute-start.1) | collective-permute-done | bytes 86048 | tf_op jit(solution)/shard_map/ppermute | solution.py:625
  13.6 3.7 %shard_map.112 = (f32[3,64,128]{2,1,0:T(8,128)S(1)}, bf16[128,256]{1,0:T(8,128)(2,1)S(1)}, f32[64,128]{1,0:T(8,128)S(1)}, f32[8,128]{1,0:T(8,128)S(1)}, f32[8,52...) custom-call(s32[4]{0:T(128)S(1)} %pad_add_fusion.where_ref, ...), custom_call_target="tpu_custom_call" | custom-call | tf_op jit(solution)/shard_map/pallas_call | solution.py:579
  17.3 16.3 %all_to_all.25.own_ref = f32[8,40,128]{2,1,0:T(8,128)S(1)} all-to-all(f32[8,40,128]{2,1,0:T(8,128)S(1)} %get-tuple-element.53), channel_id=1, replica_groups={{0,32,64,96,128,160,192,224},{8,40,72,104,136,168,200,232},{16,48,80,11..., dimensions={0} | all-to-all | bytes 327680 | tf_op jit(solution)/shard_map/all_to_all | solution.py:614
  33.6 0.0 collective-permute-start.2
  33.6 1.4 %collective-permute-done.2.other_ref = f32[8,40,128]{2,1,0:T(8,128)S(1)} collective-permute-done((f32[8,40,128]{2,1,0:T(8,128)S(1)}, f32[8,40,128]{2,1,0:T(8,128)S(1)}, u32[]{:S(2)}, u32[]{:S(2)}) %collective-permute-start.2) | collective-permute-done | bytes 163872 | tf_op jit(solution)/shard_map/ppermute | solution.py:615
  35.0 5.1 %shard_map.113 = (f32[8,520,128]{2,1,0:T(8,128)S(1)}, f32[8,64,128]{2,1,0:T(8,128)S(1)}, f32[8,128]{1,0:T(8,128)S(1)}, f32[72,128]{1,0:T(8,128)S(1)}, f32[8,40,128]{2,1,0:T(8,128)S(1)}) custom-call(s32[4]{0:T(128)S(1)} %pad_add_fusion.where_ref, f32[8,40,128]{2,1,0:T(8,128)S(1)} %all_to_all.25.own_ref, f32[8,40,128]{2,1,0:T(8,128)S(1)} %collective-permute-done.2.other_ref, ...), custom_call_target="tpu_custom_call" | custom-call | tf_op jit(solution)/shard_map/pallas_call | solution.py:579
  40.1 12.5 %all_to_all.26.own_ref = f32[8,40,128]{2,1,0:T(8,128)S(1)} all-to-all(f32[8,40,128]{2,1,0:T(8,128)S(1)} %get-tuple-element.60), channel_id=1, replica_groups={{0,32,64,96,128,160,192,224},{8,40,72,104,136,168,200,232},{16,48,80,11..., dimensions={0} | all-to-all | bytes 327680 | tf_op jit(solution)/shard_map/all_to_all | solution.py:614
  52.7 0.6 collective-permute-start.3
  53.2 1.0 collective-permute-done.3.other_ref
  54.3 5.1 %shard_map.114 = (f32[8,520,128]{2,1,0:T(8,128)S(1)}, f32[8,64,128]{2,1,0:T(8,128)S(1)}, f32[8,128]{1,0:T(8,128)S(1)}, f32[72,128]{1,0:T(8,128)S(1)}, f32[8,40,128]{2,1,0:T(8,128)S(1)}) custom-call(s32[4]{0:T(128)S(1)} %pad_add_fusion.where_ref, f32[8,40,128]{2,1,0:T(8,128)S(1)} %all_to_all.26.own_ref, f32[8,40,128]{2,1,0:T(8,128)S(1)} %collective-permute-done.3.other_ref, ...), custom_call_target="tpu_custom_call" | custom-call | tf_op jit(solution)/shard_map/pallas_call | solution.py:579
  59.4 11.5 %all_to_all.27.own_ref = f32[8,40,128]{2,1,0:T(8,128)S(1)} all-to-all(f32[8,40,128]{2,1,0:T(8,128)S(1)} %get-tuple-element.65), channel_id=1, replica_groups={{0,32,64,96,128,160,192,224},{8,40,72,104,136,168,200,232},{16,48,80,11..., dimensions={0} | all-to-all | bytes 327680 | tf_op jit(solution)/shard_map/all_to_all | solution.py:614
  70.9 1.6 %collective-permute-start.4 = (f32[8,40,128]{2,1,0:T(8,128)S(1)}, f32[8,40,128]{2,1,0:T(8,128)S(1)}, u32[]{:S(2)}, u32[]{:S(2)}) collective-permute-start(f32[8,40,128]{2,1,0:T(8,128)S(1)} %all_to_all.27.own_ref), channel_id=1, source_target_pairs={{0,1},{1,0},{2,3},{3,2},{4,5},{5,4},{6,7},{7,6},{8,9},{9,8},{10,11... | collective-permute-start | bytes 491528 | tf_op jit(solution)/shard_map/ppermute | solution.py:615
  72.5 1.0 collective-permute-done.4.other_ref
  73.5 5.7 %shard_map.115 = (f32[64,128]{1,0:T(8,128)S(1)}, f32[6,64,128]{2,1,0:T(8,128)S(1)}, f32[8,64,128]{2,1,0:T(8,128)S(1)}, f32[8,128]{1,0:T(8,128)S(1)}, f32[72,128]{1,0:T(8,128)S(1)}, /*index=5*/f32[8,40,128]{2,1,0:T(8,128)S(1)}) custom-call(s32[4]{0:T(128)S(1)} %pad_add_fusion.where_ref, f32[8,40,128]{2,1,0:T(8,128)S(1)} %all_to_all.27.own_ref, ...), custom_call_target="tpu_custom_call" | custom-call | tf_op jit(solution)/shard_map/pallas_call | solution.py:579
  79.2 11.5 %all_to_all.28.own_ref = f32[8,40,128]{2,1,0:T(8,128)S(1)} all-to-all(f32[8,40,128]{2,1,0:T(8,128)S(1)} %get-tuple-element.71), channel_id=1, replica_groups={{0,32,64,96,128,160,192,224},{8,40,72,104,136,168,200,232},{16,48,80,11..., dimensions={0} | all-to-all | bytes 327680 | tf_op jit(solution)/shard_map/all_to_all | solution.py:614
  90.7 1.6 %collective-permute-start.5 = (f32[8,40,128]{2,1,0:T(8,128)S(1)}, f32[8,40,128]{2,1,0:T(8,128)S(1)}, u32[]{:S(2)}, u32[]{:S(2)}) collective-permute-start(f32[8,40,128]{2,1,0:T(8,128)S(1)} %all_to_all.28.own_ref), channel_id=1, source_target_pairs={{0,1},{1,0},{2,3},{3,2},{4,5},{5,4},{6,7},{7,6},{8,9},{9,8},{10,11... | collective-permute-start | bytes 491528 | tf_op jit(solution)/shard_map/ppermute | solution.py:615
  92.3 0.0 collective-permute-start.6
  92.3 1.2 collective-permute-done.6.across_ref
  93.5 0.0 collective-permute-done.5.other_ref
  93.5 3.1 %shard_map.116 = (f32[256,128]{1,0:T(8,128)S(1)}, f32[256,128]{1,0:T(8,128)S(1)}, f32[4,32,128]{2,1,0:T(8,128)S(1)}) custom-call(s32[4]{0:T(128)S(1)} %pad_add_fusion.where_ref, f32[8,40,128]{2,1,0:T(8,128)S(1)} %all_to_all.28.own_ref, f32[8,40,128]{2,1,0:T(8,128)S(1)} %collective-permute-done.5.other_ref, f32[6,64,128]{2,1,0:T(8,128)S(1)} %get-tuple-element.72.coef_ref, ...), custom_call_target="tpu_custom_call" | custom-call | tf_op jit(solution)/shard_map/pallas_call | solution.py:579
  96.7 0.3 collective-permute-start.7
  97.0 1.1 collective-permute-done.7
  98.1 1.6 %collective-permute-start.8 = (f32[96,128]{1,0:T(8,128)S(1)}, f32[96,128]{1,0:T(8,128)S(1)}, u32[]{:S(2)}, u32[]{:S(2)}) collective-permute-start(f32[96,128]{1,0:T(8,128)S(1)} %pad_maximum_fusion.1), channel_id=1, source_target_pairs={{0,16},{8,24},{16,0},{24,8},{32,48},{40,56},{48,32},{56,40},{64,80... | collective-permute-start | bytes 147464 | tf_op jit(solution)/shard_map/ppermute | solution.py:672
  99.8 1.1 collective-permute-start.9
  100.8 1.6 %collective-permute-start.10 = (f32[96,128]{1,0:T(8,128)S(1)}, f32[96,128]{1,0:T(8,128)S(1)}, u32[]{:S(2)}, u32[]{:S(2)}) collective-permute-start(f32[96,128]{1,0:T(8,128)S(1)} %pad_maximum_fusion.3), channel_id=1, source_target_pairs={{0,24},{8,0},{16,8},{24,16},{32,56},{40,32},{48,40},{56,48},{64,88... | collective-permute-start | bytes 147464 | tf_op jit(solution)/shard_map/ppermute | solution.py:672
  102.5 0.2 collective-permute-done.8.two_ref
  102.7 1.5 %collective-permute-done.9.one_ref = f32[96,128]{1,0:T(8,128)S(1)} collective-permute-done((f32[96,128]{1,0:T(8,128)S(1)}, f32[96,128]{1,0:T(8,128)S(1)}, u32[]{:S(2)}, u32[]{:S(2)}) %collective-permute-start.9) | collective-permute-done | bytes 49184 | tf_op jit(solution)/shard_map/ppermute | solution.py:672
  104.2 0.0 collective-permute-done.10.three_ref
  104.2 3.0 %collective-permute-start.13 = (f32[64,128]{1,0:T(8,128)S(1)}, f32[64,128]{1,0:T(8,128)S(1)}, u32[]{:S(2)}, u32[]{:S(2)}) collective-permute-start(f32[64,128]{1,0:T(8,128)S(1)} %fusion), channel_id=1, source_target_pairs={{0,4},{1,5},{2,6},{3,7},{4,0},{5,1},{6,2},{7,3},{8,12},{9,13},{10,... | collective-permute-start | bytes 98312 | tf_op jit(solution)/shard_map/ppermute | solution.py:672
  107.2 0.4 collective-permute-start.12
  107.6 2.3 %collective-permute-start.11 = (f32[64,128]{1,0:T(8,128)S(1)}, f32[64,128]{1,0:T(8,128)S(1)}, u32[]{:S(2)}, u32[]{:S(2)}) collective-permute-start(f32[64,128]{1,0:T(8,128)S(1)} %fusion), channel_id=1, source_target_pairs={{0,6},{1,7},{2,0},{3,1},{4,2},{5,3},{6,4},{7,5},{8,14},{9,15},{10,... | collective-permute-start | bytes 98312 | tf_op jit(solution)/shard_map/ppermute | solution.py:672
  109.8 0.0 collective-permute-done.13
  109.9 1.3 collective-permute-done.12
  111.1 0.0 collective-permute-done.11
  111.2 11.8 %all_to_all.29 = f32[8,64,128]{2,1,0:T(8,128)S(1)} all-to-all(f32[8,64,128]{2,1,0:T(8,128)S(1)} %broadcast_in_dim.10), channel_id=1, replica_groups={{0,32,64,96,128,160,192,224},{8,40,72,104,136,168,200,232},{16,48,80,11..., dimensions={0} | all-to-all | bytes 524288 | tf_op jit(solution)/shard_map/all_to_all | solution.py:680
  123.0 4.2 %collective-permute-start.14 = (f32[64,128]{1,0:T(8,128)S(1)}, f32[64,128]{1,0:T(8,128)S(1)}, u32[]{:S(2)}, u32[]{:S(2)}) collective-permute-start(f32[64,128]{1,0:T(8,128)S(1)} %reduce_sum.9), channel_id=1, source_target_pairs={{0,1},{1,0},{2,3},{3,2},{4,5},{5,4},{6,7},{7,6},{8,9},{9,8},{10,11... | collective-permute-start | bytes 98312 | tf_op jit(solution)/shard_map/ppermute | solution.py:681
  127.2 0.9 collective-permute-done.14
  128.1 1.1 collective-permute-start.17
  129.2 2.3 %collective-permute-start.16 = (f32[2,64,128]{2,1,0:T(8,128)S(1)}, f32[2,64,128]{2,1,0:T(8,128)S(1)}, u32[]{:S(2)}, u32[]{:S(2)}) collective-permute-start(f32[2,64,128]{2,1,0:T(8,128)S(1)} %pad_maximum_fusion.both_ref), channel_id=1, source_target_pairs={{0,8},{8,16},{16,24},{24,0},{32,40},{40,48},{48,56},{56,32},{64,72... | collective-permute-start | bytes 196616 | tf_op jit(solution)/shard_map/ppermute | solution.py:672
  131.5 0.3 collective-permute-start.15
  131.9 1.3 shard_map.117
  133.2 0.0 collective-permute-done.17.two_ref
  133.2 1.6 %collective-permute-done.16.one_ref = f32[2,64,128]{2,1,0:T(8,128)S(1)} collective-permute-done((f32[2,64,128]{2,1,0:T(8,128)S(1)}, f32[2,64,128]{2,1,0:T(8,128)S(1)}, u32[]{:S(2)}, u32[]{:S(2)}) %collective-permute-start.16) | collective-permute-done | bytes 65568 | tf_op jit(solution)/shard_map/ppermute | solution.py:672
  134.8 0.2 collective-permute-done.15.three_ref
  135.0 1.3 shard_map.118
  (12 shorter events, 0.1 us)
Async XLA Ops:
  2.4 8.2 %collective-permute-start = (f32[168,128]{1,0:T(8,128)S(1)}, f32[168,128]{1,0:T(8,128)S(1)}, u32[]{:S(2)}, u32[]{:S(2)}) collective-permute-start(f32[168,128]{1,0:T(8,128)S(1)} %get-tuple-element.46), channel_id=1, source_target_pairs={{0,0},{1,16},{2,2},{3,18},{4,4},{5,20},{6,6},{7,22},{8,8},{9,24},{... | collective-permute-start | bytes 258056 | tf_op jit(solution)/shard_map/ppermute | solution.py:624
  8.4 5.2 %collective-permute-start.1 = (f32[168,128]{1,0:T(8,128)S(1)}, f32[168,128]{1,0:T(8,128)S(1)}, u32[]{:S(2)}, u32[]{:S(2)}) collective-permute-start(f32[168,128]{1,0:T(8,128)S(1)} %get-tuple-element.47), channel_id=1, source_target_pairs={{0,8},{1,24},{2,10},{3,26},{4,12},{5,28},{6,14},{7,30},{8,0},{9,16... | collective-permute-start | bytes 258056 | tf_op jit(solution)/shard_map/ppermute | solution.py:625
  33.6 1.4 %collective-permute-start.2 = (f32[8,40,128]{2,1,0:T(8,128)S(1)}, f32[8,40,128]{2,1,0:T(8,128)S(1)}, u32[]{:S(2)}, u32[]{:S(2)}) collective-permute-start(f32[8,40,128]{2,1,0:T(8,128)S(1)} %all_to_all.25.own_ref), channel_id=1, source_target_pairs={{0,1},{1,0},{2,3},{3,2},{4,5},{5,4},{6,7},{7,6},{8,9},{9,8},{10,11... | collective-permute-start | bytes 491528 | tf_op jit(solution)/shard_map/ppermute | solution.py:615
  52.7 1.6 %collective-permute-start.3 = (f32[8,40,128]{2,1,0:T(8,128)S(1)}, f32[8,40,128]{2,1,0:T(8,128)S(1)}, u32[]{:S(2)}, u32[]{:S(2)}) collective-permute-start(f32[8,40,128]{2,1,0:T(8,128)S(1)} %all_to_all.26.own_ref), channel_id=1, source_target_pairs={{0,1},{1,0},{2,3},{3,2},{4,5},{5,4},{6,7},{7,6},{8,9},{9,8},{10,11... | collective-permute-start | bytes 491528 | tf_op jit(solution)/shard_map/ppermute | solution.py:615
  70.9 2.6 %collective-permute-start.4 = (f32[8,40,128]{2,1,0:T(8,128)S(1)}, f32[8,40,128]{2,1,0:T(8,128)S(1)}, u32[]{:S(2)}, u32[]{:S(2)}) collective-permute-start(f32[8,40,128]{2,1,0:T(8,128)S(1)} %all_to_all.27.own_ref), channel_id=1, source_target_pairs={{0,1},{1,0},{2,3},{3,2},{4,5},{5,4},{6,7},{7,6},{8,9},{9,8},{10,11... | collective-permute-start | bytes 491528 | tf_op jit(solution)/shard_map/ppermute | solution.py:615
  90.7 2.8 %collective-permute-start.5 = (f32[8,40,128]{2,1,0:T(8,128)S(1)}, f32[8,40,128]{2,1,0:T(8,128)S(1)}, u32[]{:S(2)}, u32[]{:S(2)}) collective-permute-start(f32[8,40,128]{2,1,0:T(8,128)S(1)} %all_to_all.28.own_ref), channel_id=1, source_target_pairs={{0,1},{1,0},{2,3},{3,2},{4,5},{5,4},{6,7},{7,6},{8,9},{9,8},{10,11... | collective-permute-start | bytes 491528 | tf_op jit(solution)/shard_map/ppermute | solution.py:615
  92.3 1.2 collective-permute-start.6
  96.7 1.4 %collective-permute-start.7 = (f32[256,128]{1,0:T(8,128)S(1)}, f32[256,128]{1,0:T(8,128)S(1)}, u32[]{:S(2)}, u32[]{:S(2)}) collective-permute-start(f32[256,128]{1,0:T(8,128)S(1)} %get-tuple-element.82), channel_id=1, source_target_pairs={{0,1},{1,0},{2,3},{3,2},{4,5},{5,4},{6,7},{7,6},{8,9},{9,8},{10,11... | collective-permute-start | bytes 393224 | tf_op jit(solution)/shard_map/ppermute | solution.py:675
  98.1 4.5 %collective-permute-start.8 = (f32[96,128]{1,0:T(8,128)S(1)}, f32[96,128]{1,0:T(8,128)S(1)}, u32[]{:S(2)}, u32[]{:S(2)}) collective-permute-start(f32[96,128]{1,0:T(8,128)S(1)} %pad_maximum_fusion.1), channel_id=1, source_target_pairs={{0,16},{8,24},{16,0},{24,8},{32,48},{40,56},{48,32},{56,40},{64,80... | collective-permute-start | bytes 147464 | tf_op jit(solution)/shard_map/ppermute | solution.py:672
  99.8 4.4 %collective-permute-start.9 = (f32[96,128]{1,0:T(8,128)S(1)}, f32[96,128]{1,0:T(8,128)S(1)}, u32[]{:S(2)}, u32[]{:S(2)}) collective-permute-start(f32[96,128]{1,0:T(8,128)S(1)} %pad_maximum_fusion.2), channel_id=1, source_target_pairs={{0,8},{8,16},{16,24},{24,0},{32,40},{40,48},{48,56},{56,32},{64,72... | collective-permute-start | bytes 147464 | tf_op jit(solution)/shard_map/ppermute | solution.py:672
  100.8 3.3 %collective-permute-start.10 = (f32[96,128]{1,0:T(8,128)S(1)}, f32[96,128]{1,0:T(8,128)S(1)}, u32[]{:S(2)}, u32[]{:S(2)}) collective-permute-start(f32[96,128]{1,0:T(8,128)S(1)} %pad_maximum_fusion.3), channel_id=1, source_target_pairs={{0,24},{8,0},{16,8},{24,16},{32,56},{40,32},{48,40},{56,48},{64,88... | collective-permute-start | bytes 147464 | tf_op jit(solution)/shard_map/ppermute | solution.py:672
  104.2 5.7 %collective-permute-start.13 = (f32[64,128]{1,0:T(8,128)S(1)}, f32[64,128]{1,0:T(8,128)S(1)}, u32[]{:S(2)}, u32[]{:S(2)}) collective-permute-start(f32[64,128]{1,0:T(8,128)S(1)} %fusion), channel_id=1, source_target_pairs={{0,4},{1,5},{2,6},{3,7},{4,0},{5,1},{6,2},{7,3},{8,12},{9,13},{10,... | collective-permute-start | bytes 98312 | tf_op jit(solution)/shard_map/ppermute | solution.py:672
  107.2 4.0 %collective-permute-start.12 = (f32[64,128]{1,0:T(8,128)S(1)}, f32[64,128]{1,0:T(8,128)S(1)}, u32[]{:S(2)}, u32[]{:S(2)}) collective-permute-start(f32[64,128]{1,0:T(8,128)S(1)} %fusion), channel_id=1, source_target_pairs={{0,2},{1,3},{2,4},{3,5},{4,6},{5,7},{6,0},{7,1},{8,10},{9,11},{10,... | collective-permute-start | bytes 98312 | tf_op jit(solution)/shard_map/ppermute | solution.py:672
  107.6 3.6 %collective-permute-start.11 = (f32[64,128]{1,0:T(8,128)S(1)}, f32[64,128]{1,0:T(8,128)S(1)}, u32[]{:S(2)}, u32[]{:S(2)}) collective-permute-start(f32[64,128]{1,0:T(8,128)S(1)} %fusion), channel_id=1, source_target_pairs={{0,6},{1,7},{2,0},{3,1},{4,2},{5,3},{6,4},{7,5},{8,14},{9,15},{10,... | collective-permute-start | bytes 98312 | tf_op jit(solution)/shard_map/ppermute | solution.py:672
  123.0 5.0 %collective-permute-start.14 = (f32[64,128]{1,0:T(8,128)S(1)}, f32[64,128]{1,0:T(8,128)S(1)}, u32[]{:S(2)}, u32[]{:S(2)}) collective-permute-start(f32[64,128]{1,0:T(8,128)S(1)} %reduce_sum.9), channel_id=1, source_target_pairs={{0,1},{1,0},{2,3},{3,2},{4,5},{5,4},{6,7},{7,6},{8,9},{9,8},{10,11... | collective-permute-start | bytes 98312 | tf_op jit(solution)/shard_map/ppermute | solution.py:681
  128.1 5.2 %collective-permute-start.17 = (f32[2,64,128]{2,1,0:T(8,128)S(1)}, f32[2,64,128]{2,1,0:T(8,128)S(1)}, u32[]{:S(2)}, u32[]{:S(2)}) collective-permute-start(f32[2,64,128]{2,1,0:T(8,128)S(1)} %pad_maximum_fusion.both_ref), channel_id=1, source_target_pairs={{0,16},{8,24},{16,0},{24,8},{32,48},{40,56},{48,32},{56,40},{64,80... | collective-permute-start | bytes 196616 | tf_op jit(solution)/shard_map/ppermute | solution.py:672
  129.2 5.6 %collective-permute-start.16 = (f32[2,64,128]{2,1,0:T(8,128)S(1)}, f32[2,64,128]{2,1,0:T(8,128)S(1)}, u32[]{:S(2)}, u32[]{:S(2)}) collective-permute-start(f32[2,64,128]{2,1,0:T(8,128)S(1)} %pad_maximum_fusion.both_ref), channel_id=1, source_target_pairs={{0,8},{8,16},{16,24},{24,0},{32,40},{40,48},{48,56},{56,32},{64,72... | collective-permute-start | bytes 196616 | tf_op jit(solution)/shard_map/ppermute | solution.py:672
  131.5 3.5 %collective-permute-start.15 = (f32[2,64,128]{2,1,0:T(8,128)S(1)}, f32[2,64,128]{2,1,0:T(8,128)S(1)}, u32[]{:S(2)}, u32[]{:S(2)}) collective-permute-start(f32[2,64,128]{2,1,0:T(8,128)S(1)} %pad_maximum_fusion.both_ref), channel_id=1, source_target_pairs={{0,24},{8,0},{16,8},{24,16},{32,56},{40,32},{48,40},{56,48},{64,88... | collective-permute-start | bytes 196616 | tf_op jit(solution)/shard_map/ppermute | solution.py:672

commit v4 on v3

--- a/solution.py
+++ b/solution.py
@@ -14,7 +14,7 @@
 STEPS = 8
 COLS = H + 1
 ROWS = COLS * CHUNKS
-BLOCK = 13
+BLOCKS = (0, 22, 44, 65)
 MAP = 40
 PART = 168
 F32 = jnp.float32
@@ -64,9 +64,21 @@
     return jnp.where(low, value, other) if half == 0 else jnp.where(low, other, value)
 
 
-def right_doubled(matrix):
-    high, low = split(matrix)
-    return jnp.concatenate([high, low, high, low], axis=0)
+def stacked_rows(value):
+    high = value.astype(BF16).astype(F32)
+    return jnp.concatenate([high, value - high], axis=0).astype(BF16)
+
+
+def times_doubled(value, matrix):
+    count = value.shape[0]
+    both = mm(stacked_rows(value), jnp.concatenate(split(matrix), axis=0))
+    return both[:count] + both[count:]
+
+
+def times_wide(value, wide):
+    count, width = value.shape[0], wide.shape[1] // 2
+    both = mm(stacked_rows(value), wide)
+    return both[:count, :width] + both[count:, :width] + both[:count, width:]
 
 
 def left_doubled(value):
@@ -88,7 +100,7 @@
 
 
 def weights_kernel(
-    u_hbm, scale_hbm, other_hbm, w_hbm, w3_ref, ws_ref, uth_ref, utl_ref, ud_ref, bias_ref, w_ref,
+    u_hbm, scale_hbm, other_hbm, w_hbm, w3_ref, ws_ref, ut_ref, ud_ref, bias_ref, w_ref,
     u_ref, scale_ref, other_ref, sems,
 ):
     fetch((u_hbm, scale_hbm, other_hbm, w_hbm), (u_ref, scale_ref, other_ref, w_ref), sems)
@@ -112,8 +124,7 @@
             ws_ref[LANES : 2 * LANES, 3 * LANES :] = low
             ws_ref[2 * LANES : 3 * LANES, 3 * LANES :] = low
         high, low = split(diag.T)
-        uth_ref[at, :] = high
-        utl_ref[at, :] = low
+        ut_ref[at, :] = jnp.concatenate([high, low], axis=1)
     scale = scale_ref[...]
     rows = [jnp.log(scale), other_ref[0:1, :], other_ref[1:2, :], other_ref[2:3, :], scale]
     rows = [jnp.concatenate([row, row], axis=1) for row in rows]
@@ -165,17 +176,17 @@
 
 def scan_maps(coef, ws_ref, ud_ref, maps_ref):
     update, cz, cr, cn, _, offset = coef
-    shape = (BLOCK, CHUNKS, LANES)
     for j in range(STEPS):
         at = slice(j * CHUNKS, (j + 1) * CHUNKS)
         up_j, cz_j, cr_j, cn_j = (a[at][None] for a in (update, cz, cr, cn))
-        for b in range(COLS // BLOCK):
-            rows = slice(b * BLOCK * CHUNKS, (b + 1) * BLOCK * CHUNKS)
-            last = b == COLS // BLOCK - 1
+        for begin, end in zip(BLOCKS, BLOCKS[1:]):
+            rows = slice(begin * CHUNKS, end * CHUNKS)
+            last = end == COLS
+            shape = (end - begin, CHUNKS, LANES)
             if j == 0:
-                real = BLOCK - 1 if last else BLOCK
-                cols = slice(b * BLOCK, b * BLOCK + real)
-                k = lax.broadcasted_iota(jnp.int32, (real, CHUNKS, LANES), 0) + b * BLOCK
+                real = end - begin - 1 if last else end - begin
+                cols = slice(begin, begin + real)
+                k = lax.broadcasted_iota(jnp.int32, (real, CHUNKS, LANES), 0) + begin
                 lane = lax.broadcasted_iota(jnp.int32, (real, CHUNKS, LANES), 2) % H
                 new = jnp.where(k == lane, up_j, 0.0)
                 for c, g in ((cz_j, 0), (cr_j, 1), (cn_j, 2)):
@@ -187,8 +198,8 @@
                 mz, mr, mn = (part.reshape(shape) for part in gate_products(old, ws_ref))
                 new = up_j * old.reshape(shape) + cz_j * mz + cr_j * mr + cn_j * mn
                 if last:
-                    new = jnp.concatenate([new[: BLOCK - 1], new[BLOCK - 1 :] + offset[at][None]], axis=0)
-            maps_ref[j, rows, :] = new.reshape(BLOCK * CHUNKS, LANES)
+                    new = jnp.concatenate([new[:-1], new[-1:] + offset[at][None]], axis=0)
+            maps_ref[j, rows, :] = new.reshape((end - begin) * CHUNKS, LANES)
 
 
 def chunk_matrix(maps_ref, c):
@@ -201,7 +212,7 @@
 
 def compose(earlier, later):
     row = lax.broadcasted_iota(jnp.int32, (72, LANES), 0)
-    both = mm(left3(earlier), right3(block_diagonal(later[:H])))
+    both = times_wide(earlier, jnp.concatenate(split(block_diagonal(later[:H])), axis=1))
     return both + jnp.where(row == H, later[H : H + 1], 0.0)
 
 
@@ -246,7 +257,7 @@
 def join_halves(total):
     row = lax.broadcasted_iota(jnp.int32, (72, LANES), 0)
     second = doubled(total, 1)
-    both = mm(left_doubled(doubled(total, 0)), right_doubled(second[:H]))
+    both = times_doubled(doubled(total, 0), second[:H])
     return both + jnp.where(row == H, second, 0.0)
 
 
@@ -276,7 +287,7 @@
 
 
 def apply_row(state, matrix, vector):
-    return mm(left_doubled(state), right_doubled(matrix)) + vector
+    return times_doubled(state, matrix) + vector
 
 
 def enter_device(where_ref, own_ref, other_ref, start, reverse):
@@ -470,7 +481,7 @@
 
 
 def gradient_kernel(
-    where_ref, own_ref, other_ref, coef_ref, chunk_ref, vector_ref, half_ref, cot_ref, uth_ref, utl_ref,
+    where_ref, own_ref, other_ref, coef_ref, chunk_ref, vector_ref, half_ref, cot_ref, ut_ref,
     xin_ref, bias_ref, states_ref, across_ref, keep_ref, give_ref, home_ref, full_ref,
 ):
     low = lane_low((CHUNKS, LANES))
@@ -494,9 +505,7 @@
         dz[j], dr[j], dn[j] = coef_ref[2, at, :] * lam, coef_ref[3, at, :] * lam, coef_ref[4, at, :] * lam
         ds[j] = coef_ref[5, at, :] * lam
         if j > 0:
-            high, low_part = split(jnp.concatenate([dz[j], dr[j], dn[j]], axis=1))
-            both = mm(jnp.concatenate([high, low_part], axis=0), uth_ref[...])
-            pulled = both[:CHUNKS] + both[CHUNKS:] + mm(high, utl_ref[...])
+            pulled = times_wide(jnp.concatenate([dz[j], dr[j], dn[j]], axis=1), ut_ref[...])
             passed = coef_ref[1, at, :] * lam + pulled
     dz, dr, dn, ds = (jnp.concatenate(part, axis=0) for part in (dz, dr, dn, ds))
 
@@ -623,10 +632,10 @@
     )
     one = lax.ppermute(one, axes, there[0])
     two = lax.ppermute(two, axes, there[1])
-    w3, ws, uth, utl, ud, bias, w = call(
+    w3, ws, ut, ud, bias, w = call(
         weights_kernel,
         [
-            ((384, 384), BF16), ((384, 512), BF16), ((384, LANES), BF16), ((384, LANES), BF16),
+            ((384, 384), BF16), ((384, 512), BF16), ((384, 2 * LANES), BF16),
             ((3, H, LANES), F32), ((8, LANES), F32), ((192, 256), BF16),
         ],
         "hhhh", u_rec, timescale[None, :], other_bias, w_in.T,
@@ -663,8 +672,8 @@
     across = lax.ppermute(states, "batch", cores)
     own, other = exchange(send)
     keep, give, home = call(
-        gradient_kernel, [((256, LANES), F32), ((256, LANES), F32), ((4, 32, LANES), F32)], "svvvvvvvvvvvvv",
-        where, own, other, coef, chunk, vector, half, cot, uth, utl, xin, bias, states, across,
+        gradient_kernel, [((256, LANES), F32), ((256, LANES), F32), ((4, 32, LANES), F32)], "svvvvvvvvvvvv",
+        where, own, other, coef, chunk, vector, half, cot, ut, xin, bias, states, across,
         scratch=[pltpu.VMEM((512, LANES), F32)],
     )
 

time: 137 us -> 136 us (level)
  no operation moved by 1% of the time
where the time goes in v4:
time: 136 us; the launch traced here: 135 us
  blocking collectives  63.7 us (47%)
  starting transfers between devices  28.7 us (21%)
  Pallas kernels  27 us (20%)
  waiting for transfers between devices  14.8 us (11%)
    all_to_all x4, blocking collectives, exchange(): lax.all_to_all(value, 'seq', 0, 0, axis_index_groups=along_z, tiled=True)  51.9 us
    pallas_call x9, Pallas kernels, call(): pl.pallas_call(kernel, out_shape=[jax.ShapeDtypeStruct(*out) for out in o...  27 us
    ppermute x9, starting transfers between devices, around(): got = {d: lax.ppermute(value_of(d), axis, steps[d]) for d in order}  13.8 us
    all_to_all x1, blocking collectives, local(): lax.all_to_all(wide, 'seq', 0, 0, axis_index_groups=along_z, tiled=True)  11.8 us
    ppermute x1, starting transfers between devices, local(): one = lax.ppermute(one, axes, there[0])  6.04 us
    ppermute x9, waiting for transfers between devices, around(): got = {d: lax.ppermute(value_of(d), axis, steps[d]) for d in order}  4.79 us
    ppermute x1, starting transfers between devices, local(): other = lax.ppermute(part, 'batch', cores)  4.17 us
    ppermute x4, starting transfers between devices, exchange(): return (own, lax.ppermute(own, 'batch', cores))  3.74 us
  transfers between devices with their start and end apart: 18, of which 13 were waited for; matrix products, arithmetic and copies ran while one was open for 0% of the time, Pallas kernels for 2%

profile of v4, /device:TPU:1, one launch (start us, length us, event | category | flops | bytes accessed | tf_op | source)
XLA Modules:
  0.0 135.2 jit_solution(15558259916929313984)
XLA Ops:
  0.7 0.1 pad_add_fusion.where_ref
  0.8 1.6 %shard_map.110 = (f32[168,128]{1,0:T(8,128)S(1)}, f32[168,128]{1,0:T(8,128)S(1)}) custom-call(s32[4]{0:T(128)S(1)} %pad_add_fusion.where_ref, bf16[2,64,256]{2,1,0:T(8,128)(2,1)} %x_hbm.1, f32[64,2,64]{2,1,0:T(2,128)} %cot_hbm.1, f32[2,64]{1,0:T(2,128)} %bitcast.20), custom_call_target="tpu_custom_call" | custom-call | tf_op jit(solution)/shard_map/pallas_call | solution.py:588
  2.4 6.0 %collective-permute-start = (f32[168,128]{1,0:T(8,128)S(1)}, f32[168,128]{1,0:T(8,128)S(1)}, u32[]{:S(2)}, u32[]{:S(2)}) collective-permute-start(f32[168,128]{1,0:T(8,128)S(1)} %get-tuple-element.45), channel_id=1, source_target_pairs={{0,0},{1,16},{2,2},{3,18},{4,4},{5,20},{6,6},{7,22},{8,8},{9,24},{... | collective-permute-start | bytes 258056 | tf_op jit(solution)/shard_map/ppermute | solution.py:633
  8.4 0.7 collective-permute-start.1
  9.1 1.2 shard_map.111
  10.3 0.3 collective-permute-done.a_ref
  10.6 3.1 %collective-permute-done.1.b_ref = f32[168,128]{1,0:T(8,128)S(1)} collective-permute-done((f32[168,128]{1,0:T(8,128)S(1)}, f32[168,128]{1,0:T(8,128)S(1)}, u32[]{:S(2)}, u32[]{:S(2)}) %collective-permute-start.1) | collective-permute-done | bytes 86048 | tf_op jit(solution)/shard_map/ppermute | solution.py:634
  13.6 3.4 %shard_map.112 = (f32[3,64,128]{2,1,0:T(8,128)S(1)}, bf16[128,256]{1,0:T(8,128)(2,1)S(1)}, f32[64,128]{1,0:T(8,128)S(1)}, f32[8,128]{1,0:T(8,128)S(1)}, f32[8,52...) custom-call(s32[4]{0:T(128)S(1)} %pad_add_fusion.where_ref, ...), custom_call_target="tpu_custom_call" | custom-call | tf_op jit(solution)/shard_map/pallas_call | solution.py:588
  17.1 16.3 %all_to_all.25.own_ref = f32[8,40,128]{2,1,0:T(8,128)S(1)} all-to-all(f32[8,40,128]{2,1,0:T(8,128)S(1)} %get-tuple-element.52), channel_id=1, replica_groups={{0,32,64,96,128,160,192,224},{8,40,72,104,136,168,200,232},{16,48,80,11..., dimensions={0} | all-to-all | bytes 327680 | tf_op jit(solution)/shard_map/all_to_all | solution.py:623
  33.4 0.0 collective-permute-start.2
  33.4 1.4 %collective-permute-done.2.other_ref = f32[8,40,128]{2,1,0:T(8,128)S(1)} collective-permute-done((f32[8,40,128]{2,1,0:T(8,128)S(1)}, f32[8,40,128]{2,1,0:T(8,128)S(1)}, u32[]{:S(2)}, u32[]{:S(2)}) %collective-permute-start.2) | collective-permute-done | bytes 163872 | tf_op jit(solution)/shard_map/ppermute | solution.py:624
  34.8 4.9 %shard_map.113 = (f32[8,520,128]{2,1,0:T(8,128)S(1)}, f32[8,64,128]{2,1,0:T(8,128)S(1)}, f32[8,128]{1,0:T(8,128)S(1)}, f32[72,128]{1,0:T(8,128)S(1)}, f32[8,40,128]{2,1,0:T(8,128)S(1)}) custom-call(s32[4]{0:T(128)S(1)} %pad_add_fusion.where_ref, f32[8,40,128]{2,1,0:T(8,128)S(1)} %all_to_all.25.own_ref, f32[8,40,128]{2,1,0:T(8,128)S(1)} %collective-permute-done.2.other_ref, ...), custom_call_target="tpu_custom_call" | custom-call | tf_op jit(solution)/shard_map/pallas_call | solution.py:588
  39.7 12.5 %all_to_all.26.own_ref = f32[8,40,128]{2,1,0:T(8,128)S(1)} all-to-all(f32[8,40,128]{2,1,0:T(8,128)S(1)} %get-tuple-element.59), channel_id=1, replica_groups={{0,32,64,96,128,160,192,224},{8,40,72,104,136,168,200,232},{16,48,80,11..., dimensions={0} | all-to-all | bytes 327680 | tf_op jit(solution)/shard_map/all_to_all | solution.py:623
  52.2 0.6 collective-permute-start.3
  52.8 1.0 collective-permute-done.3.other_ref
  53.8 4.9 %shard_map.114 = (f32[8,520,128]{2,1,0:T(8,128)S(1)}, f32[8,64,128]{2,1,0:T(8,128)S(1)}, f32[8,128]{1,0:T(8,128)S(1)}, f32[72,128]{1,0:T(8,128)S(1)}, f32[8,40,128]{2,1,0:T(8,128)S(1)}) custom-call(s32[4]{0:T(128)S(1)} %pad_add_fusion.where_ref, f32[8,40,128]{2,1,0:T(8,128)S(1)} %all_to_all.26.own_ref, f32[8,40,128]{2,1,0:T(8,128)S(1)} %collective-permute-done.3.other_ref, ...), custom_call_target="tpu_custom_call" | custom-call | tf_op jit(solution)/shard_map/pallas_call | solution.py:588
  58.7 11.5 %all_to_all.27.own_ref = f32[8,40,128]{2,1,0:T(8,128)S(1)} all-to-all(f32[8,40,128]{2,1,0:T(8,128)S(1)} %get-tuple-element.64), channel_id=1, replica_groups={{0,32,64,96,128,160,192,224},{8,40,72,104,136,168,200,232},{16,48,80,11..., dimensions={0} | all-to-all | bytes 327680 | tf_op jit(solution)/shard_map/all_to_all | solution.py:623
  70.2 1.6 %collective-permute-start.4 = (f32[8,40,128]{2,1,0:T(8,128)S(1)}, f32[8,40,128]{2,1,0:T(8,128)S(1)}, u32[]{:S(2)}, u32[]{:S(2)}) collective-permute-start(f32[8,40,128]{2,1,0:T(8,128)S(1)} %all_to_all.27.own_ref), channel_id=1, source_target_pairs={{0,1},{1,0},{2,3},{3,2},{4,5},{5,4},{6,7},{7,6},{8,9},{9,8},{10,11... | collective-permute-start | bytes 491528 | tf_op jit(solution)/shard_map/ppermute | solution.py:624
  71.8 1.0 collective-permute-done.4.other_ref
  72.9 5.3 %shard_map.115 = (f32[64,128]{1,0:T(8,128)S(1)}, f32[6,64,128]{2,1,0:T(8,128)S(1)}, f32[8,64,128]{2,1,0:T(8,128)S(1)}, f32[8,128]{1,0:T(8,128)S(1)}, f32[72,128]{1,0:T(8,128)S(1)}, /*index=5*/f32[8,40,128]{2,1,0:T(8,128)S(1)}) custom-call(s32[4]{0:T(128)S(1)} %pad_add_fusion.where_ref, f32[8,40,128]{2,1,0:T(8,128)S(1)} %all_to_all.27.own_ref, ...), custom_call_target="tpu_custom_call" | custom-call | tf_op jit(solution)/shard_map/pallas_call | solution.py:588
  78.2 11.5 %all_to_all.28.own_ref = f32[8,40,128]{2,1,0:T(8,128)S(1)} all-to-all(f32[8,40,128]{2,1,0:T(8,128)S(1)} %get-tuple-element.70), channel_id=1, replica_groups={{0,32,64,96,128,160,192,224},{8,40,72,104,136,168,200,232},{16,48,80,11..., dimensions={0} | all-to-all | bytes 327680 | tf_op jit(solution)/shard_map/all_to_all | solution.py:623
  89.7 1.6 %collective-permute-start.5 = (f32[8,40,128]{2,1,0:T(8,128)S(1)}, f32[8,40,128]{2,1,0:T(8,128)S(1)}, u32[]{:S(2)}, u32[]{:S(2)}) collective-permute-start(f32[8,40,128]{2,1,0:T(8,128)S(1)} %all_to_all.28.own_ref), channel_id=1, source_target_pairs={{0,1},{1,0},{2,3},{3,2},{4,5},{5,4},{6,7},{7,6},{8,9},{9,8},{10,11... | collective-permute-start | bytes 491528 | tf_op jit(solution)/shard_map/ppermute | solution.py:624
  91.3 0.0 collective-permute-start.6
  91.3 1.2 collective-permute-done.6.across_ref
  92.5 0.0 collective-permute-done.5.other_ref
  92.5 3.0 %shard_map.116 = (f32[256,128]{1,0:T(8,128)S(1)}, f32[256,128]{1,0:T(8,128)S(1)}, f32[4,32,128]{2,1,0:T(8,128)S(1)}) custom-call(s32[4]{0:T(128)S(1)} %pad_add_fusion.where_ref, f32[8,40,128]{2,1,0:T(8,128)S(1)} %all_to_all.28.own_ref, f32[8,40,128]{2,1,0:T(8,128)S(1)} %collective-permute-done.5.other_ref, f32[6,64,128]{2,1,0:T(8,128)S(1)} %get-tuple-element.71.coef_ref, ...), custom_call_target="tpu_custom_call" | custom-call | tf_op jit(solution)/shard_map/pallas_call | solution.py:588
  95.5 0.3 collective-permute-start.7
  95.9 1.1 collective-permute-done.7
  97.0 1.6 %collective-permute-start.8 = (f32[96,128]{1,0:T(8,128)S(1)}, f32[96,128]{1,0:T(8,128)S(1)}, u32[]{:S(2)}, u32[]{:S(2)}) collective-permute-start(f32[96,128]{1,0:T(8,128)S(1)} %pad_maximum_fusion.1), channel_id=1, source_target_pairs={{0,16},{8,24},{16,0},{24,8},{32,48},{40,56},{48,32},{56,40},{64,80... | collective-permute-start | bytes 147464 | tf_op jit(solution)/shard_map/ppermute | solution.py:681
  98.6 1.1 collective-permute-start.9
  99.7 1.6 %collective-permute-start.10 = (f32[96,128]{1,0:T(8,128)S(1)}, f32[96,128]{1,0:T(8,128)S(1)}, u32[]{:S(2)}, u32[]{:S(2)}) collective-permute-start(f32[96,128]{1,0:T(8,128)S(1)} %pad_maximum_fusion.3), channel_id=1, source_target_pairs={{0,24},{8,0},{16,8},{24,16},{32,56},{40,32},{48,40},{56,48},{64,88... | collective-permute-start | bytes 147464 | tf_op jit(solution)/shard_map/ppermute | solution.py:681
  101.3 0.2 collective-permute-done.8.two_ref
  101.5 1.5 %collective-permute-done.9.one_ref = f32[96,128]{1,0:T(8,128)S(1)} collective-permute-done((f32[96,128]{1,0:T(8,128)S(1)}, f32[96,128]{1,0:T(8,128)S(1)}, u32[]{:S(2)}, u32[]{:S(2)}) %collective-permute-start.9) | collective-permute-done | bytes 49184 | tf_op jit(solution)/shard_map/ppermute | solution.py:681
  103.0 0.0 collective-permute-done.10.three_ref
  103.0 3.0 %collective-permute-start.13 = (f32[64,128]{1,0:T(8,128)S(1)}, f32[64,128]{1,0:T(8,128)S(1)}, u32[]{:S(2)}, u32[]{:S(2)}) collective-permute-start(f32[64,128]{1,0:T(8,128)S(1)} %fusion), channel_id=1, source_target_pairs={{0,4},{1,5},{2,6},{3,7},{4,0},{5,1},{6,2},{7,3},{8,12},{9,13},{10,... | collective-permute-start | bytes 98312 | tf_op jit(solution)/shard_map/ppermute | solution.py:681
  106.0 0.4 collective-permute-start.12
  106.4 2.3 %collective-permute-start.11 = (f32[64,128]{1,0:T(8,128)S(1)}, f32[64,128]{1,0:T(8,128)S(1)}, u32[]{:S(2)}, u32[]{:S(2)}) collective-permute-start(f32[64,128]{1,0:T(8,128)S(1)} %fusion), channel_id=1, source_target_pairs={{0,6},{1,7},{2,0},{3,1},{4,2},{5,3},{6,4},{7,5},{8,14},{9,15},{10,... | collective-permute-start | bytes 98312 | tf_op jit(solution)/shard_map/ppermute | solution.py:681
  108.7 0.0 collective-permute-done.13
  108.7 1.3 collective-permute-done.12
  110.0 0.0 collective-permute-done.11
  110.1 11.8 %all_to_all.29 = f32[8,64,128]{2,1,0:T(8,128)S(1)} all-to-all(f32[8,64,128]{2,1,0:T(8,128)S(1)} %broadcast_in_dim.10), channel_id=1, replica_groups={{0,32,64,96,128,160,192,224},{8,40,72,104,136,168,200,232},{16,48,80,11..., dimensions={0} | all-to-all | bytes 524288 | tf_op jit(solution)/shard_map/all_to_all | solution.py:689
  121.9 4.2 %collective-permute-start.14 = (f32[64,128]{1,0:T(8,128)S(1)}, f32[64,128]{1,0:T(8,128)S(1)}, u32[]{:S(2)}, u32[]{:S(2)}) collective-permute-start(f32[64,128]{1,0:T(8,128)S(1)} %reduce_sum.9), channel_id=1, source_target_pairs={{0,1},{1,0},{2,3},{3,2},{4,5},{5,4},{6,7},{7,6},{8,9},{9,8},{10,11... | collective-permute-start | bytes 98312 | tf_op jit(solution)/shard_map/ppermute | solution.py:690
  126.1 0.9 collective-permute-done.14
  126.9 1.1 collective-permute-start.17
  128.1 2.3 %collective-permute-start.16 = (f32[2,64,128]{2,1,0:T(8,128)S(1)}, f32[2,64,128]{2,1,0:T(8,128)S(1)}, u32[]{:S(2)}, u32[]{:S(2)}) collective-permute-start(f32[2,64,128]{2,1,0:T(8,128)S(1)} %pad_maximum_fusion.both_ref), channel_id=1, source_target_pairs={{0,8},{8,16},{16,24},{24,0},{32,40},{40,48},{48,56},{56,32},{64,72... | collective-permute-start | bytes 196616 | tf_op jit(solution)/shard_map/ppermute | solution.py:681
  130.4 0.3 collective-permute-start.15
  130.7 1.3 shard_map.117
  132.1 0.0 collective-permute-done.17.two_ref
  132.1 1.6 %collective-permute-done.16.one_ref = f32[2,64,128]{2,1,0:T(8,128)S(1)} collective-permute-done((f32[2,64,128]{2,1,0:T(8,128)S(1)}, f32[2,64,128]{2,1,0:T(8,128)S(1)}, u32[]{:S(2)}, u32[]{:S(2)}) %collective-permute-start.16) | collective-permute-done | bytes 65568 | tf_op jit(solution)/shard_map/ppermute | solution.py:681
  133.6 0.2 collective-permute-done.15.three_ref
  133.9 1.3 shard_map.118
  (12 shorter events, 0.1 us)
Async XLA Ops:
  2.4 8.2 %collective-permute-start = (f32[168,128]{1,0:T(8,128)S(1)}, f32[168,128]{1,0:T(8,128)S(1)}, u32[]{:S(2)}, u32[]{:S(2)}) collective-permute-start(f32[168,128]{1,0:T(8,128)S(1)} %get-tuple-element.45), channel_id=1, source_target_pairs={{0,0},{1,16},{2,2},{3,18},{4,4},{5,20},{6,6},{7,22},{8,8},{9,24},{... | collective-permute-start | bytes 258056 | tf_op jit(solution)/shard_map/ppermute | solution.py:633
  8.4 5.2 %collective-permute-start.1 = (f32[168,128]{1,0:T(8,128)S(1)}, f32[168,128]{1,0:T(8,128)S(1)}, u32[]{:S(2)}, u32[]{:S(2)}) collective-permute-start(f32[168,128]{1,0:T(8,128)S(1)} %get-tuple-element.46), channel_id=1, source_target_pairs={{0,8},{1,24},{2,10},{3,26},{4,12},{5,28},{6,14},{7,30},{8,0},{9,16... | collective-permute-start | bytes 258056 | tf_op jit(solution)/shard_map/ppermute | solution.py:634
  33.4 1.4 %collective-permute-start.2 = (f32[8,40,128]{2,1,0:T(8,128)S(1)}, f32[8,40,128]{2,1,0:T(8,128)S(1)}, u32[]{:S(2)}, u32[]{:S(2)}) collective-permute-start(f32[8,40,128]{2,1,0:T(8,128)S(1)} %all_to_all.25.own_ref), channel_id=1, source_target_pairs={{0,1},{1,0},{2,3},{3,2},{4,5},{5,4},{6,7},{7,6},{8,9},{9,8},{10,11... | collective-permute-start | bytes 491528 | tf_op jit(solution)/shard_map/ppermute | solution.py:624
  52.2 1.6 %collective-permute-start.3 = (f32[8,40,128]{2,1,0:T(8,128)S(1)}, f32[8,40,128]{2,1,0:T(8,128)S(1)}, u32[]{:S(2)}, u32[]{:S(2)}) collective-permute-start(f32[8,40,128]{2,1,0:T(8,128)S(1)} %all_to_all.26.own_ref), channel_id=1, source_target_pairs={{0,1},{1,0},{2,3},{3,2},{4,5},{5,4},{6,7},{7,6},{8,9},{9,8},{10,11... | collective-permute-start | bytes 491528 | tf_op jit(solution)/shard_map/ppermute | solution.py:624
  70.2 2.6 %collective-permute-start.4 = (f32[8,40,128]{2,1,0:T(8,128)S(1)}, f32[8,40,128]{2,1,0:T(8,128)S(1)}, u32[]{:S(2)}, u32[]{:S(2)}) collective-permute-start(f32[8,40,128]{2,1,0:T(8,128)S(1)} %all_to_all.27.own_ref), channel_id=1, source_target_pairs={{0,1},{1,0},{2,3},{3,2},{4,5},{5,4},{6,7},{7,6},{8,9},{9,8},{10,11... | collective-permute-start | bytes 491528 | tf_op jit(solution)/shard_map/ppermute | solution.py:624
  89.7 2.8 %collective-permute-start.5 = (f32[8,40,128]{2,1,0:T(8,128)S(1)}, f32[8,40,128]{2,1,0:T(8,128)S(1)}, u32[]{:S(2)}, u32[]{:S(2)}) collective-permute-start(f32[8,40,128]{2,1,0:T(8,128)S(1)} %all_to_all.28.own_ref), channel_id=1, source_target_pairs={{0,1},{1,0},{2,3},{3,2},{4,5},{5,4},{6,7},{7,6},{8,9},{9,8},{10,11... | collective-permute-start | bytes 491528 | tf_op jit(solution)/shard_map/ppermute | solution.py:624
  91.3 1.2 collective-permute-start.6
  95.5 1.4 %collective-permute-start.7 = (f32[256,128]{1,0:T(8,128)S(1)}, f32[256,128]{1,0:T(8,128)S(1)}, u32[]{:S(2)}, u32[]{:S(2)}) collective-permute-start(f32[256,128]{1,0:T(8,128)S(1)} %get-tuple-element.80), channel_id=1, source_target_pairs={{0,1},{1,0},{2,3},{3,2},{4,5},{5,4},{6,7},{7,6},{8,9},{9,8},{10,11... | collective-permute-start | bytes 393224 | tf_op jit(solution)/shard_map/ppermute | solution.py:684
  97.0 4.5 %collective-permute-start.8 = (f32[96,128]{1,0:T(8,128)S(1)}, f32[96,128]{1,0:T(8,128)S(1)}, u32[]{:S(2)}, u32[]{:S(2)}) collective-permute-start(f32[96,128]{1,0:T(8,128)S(1)} %pad_maximum_fusion.1), channel_id=1, source_target_pairs={{0,16},{8,24},{16,0},{24,8},{32,48},{40,56},{48,32},{56,40},{64,80... | collective-permute-start | bytes 147464 | tf_op jit(solution)/shard_map/ppermute | solution.py:681
  98.6 4.4 %collective-permute-start.9 = (f32[96,128]{1,0:T(8,128)S(1)}, f32[96,128]{1,0:T(8,128)S(1)}, u32[]{:S(2)}, u32[]{:S(2)}) collective-permute-start(f32[96,128]{1,0:T(8,128)S(1)} %pad_maximum_fusion.2), channel_id=1, source_target_pairs={{0,8},{8,16},{16,24},{24,0},{32,40},{40,48},{48,56},{56,32},{64,72... | collective-permute-start | bytes 147464 | tf_op jit(solution)/shard_map/ppermute | solution.py:681
  99.7 3.3 %collective-permute-start.10 = (f32[96,128]{1,0:T(8,128)S(1)}, f32[96,128]{1,0:T(8,128)S(1)}, u32[]{:S(2)}, u32[]{:S(2)}) collective-permute-start(f32[96,128]{1,0:T(8,128)S(1)} %pad_maximum_fusion.3), channel_id=1, source_target_pairs={{0,24},{8,0},{16,8},{24,16},{32,56},{40,32},{48,40},{56,48},{64,88... | collective-permute-start | bytes 147464 | tf_op jit(solution)/shard_map/ppermute | solution.py:681
  103.0 5.7 %collective-permute-start.13 = (f32[64,128]{1,0:T(8,128)S(1)}, f32[64,128]{1,0:T(8,128)S(1)}, u32[]{:S(2)}, u32[]{:S(2)}) collective-permute-start(f32[64,128]{1,0:T(8,128)S(1)} %fusion), channel_id=1, source_target_pairs={{0,4},{1,5},{2,6},{3,7},{4,0},{5,1},{6,2},{7,3},{8,12},{9,13},{10,... | collective-permute-start | bytes 98312 | tf_op jit(solution)/shard_map/ppermute | solution.py:681
  106.0 4.0 %collective-permute-start.12 = (f32[64,128]{1,0:T(8,128)S(1)}, f32[64,128]{1,0:T(8,128)S(1)}, u32[]{:S(2)}, u32[]{:S(2)}) collective-permute-start(f32[64,128]{1,0:T(8,128)S(1)} %fusion), channel_id=1, source_target_pairs={{0,2},{1,3},{2,4},{3,5},{4,6},{5,7},{6,0},{7,1},{8,10},{9,11},{10,... | collective-permute-start | bytes 98312 | tf_op jit(solution)/shard_map/ppermute | solution.py:681
  106.4 3.6 %collective-permute-start.11 = (f32[64,128]{1,0:T(8,128)S(1)}, f32[64,128]{1,0:T(8,128)S(1)}, u32[]{:S(2)}, u32[]{:S(2)}) collective-permute-start(f32[64,128]{1,0:T(8,128)S(1)} %fusion), channel_id=1, source_target_pairs={{0,6},{1,7},{2,0},{3,1},{4,2},{5,3},{6,4},{7,5},{8,14},{9,15},{10,... | collective-permute-start | bytes 98312 | tf_op jit(solution)/shard_map/ppermute | solution.py:681
  121.9 5.0 %collective-permute-start.14 = (f32[64,128]{1,0:T(8,128)S(1)}, f32[64,128]{1,0:T(8,128)S(1)}, u32[]{:S(2)}, u32[]{:S(2)}) collective-permute-start(f32[64,128]{1,0:T(8,128)S(1)} %reduce_sum.9), channel_id=1, source_target_pairs={{0,1},{1,0},{2,3},{3,2},{4,5},{5,4},{6,7},{7,6},{8,9},{9,8},{10,11... | collective-permute-start | bytes 98312 | tf_op jit(solution)/shard_map/ppermute | solution.py:690
  126.9 5.2 %collective-permute-start.17 = (f32[2,64,128]{2,1,0:T(8,128)S(1)}, f32[2,64,128]{2,1,0:T(8,128)S(1)}, u32[]{:S(2)}, u32[]{:S(2)}) collective-permute-start(f32[2,64,128]{2,1,0:T(8,128)S(1)} %pad_maximum_fusion.both_ref), channel_id=1, source_target_pairs={{0,16},{8,24},{16,0},{24,8},{32,48},{40,56},{48,32},{56,40},{64,80... | collective-permute-start | bytes 196616 | tf_op jit(solution)/shard_map/ppermute | solution.py:681
  128.1 5.6 %collective-permute-start.16 = (f32[2,64,128]{2,1,0:T(8,128)S(1)}, f32[2,64,128]{2,1,0:T(8,128)S(1)}, u32[]{:S(2)}, u32[]{:S(2)}) collective-permute-start(f32[2,64,128]{2,1,0:T(8,128)S(1)} %pad_maximum_fusion.both_ref), channel_id=1, source_target_pairs={{0,8},{8,16},{16,24},{24,0},{32,40},{40,48},{48,56},{56,32},{64,72... | collective-permute-start | bytes 196616 | tf_op jit(solution)/shard_map/ppermute | solution.py:681
  130.4 3.5 %collective-permute-start.15 = (f32[2,64,128]{2,1,0:T(8,128)S(1)}, f32[2,64,128]{2,1,0:T(8,128)S(1)}, u32[]{:S(2)}, u32[]{:S(2)}) collective-permute-start(f32[2,64,128]{2,1,0:T(8,128)S(1)} %pad_maximum_fusion.both_ref), channel_id=1, source_target_pairs={{0,24},{8,0},{16,8},{24,16},{32,56},{40,32},{48,40},{56,48},{64,88... | collective-permute-start | bytes 196616 | tf_op jit(solution)/shard_map/ppermute | solution.py:681

commit v5 on v4

--- a/solution.py
+++ b/solution.py
@@ -302,7 +302,8 @@
     for n in reversed(order) if reverse else order:
         z, kappa = n // 2, n % 2
         reached = (mine < n) if reverse else (mine > n)
-        packed = jnp.where(core == kappa, own_ref[z], other_ref[z])
+        at = (z + planes // 2) % planes
+        packed = jnp.where(core == kappa, own_ref[at], other_ref[at])
         to_column = kappa == (1 if reverse else 0)
         matrix, vector = unpack_map(packed, not to_column)
         vector = jnp.where(reached, vector, 0.0)
@@ -614,7 +615,7 @@
         d: [(z * width + x, z * width + (x + d) % width) for z in range(planes) for x in range(width)]
         for d in range(1, width)
     }
-    along_z = [[z * width + x for z in range(planes)] for x in range(width)]
+    along_z = [[(z + planes // 2) % planes * width + x for z in range(planes)] for x in range(width)]
     step_y = {d: [(b, (b + 2 * d) % (2 * ys)) for b in range(2 * ys)] for d in range(1, ys)}
     cores = [(b, b ^ 1) for b in range(2 * ys)]
     axes = ("seq", "batch")

time: 136 us -> 133 us (0.978)
  blocking collectives: 63.7 us -> 61.1 us
    all_to_all x4, blocking collectives: 51.9 us -> 49.4 us  [exchange(): lax.all_to_all(value, 'seq', 0, 0, axis_index_groups=along_z, tiled=True)]
where the time goes in v5:
time: 133 us; the launch traced here: 132 us
  blocking collectives  61.1 us (46%)
  starting transfers between devices  27.8 us (21%)
  Pallas kernels  27 us (20%)
  waiting for transfers between devices  14.7 us (11%)
    all_to_all x4, blocking collectives, exchange(): lax.all_to_all(value, 'seq', 0, 0, axis_index_groups=along_z, tiled=True)  49.4 us
    pallas_call x9, Pallas kernels, call(): pl.pallas_call(kernel, out_shape=[jax.ShapeDtypeStruct(*out) for out in o...  27 us
    ppermute x9, starting transfers between devices, around(): got = {d: lax.ppermute(value_of(d), axis, steps[d]) for d in order}  13.8 us
    all_to_all x1, blocking collectives, local(): lax.all_to_all(wide, 'seq', 0, 0, axis_index_groups=along_z, tiled=True)  11.7 us
    ppermute x1, starting transfers between devices, local(): one = lax.ppermute(one, axes, there[0])  6.04 us
    ppermute x9, waiting for transfers between devices, around(): got = {d: lax.ppermute(value_of(d), axis, steps[d]) for d in order}  4.79 us
    ppermute x1, starting transfers between devices, local(): other = lax.ppermute(part, 'batch', cores)  4.24 us
    ppermute x4, waiting for transfers between devices, exchange(): return (own, lax.ppermute(own, 'batch', cores))  3.45 us
  transfers between devices with their start and end apart: 18, of which 13 were waited for; matrix products, arithmetic and copies ran while one was open for 0% of the time, Pallas kernels for 2%

profile of v5, /device:TPU:1, one launch (start us, length us, event | category | flops | bytes accessed | tf_op | source)
XLA Modules:
  0.0 131.7 jit_solution(12407650593740120924)
XLA Ops:
  0.7 0.1 pad_add_fusion.where_ref
  0.8 1.6 %shard_map.110 = (f32[168,128]{1,0:T(8,128)S(1)}, f32[168,128]{1,0:T(8,128)S(1)}) custom-call(s32[4]{0:T(128)S(1)} %pad_add_fusion.where_ref, bf16[2,64,256]{2,1,0:T(8,128)(2,1)} %x_hbm.1, f32[64,2,64]{2,1,0:T(2,128)} %cot_hbm.1, f32[2,64]{1,0:T(2,128)} %bitcast.20), custom_call_target="tpu_custom_call" | custom-call | tf_op jit(solution)/shard_map/pallas_call | solution.py:589
  2.4 6.0 %collective-permute-start = (f32[168,128]{1,0:T(8,128)S(1)}, f32[168,128]{1,0:T(8,128)S(1)}, u32[]{:S(2)}, u32[]{:S(2)}) collective-permute-start(f32[168,128]{1,0:T(8,128)S(1)} %get-tuple-element.45), channel_id=1, source_target_pairs={{0,0},{1,16},{2,2},{3,18},{4,4},{5,20},{6,6},{7,22},{8,8},{9,24},{... | collective-permute-start | bytes 258056 | tf_op jit(solution)/shard_map/ppermute | solution.py:634
  8.4 0.7 collective-permute-start.1
  9.1 1.2 shard_map.111
  10.3 0.3 collective-permute-done.a_ref
  10.6 3.1 %collective-permute-done.1.b_ref = f32[168,128]{1,0:T(8,128)S(1)} collective-permute-done((f32[168,128]{1,0:T(8,128)S(1)}, f32[168,128]{1,0:T(8,128)S(1)}, u32[]{:S(2)}, u32[]{:S(2)}) %collective-permute-start.1) | collective-permute-done | bytes 86048 | tf_op jit(solution)/shard_map/ppermute | solution.py:635
  13.6 3.4 %shard_map.112 = (f32[3,64,128]{2,1,0:T(8,128)S(1)}, bf16[128,256]{1,0:T(8,128)(2,1)S(1)}, f32[64,128]{1,0:T(8,128)S(1)}, f32[8,128]{1,0:T(8,128)S(1)}, f32[8,52...) custom-call(s32[4]{0:T(128)S(1)} %pad_add_fusion.where_ref, ...), custom_call_target="tpu_custom_call" | custom-call | tf_op jit(solution)/shard_map/pallas_call | solution.py:589
  17.1 12.8 %all_to_all.25.own_ref = f32[8,40,128]{2,1,0:T(8,128)S(1)} all-to-all(f32[8,40,128]{2,1,0:T(8,128)S(1)} %get-tuple-element.52), channel_id=1, replica_groups={{128,160,192,224,0,32,64,96},{136,168,200,232,8,40,72,104},{144,176,208..., dimensions={0} | all-to-all | bytes 327680 | tf_op jit(solution)/shard_map/all_to_all | solution.py:624
  29.9 0.0 collective-permute-start.2
  29.9 1.4 %collective-permute-done.2.other_ref = f32[8,40,128]{2,1,0:T(8,128)S(1)} collective-permute-done((f32[8,40,128]{2,1,0:T(8,128)S(1)}, f32[8,40,128]{2,1,0:T(8,128)S(1)}, u32[]{:S(2)}, u32[]{:S(2)}) %collective-permute-start.2) | collective-permute-done | bytes 163872 | tf_op jit(solution)/shard_map/ppermute | solution.py:625
  31.3 4.9 %shard_map.113 = (f32[8,520,128]{2,1,0:T(8,128)S(1)}, f32[8,64,128]{2,1,0:T(8,128)S(1)}, f32[8,128]{1,0:T(8,128)S(1)}, f32[72,128]{1,0:T(8,128)S(1)}, f32[8,40,128]{2,1,0:T(8,128)S(1)}) custom-call(s32[4]{0:T(128)S(1)} %pad_add_fusion.where_ref, f32[8,40,128]{2,1,0:T(8,128)S(1)} %all_to_all.25.own_ref, f32[8,40,128]{2,1,0:T(8,128)S(1)} %collective-permute-done.2.other_ref, ...), custom_call_target="tpu_custom_call" | custom-call | tf_op jit(solution)/shard_map/pallas_call | solution.py:589
  36.2 12.1 %all_to_all.26.own_ref = f32[8,40,128]{2,1,0:T(8,128)S(1)} all-to-all(f32[8,40,128]{2,1,0:T(8,128)S(1)} %get-tuple-element.59), channel_id=1, replica_groups={{128,160,192,224,0,32,64,96},{136,168,200,232,8,40,72,104},{144,176,208..., dimensions={0} | all-to-all | bytes 327680 | tf_op jit(solution)/shard_map/all_to_all | solution.py:624
  48.3 1.0 collective-permute-start.3
  49.3 1.0 collective-permute-done.3.other_ref
  50.4 4.9 %shard_map.114 = (f32[8,520,128]{2,1,0:T(8,128)S(1)}, f32[8,64,128]{2,1,0:T(8,128)S(1)}, f32[8,128]{1,0:T(8,128)S(1)}, f32[72,128]{1,0:T(8,128)S(1)}, f32[8,40,128]{2,1,0:T(8,128)S(1)}) custom-call(s32[4]{0:T(128)S(1)} %pad_add_fusion.where_ref, f32[8,40,128]{2,1,0:T(8,128)S(1)} %all_to_all.26.own_ref, f32[8,40,128]{2,1,0:T(8,128)S(1)} %collective-permute-done.3.other_ref, ...), custom_call_target="tpu_custom_call" | custom-call | tf_op jit(solution)/shard_map/pallas_call | solution.py:589
  55.3 12.2 %all_to_all.27.own_ref = f32[8,40,128]{2,1,0:T(8,128)S(1)} all-to-all(f32[8,40,128]{2,1,0:T(8,128)S(1)} %get-tuple-element.64), channel_id=1, replica_groups={{128,160,192,224,0,32,64,96},{136,168,200,232,8,40,72,104},{144,176,208..., dimensions={0} | all-to-all | bytes 327680 | tf_op jit(solution)/shard_map/all_to_all | solution.py:624
  67.5 0.9 collective-permute-start.4
  68.4 1.0 collective-permute-done.4.other_ref
  69.4 5.3 %shard_map.115 = (f32[64,128]{1,0:T(8,128)S(1)}, f32[6,64,128]{2,1,0:T(8,128)S(1)}, f32[8,64,128]{2,1,0:T(8,128)S(1)}, f32[8,128]{1,0:T(8,128)S(1)}, f32[72,128]{1,0:T(8,128)S(1)}, /*index=5*/f32[8,40,128]{2,1,0:T(8,128)S(1)}) custom-call(s32[4]{0:T(128)S(1)} %pad_add_fusion.where_ref, f32[8,40,128]{2,1,0:T(8,128)S(1)} %all_to_all.27.own_ref, ...), custom_call_target="tpu_custom_call" | custom-call | tf_op jit(solution)/shard_map/pallas_call | solution.py:589
  74.8 12.2 %all_to_all.28.own_ref = f32[8,40,128]{2,1,0:T(8,128)S(1)} all-to-all(f32[8,40,128]{2,1,0:T(8,128)S(1)} %get-tuple-element.70), channel_id=1, replica_groups={{128,160,192,224,0,32,64,96},{136,168,200,232,8,40,72,104},{144,176,208..., dimensions={0} | all-to-all | bytes 327680 | tf_op jit(solution)/shard_map/all_to_all | solution.py:624
  87.0 0.9 collective-permute-start.5
  87.9 0.0 collective-permute-start.6
  87.9 1.2 collective-permute-done.6.across_ref
  89.1 0.0 collective-permute-done.5.other_ref
  89.1 3.0 %shard_map.116 = (f32[256,128]{1,0:T(8,128)S(1)}, f32[256,128]{1,0:T(8,128)S(1)}, f32[4,32,128]{2,1,0:T(8,128)S(1)}) custom-call(s32[4]{0:T(128)S(1)} %pad_add_fusion.where_ref, f32[8,40,128]{2,1,0:T(8,128)S(1)} %all_to_all.28.own_ref, f32[8,40,128]{2,1,0:T(8,128)S(1)} %collective-permute-done.5.other_ref, f32[6,64,128]{2,1,0:T(8,128)S(1)} %get-tuple-element.71.coef_ref, ...), custom_call_target="tpu_custom_call" | custom-call | tf_op jit(solution)/shard_map/pallas_call | solution.py:589
  92.1 0.3 collective-permute-start.7
  92.4 1.1 collective-permute-done.7
  93.6 1.6 %collective-permute-start.8 = (f32[96,128]{1,0:T(8,128)S(1)}, f32[96,128]{1,0:T(8,128)S(1)}, u32[]{:S(2)}, u32[]{:S(2)}) collective-permute-start(f32[96,128]{1,0:T(8,128)S(1)} %pad_maximum_fusion.1), channel_id=1, source_target_pairs={{0,16},{8,24},{16,0},{24,8},{32,48},{40,56},{48,32},{56,40},{64,80... | collective-permute-start | bytes 147464 | tf_op jit(solution)/shard_map/ppermute | solution.py:682
  95.2 1.1 collective-permute-start.9
  96.3 1.6 %collective-permute-start.10 = (f32[96,128]{1,0:T(8,128)S(1)}, f32[96,128]{1,0:T(8,128)S(1)}, u32[]{:S(2)}, u32[]{:S(2)}) collective-permute-start(f32[96,128]{1,0:T(8,128)S(1)} %pad_maximum_fusion.3), channel_id=1, source_target_pairs={{0,24},{8,0},{16,8},{24,16},{32,56},{40,32},{48,40},{56,48},{64,88... | collective-permute-start | bytes 147464 | tf_op jit(solution)/shard_map/ppermute | solution.py:682
  97.9 0.2 collective-permute-done.8.two_ref
  98.1 1.5 %collective-permute-done.9.one_ref = f32[96,128]{1,0:T(8,128)S(1)} collective-permute-done((f32[96,128]{1,0:T(8,128)S(1)}, f32[96,128]{1,0:T(8,128)S(1)}, u32[]{:S(2)}, u32[]{:S(2)}) %collective-permute-start.9) | collective-permute-done | bytes 49184 | tf_op jit(solution)/shard_map/ppermute | solution.py:682
  99.6 0.0 collective-permute-done.10.three_ref
  99.6 3.0 %collective-permute-start.13 = (f32[64,128]{1,0:T(8,128)S(1)}, f32[64,128]{1,0:T(8,128)S(1)}, u32[]{:S(2)}, u32[]{:S(2)}) collective-permute-start(f32[64,128]{1,0:T(8,128)S(1)} %fusion), channel_id=1, source_target_pairs={{0,4},{1,5},{2,6},{3,7},{4,0},{5,1},{6,2},{7,3},{8,12},{9,13},{10,... | collective-permute-start | bytes 98312 | tf_op jit(solution)/shard_map/ppermute | solution.py:682
  102.6 0.4 collective-permute-start.12
  103.0 2.3 %collective-permute-start.11 = (f32[64,128]{1,0:T(8,128)S(1)}, f32[64,128]{1,0:T(8,128)S(1)}, u32[]{:S(2)}, u32[]{:S(2)}) collective-permute-start(f32[64,128]{1,0:T(8,128)S(1)} %fusion), channel_id=1, source_target_pairs={{0,6},{1,7},{2,0},{3,1},{4,2},{5,3},{6,4},{7,5},{8,14},{9,15},{10,... | collective-permute-start | bytes 98312 | tf_op jit(solution)/shard_map/ppermute | solution.py:682
  105.3 0.0 collective-permute-done.13
  105.3 1.3 collective-permute-done.12
  106.6 0.0 collective-permute-done.11
  106.6 11.7 %all_to_all.29 = f32[8,64,128]{2,1,0:T(8,128)S(1)} all-to-all(f32[8,64,128]{2,1,0:T(8,128)S(1)} %broadcast_in_dim.10), channel_id=1, replica_groups={{128,160,192,224,0,32,64,96},{136,168,200,232,8,40,72,104},{144,176,208..., dimensions={0} | all-to-all | bytes 524288 | tf_op jit(solution)/shard_map/all_to_all | solution.py:690
  118.4 4.2 %collective-permute-start.14 = (f32[64,128]{1,0:T(8,128)S(1)}, f32[64,128]{1,0:T(8,128)S(1)}, u32[]{:S(2)}, u32[]{:S(2)}) collective-permute-start(f32[64,128]{1,0:T(8,128)S(1)} %reduce_sum.9), channel_id=1, source_target_pairs={{0,1},{1,0},{2,3},{3,2},{4,5},{5,4},{6,7},{7,6},{8,9},{9,8},{10,11... | collective-permute-start | bytes 98312 | tf_op jit(solution)/shard_map/ppermute | solution.py:691
  122.6 0.9 collective-permute-done.14
  123.5 1.1 collective-permute-start.17
  124.6 2.4 %collective-permute-start.16 = (f32[2,64,128]{2,1,0:T(8,128)S(1)}, f32[2,64,128]{2,1,0:T(8,128)S(1)}, u32[]{:S(2)}, u32[]{:S(2)}) collective-permute-start(f32[2,64,128]{2,1,0:T(8,128)S(1)} %pad_maximum_fusion.both_ref), channel_id=1, source_target_pairs={{0,8},{8,16},{16,24},{24,0},{32,40},{40,48},{48,56},{56,32},{64,72... | collective-permute-start | bytes 196616 | tf_op jit(solution)/shard_map/ppermute | solution.py:682
  127.0 0.3 collective-permute-start.15
  127.3 1.3 %shard_map.117 = f32[64,2,64]{2,1,0:T(2,128)} custom-call(s32[4]{0:T(128)S(1)} %pad_add_fusion.where_ref, f32[4,32,128]{2,1,0:T(8,128)S(1)} %get-tuple-element.78.home_ref, f32[96,128]{1,0:T(8,128)S(1)} %collective-permute-done.8.two_ref, f32[96,128]{1,0:T(8,128)S(1)} %collective-permute-done.9.one_ref, f32[96,128]{1,0:T(8,128)S(1)} %collective-permute-done.10.three_ref), custom_call_target="tpu_custom_call" | custom-call | tf_op jit(solution)/shard_map/pallas_call | solution.py:589
  128.6 0.0 collective-permute-done.17.two_ref
  128.6 1.6 %collective-permute-done.16.one_ref = f32[2,64,128]{2,1,0:T(8,128)S(1)} collective-permute-done((f32[2,64,128]{2,1,0:T(8,128)S(1)}, f32[2,64,128]{2,1,0:T(8,128)S(1)}, u32[]{:S(2)}, u32[]{:S(2)}) %collective-permute-start.16) | collective-permute-done | bytes 65568 | tf_op jit(solution)/shard_map/ppermute | solution.py:682
  130.2 0.2 collective-permute-done.15.three_ref
  130.4 1.3 shard_map.118
  (12 shorter events, 0.1 us)
Async XLA Ops:
  2.4 8.2 %collective-permute-start = (f32[168,128]{1,0:T(8,128)S(1)}, f32[168,128]{1,0:T(8,128)S(1)}, u32[]{:S(2)}, u32[]{:S(2)}) collective-permute-start(f32[168,128]{1,0:T(8,128)S(1)} %get-tuple-element.45), channel_id=1, source_target_pairs={{0,0},{1,16},{2,2},{3,18},{4,4},{5,20},{6,6},{7,22},{8,8},{9,24},{... | collective-permute-start | bytes 258056 | tf_op jit(solution)/shard_map/ppermute | solution.py:634
  8.4 5.2 %collective-permute-start.1 = (f32[168,128]{1,0:T(8,128)S(1)}, f32[168,128]{1,0:T(8,128)S(1)}, u32[]{:S(2)}, u32[]{:S(2)}) collective-permute-start(f32[168,128]{1,0:T(8,128)S(1)} %get-tuple-element.46), channel_id=1, source_target_pairs={{0,8},{1,24},{2,10},{3,26},{4,12},{5,28},{6,14},{7,30},{8,0},{9,16... | collective-permute-start | bytes 258056 | tf_op jit(solution)/shard_map/ppermute | solution.py:635
  29.9 1.4 %collective-permute-start.2 = (f32[8,40,128]{2,1,0:T(8,128)S(1)}, f32[8,40,128]{2,1,0:T(8,128)S(1)}, u32[]{:S(2)}, u32[]{:S(2)}) collective-permute-start(f32[8,40,128]{2,1,0:T(8,128)S(1)} %all_to_all.25.own_ref), channel_id=1, source_target_pairs={{0,1},{1,0},{2,3},{3,2},{4,5},{5,4},{6,7},{7,6},{8,9},{9,8},{10,11... | collective-permute-start | bytes 491528 | tf_op jit(solution)/shard_map/ppermute | solution.py:625
  48.3 2.0 %collective-permute-start.3 = (f32[8,40,128]{2,1,0:T(8,128)S(1)}, f32[8,40,128]{2,1,0:T(8,128)S(1)}, u32[]{:S(2)}, u32[]{:S(2)}) collective-permute-start(f32[8,40,128]{2,1,0:T(8,128)S(1)} %all_to_all.26.own_ref), channel_id=1, source_target_pairs={{0,1},{1,0},{2,3},{3,2},{4,5},{5,4},{6,7},{7,6},{8,9},{9,8},{10,11... | collective-permute-start | bytes 491528 | tf_op jit(solution)/shard_map/ppermute | solution.py:625
  67.5 1.9 %collective-permute-start.4 = (f32[8,40,128]{2,1,0:T(8,128)S(1)}, f32[8,40,128]{2,1,0:T(8,128)S(1)}, u32[]{:S(2)}, u32[]{:S(2)}) collective-permute-start(f32[8,40,128]{2,1,0:T(8,128)S(1)} %all_to_all.27.own_ref), channel_id=1, source_target_pairs={{0,1},{1,0},{2,3},{3,2},{4,5},{5,4},{6,7},{7,6},{8,9},{9,8},{10,11... | collective-permute-start | bytes 491528 | tf_op jit(solution)/shard_map/ppermute | solution.py:625
  87.0 2.1 %collective-permute-start.5 = (f32[8,40,128]{2,1,0:T(8,128)S(1)}, f32[8,40,128]{2,1,0:T(8,128)S(1)}, u32[]{:S(2)}, u32[]{:S(2)}) collective-permute-start(f32[8,40,128]{2,1,0:T(8,128)S(1)} %all_to_all.28.own_ref), channel_id=1, source_target_pairs={{0,1},{1,0},{2,3},{3,2},{4,5},{5,4},{6,7},{7,6},{8,9},{9,8},{10,11... | collective-permute-start | bytes 491528 | tf_op jit(solution)/shard_map/ppermute | solution.py:625
  87.9 1.2 collective-permute-start.6
  92.1 1.4 %collective-permute-start.7 = (f32[256,128]{1,0:T(8,128)S(1)}, f32[256,128]{1,0:T(8,128)S(1)}, u32[]{:S(2)}, u32[]{:S(2)}) collective-permute-start(f32[256,128]{1,0:T(8,128)S(1)} %get-tuple-element.80), channel_id=1, source_target_pairs={{0,1},{1,0},{2,3},{3,2},{4,5},{5,4},{6,7},{7,6},{8,9},{9,8},{10,11... | collective-permute-start | bytes 393224 | tf_op jit(solution)/shard_map/ppermute | solution.py:685
  93.6 4.5 %collective-permute-start.8 = (f32[96,128]{1,0:T(8,128)S(1)}, f32[96,128]{1,0:T(8,128)S(1)}, u32[]{:S(2)}, u32[]{:S(2)}) collective-permute-start(f32[96,128]{1,0:T(8,128)S(1)} %pad_maximum_fusion.1), channel_id=1, source_target_pairs={{0,16},{8,24},{16,0},{24,8},{32,48},{40,56},{48,32},{56,40},{64,80... | collective-permute-start | bytes 147464 | tf_op jit(solution)/shard_map/ppermute | solution.py:682
  95.2 4.4 %collective-permute-start.9 = (f32[96,128]{1,0:T(8,128)S(1)}, f32[96,128]{1,0:T(8,128)S(1)}, u32[]{:S(2)}, u32[]{:S(2)}) collective-permute-start(f32[96,128]{1,0:T(8,128)S(1)} %pad_maximum_fusion.2), channel_id=1, source_target_pairs={{0,8},{8,16},{16,24},{24,0},{32,40},{40,48},{48,56},{56,32},{64,72... | collective-permute-start | bytes 147464 | tf_op jit(solution)/shard_map/ppermute | solution.py:682
  96.3 3.3 %collective-permute-start.10 = (f32[96,128]{1,0:T(8,128)S(1)}, f32[96,128]{1,0:T(8,128)S(1)}, u32[]{:S(2)}, u32[]{:S(2)}) collective-permute-start(f32[96,128]{1,0:T(8,128)S(1)} %pad_maximum_fusion.3), channel_id=1, source_target_pairs={{0,24},{8,0},{16,8},{24,16},{32,56},{40,32},{48,40},{56,48},{64,88... | collective-permute-start | bytes 147464 | tf_op jit(solution)/shard_map/ppermute | solution.py:682
  99.6 5.7 %collective-permute-start.13 = (f32[64,128]{1,0:T(8,128)S(1)}, f32[64,128]{1,0:T(8,128)S(1)}, u32[]{:S(2)}, u32[]{:S(2)}) collective-permute-start(f32[64,128]{1,0:T(8,128)S(1)} %fusion), channel_id=1, source_target_pairs={{0,4},{1,5},{2,6},{3,7},{4,0},{5,1},{6,2},{7,3},{8,12},{9,13},{10,... | collective-permute-start | bytes 98312 | tf_op jit(solution)/shard_map/ppermute | solution.py:682
  102.6 4.0 %collective-permute-start.12 = (f32[64,128]{1,0:T(8,128)S(1)}, f32[64,128]{1,0:T(8,128)S(1)}, u32[]{:S(2)}, u32[]{:S(2)}) collective-permute-start(f32[64,128]{1,0:T(8,128)S(1)} %fusion), channel_id=1, source_target_pairs={{0,2},{1,3},{2,4},{3,5},{4,6},{5,7},{6,0},{7,1},{8,10},{9,11},{10,... | collective-permute-start | bytes 98312 | tf_op jit(solution)/shard_map/ppermute | solution.py:682
  103.0 3.6 %collective-permute-start.11 = (f32[64,128]{1,0:T(8,128)S(1)}, f32[64,128]{1,0:T(8,128)S(1)}, u32[]{:S(2)}, u32[]{:S(2)}) collective-permute-start(f32[64,128]{1,0:T(8,128)S(1)} %fusion), channel_id=1, source_target_pairs={{0,6},{1,7},{2,0},{3,1},{4,2},{5,3},{6,4},{7,5},{8,14},{9,15},{10,... | collective-permute-start | bytes 98312 | tf_op jit(solution)/shard_map/ppermute | solution.py:682
  118.4 5.1 %collective-permute-start.14 = (f32[64,128]{1,0:T(8,128)S(1)}, f32[64,128]{1,0:T(8,128)S(1)}, u32[]{:S(2)}, u32[]{:S(2)}) collective-permute-start(f32[64,128]{1,0:T(8,128)S(1)} %reduce_sum.9), channel_id=1, source_target_pairs={{0,1},{1,0},{2,3},{3,2},{4,5},{5,4},{6,7},{7,6},{8,9},{9,8},{10,11... | collective-permute-start | bytes 98312 | tf_op jit(solution)/shard_map/ppermute | solution.py:691
  123.5 5.2 %collective-permute-start.17 = (f32[2,64,128]{2,1,0:T(8,128)S(1)}, f32[2,64,128]{2,1,0:T(8,128)S(1)}, u32[]{:S(2)}, u32[]{:S(2)}) collective-permute-start(f32[2,64,128]{2,1,0:T(8,128)S(1)} %pad_maximum_fusion.both_ref), channel_id=1, source_target_pairs={{0,16},{8,24},{16,0},{24,8},{32,48},{40,56},{48,32},{56,40},{64,80... | collective-permute-start | bytes 196616 | tf_op jit(solution)/shard_map/ppermute | solution.py:682
  124.6 5.6 %collective-permute-start.16 = (f32[2,64,128]{2,1,0:T(8,128)S(1)}, f32[2,64,128]{2,1,0:T(8,128)S(1)}, u32[]{:S(2)}, u32[]{:S(2)}) collective-permute-start(f32[2,64,128]{2,1,0:T(8,128)S(1)} %pad_maximum_fusion.both_ref), channel_id=1, source_target_pairs={{0,8},{8,16},{16,24},{24,0},{32,40},{40,48},{48,56},{56,32},{64,72... | collective-permute-start | bytes 196616 | tf_op jit(solution)/shard_map/ppermute | solution.py:682
  127.0 3.5 %collective-permute-start.15 = (f32[2,64,128]{2,1,0:T(8,128)S(1)}, f32[2,64,128]{2,1,0:T(8,128)S(1)}, u32[]{:S(2)}, u32[]{:S(2)}) collective-permute-start(f32[2,64,128]{2,1,0:T(8,128)S(1)} %pad_maximum_fusion.both_ref), channel_id=1, source_target_pairs={{0,24},{8,0},{16,8},{24,16},{32,56},{40,32},{48,40},{56,48},{64,88... | collective-permute-start | bytes 196616 | tf_op jit(solution)/shard_map/ppermute | solution.py:682

commit v6 on v5

--- a/solution.py
+++ b/solution.py
@@ -537,22 +537,22 @@
     full_ref[480:512, :] = jnp.concatenate([tail, jnp.zeros((30, LANES), F32)], axis=0)
     core, x = where_ref[1], where_ref[3]
     for d in range(4):
-        part = lax.rem(x + d, 4)
+        part = lax.bitwise_xor(x, d)
         rows = slice(d * 64, (d + 1) * 64)
         keep_ref[rows, :] = full_ref[pl.ds(pl.multiple_of((core * 4 + part) * 64, 64), 64), :]
         give_ref[rows, :] = full_ref[pl.ds(pl.multiple_of(((1 - core) * 4 + part) * 64, 64), 64), :]
     for d in range(4):
-        part = lax.rem(x + d, 4)
+        part = lax.bitwise_xor(x, d)
         whole = jnp.where(part // 2 == core, states_ref[...], across_ref[...])
         block = jnp.where(lax.rem(part, 2) == 0, whole, swap_halves(whole))
         home_ref[d] = jnp.where(lane_low((32, LANES)), block[:32], swap_halves(block[32:]))
 
 
-def home_kernel(where_ref, home_ref, two_ref, one_ref, three_ref, traj_ref):
+def home_kernel(where_ref, home_ref, two_ref, three_ref, one_ref, traj_ref):
     core, x = where_ref[1], where_ref[3]
     blocks = [home_ref[0]] + [ref[64:96, :] for ref in (one_ref, two_ref, three_ref)]
     for e in range(2):
-        where = lax.rem(x + 4 - 2 * core - e, 4)
+        where = lax.bitwise_xor(x, 2 * core + e)
         block = blocks[0]
         for d in range(1, 4):
             block = jnp.where(where == d, blocks[d], block)
@@ -561,12 +561,12 @@
 
 
 def unpack_kernel(
-    where_ref, three_ref, one_ref, two_ref, both_ref, in_ref, rec_ref, scale_ref, bias_ref, full_ref
+    where_ref, one_ref, three_ref, two_ref, both_ref, in_ref, rec_ref, scale_ref, bias_ref, full_ref
 ):
     x = where_ref[3]
     pieces = (both_ref, one_ref, two_ref, three_ref)
     for d in range(4):
-        part = lax.rem(x + 4 - d, 4)
+        part = lax.bitwise_xor(x, d)
         for core in range(2):
             full_ref[pl.ds(pl.multiple_of((core * 4 + part) * 64, 64), 64), :] = pieces[d][core]
     in_ref[:, :LANES] = full_ref[0:192, :]
@@ -612,11 +612,11 @@
         ]
         there.append(pairs)
     step_x = {
-        d: [(z * width + x, z * width + (x + d) % width) for z in range(planes) for x in range(width)]
+        d: [(z * width + x, z * width + (x ^ d)) for z in range(planes) for x in range(width)]
         for d in range(1, width)
     }
     along_z = [[(z + planes // 2) % planes * width + x for z in range(planes)] for x in range(width)]
-    step_y = {d: [(b, (b + 2 * d) % (2 * ys)) for b in range(2 * ys)] for d in range(1, ys)}
+    step_y = {d: [(b, b ^ (2 * d)) for b in range(2 * ys)] for d in range(1, ys)}
     cores = [(b, b ^ 1) for b in range(2 * ys)]
     axes = ("seq", "batch")
 
@@ -683,15 +683,15 @@
         return [got[d] for d in order]
 
     parts = (keep + lax.ppermute(give, "batch", cores)).reshape(width, -1, LANES)
-    early = around(lambda d: jnp.concatenate([parts[d], home[d]], axis=0), "seq", step_x, (2, 1, 3))
+    early = around(lambda d: jnp.concatenate([parts[d], home[d]], axis=0), "seq", step_x, (2, 3, 1))
     part = parts[0] + sum(piece[:64] for piece in early)
-    part = part + sum(around(lambda d: part, "batch", step_y, (3, 1, 2)))
+    part = part + sum(around(lambda d: part, "batch", step_y, (1, 3, 2)))
     wide = jnp.broadcast_to(part[None], (planes,) + part.shape)
     part = lax.all_to_all(wide, "seq", 0, 0, axis_index_groups=along_z, tiled=True).sum(0)
     other = lax.ppermute(part, "batch", cores)
     first = core == 0
     both = jnp.stack([jnp.where(first, part, other), jnp.where(first, other, part)])
-    rest = around(lambda d: both, "seq", step_x, (3, 1, 2))
+    rest = around(lambda d: both, "seq", step_x, (1, 3, 2))
     (traj,) = call(home_kernel, [((H, 2, 64), F32)], "svvvv", where, home, *early)
     grad_in, grad_rec, grad_scale, grad_other = call(
         unpack_kernel,

time: 133 us -> 131 us (0.985)
  starting transfers between devices: 27.8 us -> 23.4 us
  waiting for transfers between devices: 14.7 us -> 18.4 us
    ppermute x9, starting transfers between devices: 13.8 us -> 9.3 us  [around(): got = {d: lax.ppermute(value_of(d), axis, steps[d]) for d in order}]
    ppermute x9, waiting for transfers between devices: 4.79 us -> 8.45 us  [around(): got = {d: lax.ppermute(value_of(d), axis, steps[d]) for d in order}]
  transfers between devices with their start and end apart: 18 -> 18, of which waited for: 13 -> 14; matrix products, arithmetic and copies ran while one was open for 0% -> 0% of each run, Pallas kernels for 2% -> 2%
where the time goes in v6:
time: 131 us
  blocking collectives  61.1 us (47%)
  Pallas kernels  27.1 us (21%)
  starting transfers between devices  23.4 us (18%)
  waiting for transfers between devices  18.4 us (14%)
    all_to_all x4, blocking collectives, exchange(): lax.all_to_all(value, 'seq', 0, 0, axis_index_groups=along_z, tiled=True)  49.4 us
    pallas_call x9, Pallas kernels, call(): pl.pallas_call(kernel, out_shape=[jax.ShapeDtypeStruct(*out) for out in o...  27.1 us
    all_to_all x1, blocking collectives, local(): lax.all_to_all(wide, 'seq', 0, 0, axis_index_groups=along_z, tiled=True)  11.7 us
    ppermute x9, starting transfers between devices, around(): got = {d: lax.ppermute(value_of(d), axis, steps[d]) for d in order}  9.3 us
    ppermute x9, waiting for transfers between devices, around(): got = {d: lax.ppermute(value_of(d), axis, steps[d]) for d in order}  8.45 us
    ppermute x1, starting transfers between devices, local(): one = lax.ppermute(one, axes, there[0])  6.04 us
    ppermute x1, starting transfers between devices, local(): other = lax.ppermute(part, 'batch', cores)  4.32 us
    ppermute x4, waiting for transfers between devices, exchange(): return (own, lax.ppermute(own, 'batch', cores))  3.45 us
  transfers between devices with their start and end apart: 18, of which 14 were waited for; matrix products, arithmetic and copies ran while one was open for 0% of the time, Pallas kernels for 2%

profile of v6, /device:TPU:1, one launch (start us, length us, event | category | flops | bytes accessed | tf_op | source)
XLA Modules:
  0.0 131.0 jit_solution(4049353856117684550)
XLA Ops:
  0.7 0.1 pad_add_fusion.where_ref
  0.8 1.6 %shard_map.110 = (f32[168,128]{1,0:T(8,128)S(1)}, f32[168,128]{1,0:T(8,128)S(1)}) custom-call(s32[4]{0:T(128)S(1)} %pad_add_fusion.where_ref, bf16[2,64,256]{2,1,0:T(8,128)(2,1)} %x_hbm.1, f32[64,2,64]{2,1,0:T(2,128)} %cot_hbm.1, f32[2,64]{1,0:T(2,128)} %bitcast.20), custom_call_target="tpu_custom_call" | custom-call | tf_op jit(solution)/shard_map/pallas_call | solution.py:589
  2.4 6.0 %collective-permute-start = (f32[168,128]{1,0:T(8,128)S(1)}, f32[168,128]{1,0:T(8,128)S(1)}, u32[]{:S(2)}, u32[]{:S(2)}) collective-permute-start(f32[168,128]{1,0:T(8,128)S(1)} %get-tuple-element.45), channel_id=1, source_target_pairs={{0,0},{1,16},{2,2},{3,18},{4,4},{5,20},{6,6},{7,22},{8,8},{9,24},{... | collective-permute-start | bytes 258056 | tf_op jit(solution)/shard_map/ppermute | solution.py:634
  8.4 0.7 collective-permute-start.1
  9.1 1.2 shard_map.111
  10.3 0.3 collective-permute-done.a_ref
  10.6 3.1 %collective-permute-done.1.b_ref = f32[168,128]{1,0:T(8,128)S(1)} collective-permute-done((f32[168,128]{1,0:T(8,128)S(1)}, f32[168,128]{1,0:T(8,128)S(1)}, u32[]{:S(2)}, u32[]{:S(2)}) %collective-permute-start.1) | collective-permute-done | bytes 86048 | tf_op jit(solution)/shard_map/ppermute | solution.py:635
  13.6 3.4 %shard_map.112 = (f32[3,64,128]{2,1,0:T(8,128)S(1)}, bf16[128,256]{1,0:T(8,128)(2,1)S(1)}, f32[64,128]{1,0:T(8,128)S(1)}, f32[8,128]{1,0:T(8,128)S(1)}, f32[8,52...) custom-call(s32[4]{0:T(128)S(1)} %pad_add_fusion.where_ref, ...), custom_call_target="tpu_custom_call" | custom-call | tf_op jit(solution)/shard_map/pallas_call | solution.py:589
  17.1 12.8 %all_to_all.25.own_ref = f32[8,40,128]{2,1,0:T(8,128)S(1)} all-to-all(f32[8,40,128]{2,1,0:T(8,128)S(1)} %get-tuple-element.52), channel_id=1, replica_groups={{128,160,192,224,0,32,64,96},{136,168,200,232,8,40,72,104},{144,176,208..., dimensions={0} | all-to-all | bytes 327680 | tf_op jit(solution)/shard_map/all_to_all | solution.py:624
  29.9 0.0 collective-permute-start.2
  29.9 1.4 %collective-permute-done.2.other_ref = f32[8,40,128]{2,1,0:T(8,128)S(1)} collective-permute-done((f32[8,40,128]{2,1,0:T(8,128)S(1)}, f32[8,40,128]{2,1,0:T(8,128)S(1)}, u32[]{:S(2)}, u32[]{:S(2)}) %collective-permute-start.2) | collective-permute-done | bytes 163872 | tf_op jit(solution)/shard_map/ppermute | solution.py:625
  31.3 4.9 %shard_map.113 = (f32[8,520,128]{2,1,0:T(8,128)S(1)}, f32[8,64,128]{2,1,0:T(8,128)S(1)}, f32[8,128]{1,0:T(8,128)S(1)}, f32[72,128]{1,0:T(8,128)S(1)}, f32[8,40,128]{2,1,0:T(8,128)S(1)}) custom-call(s32[4]{0:T(128)S(1)} %pad_add_fusion.where_ref, f32[8,40,128]{2,1,0:T(8,128)S(1)} %all_to_all.25.own_ref, f32[8,40,128]{2,1,0:T(8,128)S(1)} %collective-permute-done.2.other_ref, ...), custom_call_target="tpu_custom_call" | custom-call | tf_op jit(solution)/shard_map/pallas_call | solution.py:589
  36.2 12.1 %all_to_all.26.own_ref = f32[8,40,128]{2,1,0:T(8,128)S(1)} all-to-all(f32[8,40,128]{2,1,0:T(8,128)S(1)} %get-tuple-element.59), channel_id=1, replica_groups={{128,160,192,224,0,32,64,96},{136,168,200,232,8,40,72,104},{144,176,208..., dimensions={0} | all-to-all | bytes 327680 | tf_op jit(solution)/shard_map/all_to_all | solution.py:624
  48.3 1.0 collective-permute-start.3
  49.3 1.0 collective-permute-done.3.other_ref
  50.4 4.9 %shard_map.114 = (f32[8,520,128]{2,1,0:T(8,128)S(1)}, f32[8,64,128]{2,1,0:T(8,128)S(1)}, f32[8,128]{1,0:T(8,128)S(1)}, f32[72,128]{1,0:T(8,128)S(1)}, f32[8,40,128]{2,1,0:T(8,128)S(1)}) custom-call(s32[4]{0:T(128)S(1)} %pad_add_fusion.where_ref, f32[8,40,128]{2,1,0:T(8,128)S(1)} %all_to_all.26.own_ref, f32[8,40,128]{2,1,0:T(8,128)S(1)} %collective-permute-done.3.other_ref, ...), custom_call_target="tpu_custom_call" | custom-call | tf_op jit(solution)/shard_map/pallas_call | solution.py:589
  55.3 12.2 %all_to_all.27.own_ref = f32[8,40,128]{2,1,0:T(8,128)S(1)} all-to-all(f32[8,40,128]{2,1,0:T(8,128)S(1)} %get-tuple-element.64), channel_id=1, replica_groups={{128,160,192,224,0,32,64,96},{136,168,200,232,8,40,72,104},{144,176,208..., dimensions={0} | all-to-all | bytes 327680 | tf_op jit(solution)/shard_map/all_to_all | solution.py:624
  67.5 0.9 collective-permute-start.4
  68.4 1.0 collective-permute-done.4.other_ref
  69.4 5.3 %shard_map.115 = (f32[64,128]{1,0:T(8,128)S(1)}, f32[6,64,128]{2,1,0:T(8,128)S(1)}, f32[8,64,128]{2,1,0:T(8,128)S(1)}, f32[8,128]{1,0:T(8,128)S(1)}, f32[72,128]{1,0:T(8,128)S(1)}, /*index=5*/f32[8,40,128]{2,1,0:T(8,128)S(1)}) custom-call(s32[4]{0:T(128)S(1)} %pad_add_fusion.where_ref, f32[8,40,128]{2,1,0:T(8,128)S(1)} %all_to_all.27.own_ref, ...), custom_call_target="tpu_custom_call" | custom-call | tf_op jit(solution)/shard_map/pallas_call | solution.py:589
  74.8 12.2 %all_to_all.28.own_ref = f32[8,40,128]{2,1,0:T(8,128)S(1)} all-to-all(f32[8,40,128]{2,1,0:T(8,128)S(1)} %get-tuple-element.70), channel_id=1, replica_groups={{128,160,192,224,0,32,64,96},{136,168,200,232,8,40,72,104},{144,176,208..., dimensions={0} | all-to-all | bytes 327680 | tf_op jit(solution)/shard_map/all_to_all | solution.py:624
  87.0 0.9 collective-permute-start.5
  87.9 0.0 collective-permute-start.6
  87.9 1.2 collective-permute-done.6.across_ref
  89.1 0.0 collective-permute-done.5.other_ref
  89.1 3.0 %shard_map.116 = (f32[256,128]{1,0:T(8,128)S(1)}, f32[256,128]{1,0:T(8,128)S(1)}, f32[4,32,128]{2,1,0:T(8,128)S(1)}) custom-call(s32[4]{0:T(128)S(1)} %pad_add_fusion.where_ref, f32[8,40,128]{2,1,0:T(8,128)S(1)} %all_to_all.28.own_ref, f32[8,40,128]{2,1,0:T(8,128)S(1)} %collective-permute-done.5.other_ref, f32[6,64,128]{2,1,0:T(8,128)S(1)} %get-tuple-element.71.coef_ref, ...), custom_call_target="tpu_custom_call" | custom-call | tf_op jit(solution)/shard_map/pallas_call | solution.py:589
  92.1 0.3 collective-permute-start.7
  92.4 1.1 collective-permute-done.7
  93.6 1.6 %collective-permute-start.8 = (f32[96,128]{1,0:T(8,128)S(1)}, f32[96,128]{1,0:T(8,128)S(1)}, u32[]{:S(2)}, u32[]{:S(2)}) collective-permute-start(f32[96,128]{1,0:T(8,128)S(1)} %pad_maximum_fusion.1), channel_id=1, source_target_pairs={{0,16},{8,24},{16,0},{24,8},{32,48},{40,56},{48,32},{56,40},{64,80... | collective-permute-start | bytes 147464 | tf_op jit(solution)/shard_map/ppermute | solution.py:682
  95.2 0.6 collective-permute-start.9
  95.8 0.6 collective-permute-start.10
  96.4 1.7 %collective-permute-done.8.two_ref = f32[96,128]{1,0:T(8,128)S(1)} collective-permute-done((f32[96,128]{1,0:T(8,128)S(1)}, f32[96,128]{1,0:T(8,128)S(1)}, u32[]{:S(2)}, u32[]{:S(2)}) %collective-permute-start.8) | collective-permute-done | bytes 49184 | tf_op jit(solution)/shard_map/ppermute | solution.py:682
  98.1 1.3 collective-permute-done.9.three_ref
  99.3 0.0 collective-permute-done.10.one_ref
  99.4 3.0 %collective-permute-start.13 = (f32[64,128]{1,0:T(8,128)S(1)}, f32[64,128]{1,0:T(8,128)S(1)}, u32[]{:S(2)}, u32[]{:S(2)}) collective-permute-start(f32[64,128]{1,0:T(8,128)S(1)} %fusion), channel_id=1, source_target_pairs={{0,4},{1,5},{2,6},{3,7},{4,0},{5,1},{6,2},{7,3},{8,12},{9,13},{10,... | collective-permute-start | bytes 98312 | tf_op jit(solution)/shard_map/ppermute | solution.py:682
  102.4 0.8 collective-permute-start.12
  103.1 0.0 collective-permute-start.11
  103.1 0.6 collective-permute-done.13
  103.7 2.6 %collective-permute-done.12 = f32[64,128]{1,0:T(8,128)S(1)} collective-permute-done((f32[64,128]{1,0:T(8,128)S(1)}, f32[64,128]{1,0:T(8,128)S(1)}, u32[]{:S(2)}, u32[]{:S(2)}) %collective-permute-start.12) | collective-permute-done | bytes 32800 | tf_op jit(solution)/shard_map/ppermute | solution.py:682
  106.3 0.0 collective-permute-done.11
  106.4 11.7 %all_to_all.29 = f32[8,64,128]{2,1,0:T(8,128)S(1)} all-to-all(f32[8,64,128]{2,1,0:T(8,128)S(1)} %broadcast_in_dim.10), channel_id=1, replica_groups={{128,160,192,224,0,32,64,96},{136,168,200,232,8,40,72,104},{144,176,208..., dimensions={0} | all-to-all | bytes 524288 | tf_op jit(solution)/shard_map/all_to_all | solution.py:690
  118.1 4.3 %collective-permute-start.14 = (f32[64,128]{1,0:T(8,128)S(1)}, f32[64,128]{1,0:T(8,128)S(1)}, u32[]{:S(2)}, u32[]{:S(2)}) collective-permute-start(f32[64,128]{1,0:T(8,128)S(1)} %reduce_sum.9), channel_id=1, source_target_pairs={{0,1},{1,0},{2,3},{3,2},{4,5},{5,4},{6,7},{7,6},{8,9},{9,8},{10,11... | collective-permute-start | bytes 98312 | tf_op jit(solution)/shard_map/ppermute | solution.py:691
  122.5 0.9 collective-permute-done.14
  123.3 2.0 %collective-permute-start.17 = (f32[2,64,128]{2,1,0:T(8,128)S(1)}, f32[2,64,128]{2,1,0:T(8,128)S(1)}, u32[]{:S(2)}, u32[]{:S(2)}) collective-permute-start(f32[2,64,128]{2,1,0:T(8,128)S(1)} %pad_maximum_fusion.both_ref), channel_id=1, source_target_pairs={{0,16},{8,24},{16,0},{24,8},{32,48},{40,56},{48,32},{56,40},{64,80... | collective-permute-start | bytes 196616 | tf_op jit(solution)/shard_map/ppermute | solution.py:682
  125.4 0.7 collective-permute-start.16
  126.0 0.1 collective-permute-start.15
  126.1 1.3 %shard_map.117 = f32[64,2,64]{2,1,0:T(2,128)} custom-call(s32[4]{0:T(128)S(1)} %pad_add_fusion.where_ref, f32[4,32,128]{2,1,0:T(8,128)S(1)} %get-tuple-element.78.home_ref, f32[96,128]{1,0:T(8,128)S(1)} %collective-permute-done.8.two_ref, f32[96,128]{1,0:T(8,128)S(1)} %collective-permute-done.9.three_ref, f32[96,128]{1,0:T(8,128)S(1)} %collective-permute-done.10.one_ref), custom_call_target="tpu_custom_call" | custom-call | tf_op jit(solution)/shard_map/pallas_call | solution.py:589
  127.4 0.6 collective-permute-done.17.two_ref
  128.0 1.6 %collective-permute-done.16.three_ref = f32[2,64,128]{2,1,0:T(8,128)S(1)} collective-permute-done((f32[2,64,128]{2,1,0:T(8,128)S(1)}, f32[2,64,128]{2,1,0:T(8,128)S(1)}, u32[]{:S(2)}, u32[]{:S(2)}) %collective-permute-start.16) | collective-permute-done | bytes 65568 | tf_op jit(solution)/shard_map/ppermute | solution.py:682
  129.7 0.0 collective-permute-done.15.one_ref
  129.7 1.3 %shard_map.118 = (f32[192,256]{1,0:T(8,128)}, f32[64,192]{1,0:T(8,128)}, f32[1,64]{1,0:T(1,128)}, f32[3,64]{1,0:T(4,128)}) custom-call(s32[4]{0:T(128)S(1)} %pad_add_fusion.where_ref, f32[2,64,128]{2,1,0:T(8,128)S(1)} %collective-permute-done.15.one_ref, f32[2,64,128]{2,1,0:T(8,128)S(1)} %collective-permute-done.16.three_ref, ...), custom_call_target="tpu_custom_call" | custom-call | tf_op jit(solution)/shard_map/pallas_call | solution.py:589
  (12 shorter events, 0.1 us)
Async XLA Ops:
  2.4 8.2 %collective-permute-start = (f32[168,128]{1,0:T(8,128)S(1)}, f32[168,128]{1,0:T(8,128)S(1)}, u32[]{:S(2)}, u32[]{:S(2)}) collective-permute-start(f32[168,128]{1,0:T(8,128)S(1)} %get-tuple-element.45), channel_id=1, source_target_pairs={{0,0},{1,16},{2,2},{3,18},{4,4},{5,20},{6,6},{7,22},{8,8},{9,24},{... | collective-permute-start | bytes 258056 | tf_op jit(solution)/shard_map/ppermute | solution.py:634
  8.4 5.2 %collective-permute-start.1 = (f32[168,128]{1,0:T(8,128)S(1)}, f32[168,128]{1,0:T(8,128)S(1)}, u32[]{:S(2)}, u32[]{:S(2)}) collective-permute-start(f32[168,128]{1,0:T(8,128)S(1)} %get-tuple-element.46), channel_id=1, source_target_pairs={{0,8},{1,24},{2,10},{3,26},{4,12},{5,28},{6,14},{7,30},{8,0},{9,16... | collective-permute-start | bytes 258056 | tf_op jit(solution)/shard_map/ppermute | solution.py:635
  29.9 1.4 %collective-permute-start.2 = (f32[8,40,128]{2,1,0:T(8,128)S(1)}, f32[8,40,128]{2,1,0:T(8,128)S(1)}, u32[]{:S(2)}, u32[]{:S(2)}) collective-permute-start(f32[8,40,128]{2,1,0:T(8,128)S(1)} %all_to_all.25.own_ref), channel_id=1, source_target_pairs={{0,1},{1,0},{2,3},{3,2},{4,5},{5,4},{6,7},{7,6},{8,9},{9,8},{10,11... | collective-permute-start | bytes 491528 | tf_op jit(solution)/shard_map/ppermute | solution.py:625
  48.3 2.0 %collective-permute-start.3 = (f32[8,40,128]{2,1,0:T(8,128)S(1)}, f32[8,40,128]{2,1,0:T(8,128)S(1)}, u32[]{:S(2)}, u32[]{:S(2)}) collective-permute-start(f32[8,40,128]{2,1,0:T(8,128)S(1)} %all_to_all.26.own_ref), channel_id=1, source_target_pairs={{0,1},{1,0},{2,3},{3,2},{4,5},{5,4},{6,7},{7,6},{8,9},{9,8},{10,11... | collective-permute-start | bytes 491528 | tf_op jit(solution)/shard_map/ppermute | solution.py:625
  67.5 1.9 %collective-permute-start.4 = (f32[8,40,128]{2,1,0:T(8,128)S(1)}, f32[8,40,128]{2,1,0:T(8,128)S(1)}, u32[]{:S(2)}, u32[]{:S(2)}) collective-permute-start(f32[8,40,128]{2,1,0:T(8,128)S(1)} %all_to_all.27.own_ref), channel_id=1, source_target_pairs={{0,1},{1,0},{2,3},{3,2},{4,5},{5,4},{6,7},{7,6},{8,9},{9,8},{10,11... | collective-permute-start | bytes 491528 | tf_op jit(solution)/shard_map/ppermute | solution.py:625
  87.0 2.1 %collective-permute-start.5 = (f32[8,40,128]{2,1,0:T(8,128)S(1)}, f32[8,40,128]{2,1,0:T(8,128)S(1)}, u32[]{:S(2)}, u32[]{:S(2)}) collective-permute-start(f32[8,40,128]{2,1,0:T(8,128)S(1)} %all_to_all.28.own_ref), channel_id=1, source_target_pairs={{0,1},{1,0},{2,3},{3,2},{4,5},{5,4},{6,7},{7,6},{8,9},{9,8},{10,11... | collective-permute-start | bytes 491528 | tf_op jit(solution)/shard_map/ppermute | solution.py:625
  87.9 1.2 collective-permute-start.6
  92.1 1.4 %collective-permute-start.7 = (f32[256,128]{1,0:T(8,128)S(1)}, f32[256,128]{1,0:T(8,128)S(1)}, u32[]{:S(2)}, u32[]{:S(2)}) collective-permute-start(f32[256,128]{1,0:T(8,128)S(1)} %get-tuple-element.80), channel_id=1, source_target_pairs={{0,1},{1,0},{2,3},{3,2},{4,5},{5,4},{6,7},{7,6},{8,9},{9,8},{10,11... | collective-permute-start | bytes 393224 | tf_op jit(solution)/shard_map/ppermute | solution.py:685
  93.6 4.5 %collective-permute-start.8 = (f32[96,128]{1,0:T(8,128)S(1)}, f32[96,128]{1,0:T(8,128)S(1)}, u32[]{:S(2)}, u32[]{:S(2)}) collective-permute-start(f32[96,128]{1,0:T(8,128)S(1)} %pad_maximum_fusion.1), channel_id=1, source_target_pairs={{0,16},{8,24},{16,0},{24,8},{32,48},{40,56},{48,32},{56,40},{64,80... | collective-permute-start | bytes 147464 | tf_op jit(solution)/shard_map/ppermute | solution.py:682
  95.2 4.2 %collective-permute-start.9 = (f32[96,128]{1,0:T(8,128)S(1)}, f32[96,128]{1,0:T(8,128)S(1)}, u32[]{:S(2)}, u32[]{:S(2)}) collective-permute-start(f32[96,128]{1,0:T(8,128)S(1)} %pad_maximum_fusion.2), channel_id=1, source_target_pairs={{0,24},{8,16},{16,8},{24,0},{32,56},{40,48},{48,40},{56,32},{64,88... | collective-permute-start | bytes 147464 | tf_op jit(solution)/shard_map/ppermute | solution.py:682
  95.8 3.5 %collective-permute-start.10 = (f32[96,128]{1,0:T(8,128)S(1)}, f32[96,128]{1,0:T(8,128)S(1)}, u32[]{:S(2)}, u32[]{:S(2)}) collective-permute-start(f32[96,128]{1,0:T(8,128)S(1)} %pad_maximum_fusion.3), channel_id=1, source_target_pairs={{0,8},{8,0},{16,24},{24,16},{32,40},{40,32},{48,56},{56,48},{64,72... | collective-permute-start | bytes 147464 | tf_op jit(solution)/shard_map/ppermute | solution.py:682
  99.4 4.4 %collective-permute-start.13 = (f32[64,128]{1,0:T(8,128)S(1)}, f32[64,128]{1,0:T(8,128)S(1)}, u32[]{:S(2)}, u32[]{:S(2)}) collective-permute-start(f32[64,128]{1,0:T(8,128)S(1)} %fusion), channel_id=1, source_target_pairs={{0,4},{1,5},{2,6},{3,7},{4,0},{5,1},{6,2},{7,3},{8,12},{9,13},{10,... | collective-permute-start | bytes 98312 | tf_op jit(solution)/shard_map/ppermute | solution.py:682
  102.4 4.0 %collective-permute-start.12 = (f32[64,128]{1,0:T(8,128)S(1)}, f32[64,128]{1,0:T(8,128)S(1)}, u32[]{:S(2)}, u32[]{:S(2)}) collective-permute-start(f32[64,128]{1,0:T(8,128)S(1)} %fusion), channel_id=1, source_target_pairs={{0,6},{1,7},{2,4},{3,5},{4,2},{5,3},{6,0},{7,1},{8,14},{9,15},{10,... | collective-permute-start | bytes 98312 | tf_op jit(solution)/shard_map/ppermute | solution.py:682
  103.1 3.2 %collective-permute-start.11 = (f32[64,128]{1,0:T(8,128)S(1)}, f32[64,128]{1,0:T(8,128)S(1)}, u32[]{:S(2)}, u32[]{:S(2)}) collective-permute-start(f32[64,128]{1,0:T(8,128)S(1)} %fusion), channel_id=1, source_target_pairs={{0,2},{1,3},{2,0},{3,1},{4,6},{5,7},{6,4},{7,5},{8,10},{9,11},{10,... | collective-permute-start | bytes 98312 | tf_op jit(solution)/shard_map/ppermute | solution.py:682
  118.1 5.2 %collective-permute-start.14 = (f32[64,128]{1,0:T(8,128)S(1)}, f32[64,128]{1,0:T(8,128)S(1)}, u32[]{:S(2)}, u32[]{:S(2)}) collective-permute-start(f32[64,128]{1,0:T(8,128)S(1)} %reduce_sum.9), channel_id=1, source_target_pairs={{0,1},{1,0},{2,3},{3,2},{4,5},{5,4},{6,7},{7,6},{8,9},{9,8},{10,11... | collective-permute-start | bytes 98312 | tf_op jit(solution)/shard_map/ppermute | solution.py:691
  123.3 4.7 %collective-permute-start.17 = (f32[2,64,128]{2,1,0:T(8,128)S(1)}, f32[2,64,128]{2,1,0:T(8,128)S(1)}, u32[]{:S(2)}, u32[]{:S(2)}) collective-permute-start(f32[2,64,128]{2,1,0:T(8,128)S(1)} %pad_maximum_fusion.both_ref), channel_id=1, source_target_pairs={{0,16},{8,24},{16,0},{24,8},{32,48},{40,56},{48,32},{56,40},{64,80... | collective-permute-start | bytes 196616 | tf_op jit(solution)/shard_map/ppermute | solution.py:682
  125.4 4.3 %collective-permute-start.16 = (f32[2,64,128]{2,1,0:T(8,128)S(1)}, f32[2,64,128]{2,1,0:T(8,128)S(1)}, u32[]{:S(2)}, u32[]{:S(2)}) collective-permute-start(f32[2,64,128]{2,1,0:T(8,128)S(1)} %pad_maximum_fusion.both_ref), channel_id=1, source_target_pairs={{0,24},{8,16},{16,8},{24,0},{32,56},{40,48},{48,40},{56,32},{64,88... | collective-permute-start | bytes 196616 | tf_op jit(solution)/shard_map/ppermute | solution.py:682
  126.0 3.7 %collective-permute-start.15 = (f32[2,64,128]{2,1,0:T(8,128)S(1)}, f32[2,64,128]{2,1,0:T(8,128)S(1)}, u32[]{:S(2)}, u32[]{:S(2)}) collective-permute-start(f32[2,64,128]{2,1,0:T(8,128)S(1)} %pad_maximum_fusion.both_ref), channel_id=1, source_target_pairs={{0,8},{8,0},{16,24},{24,16},{32,40},{40,32},{48,56},{56,48},{64,72... | collective-permute-start | bytes 196616 | tf_op jit(solution)/shard_map/ppermute | solution.py:682

commit v7 on v6

--- a/solution.py
+++ b/solution.py
@@ -302,7 +302,7 @@
     for n in reversed(order) if reverse else order:
         z, kappa = n // 2, n % 2
         reached = (mine < n) if reverse else (mine > n)
-        at = (z + planes // 2) % planes
+        at = (z + 3) % planes
         packed = jnp.where(core == kappa, own_ref[at], other_ref[at])
         to_column = kappa == (1 if reverse else 0)
         matrix, vector = unpack_map(packed, not to_column)
@@ -615,7 +615,7 @@
         d: [(z * width + x, z * width + (x ^ d)) for z in range(planes) for x in range(width)]
         for d in range(1, width)
     }
-    along_z = [[(z + planes // 2) % planes * width + x for z in range(planes)] for x in range(width)]
+    along_z = [[(z + 5) % planes * width + x for z in range(planes)] for x in range(width)]
     step_y = {d: [(b, b ^ (2 * d)) for b in range(2 * ys)] for d in range(1, ys)}
     cores = [(b, b ^ 1) for b in range(2 * ys)]
     axes = ("seq", "batch")

time: 131 us -> 129 us (0.985)
  blocking collectives: 61.1 us -> 55.6 us
  starting transfers between devices: 23.4 us -> 27.1 us
    all_to_all x4, blocking collectives: 49.4 us -> 44.7 us  [exchange(): lax.all_to_all(value, 'seq', 0, 0, axis_index_groups=along_z, tiled=True)]
    ppermute x4, starting transfers between devices: 2.76 us -> 6.32 us  [exchange(): return (own, lax.ppermute(own, 'batch', cores))]
where the time goes in v7:
time: 129 us
  blocking collectives  55.6 us (43%)
  Pallas kernels  27.1 us (21%)
  starting transfers between devices  27.1 us (21%)
  waiting for transfers between devices  18.1 us (14%)
    all_to_all x4, blocking collectives, exchange(): lax.all_to_all(value, 'seq', 0, 0, axis_index_groups=along_z, tiled=True)  44.7 us
    pallas_call x9, Pallas kernels, call(): pl.pallas_call(kernel, out_shape=[jax.ShapeDtypeStruct(*out) for out in o...  27.1 us
    all_to_all x1, blocking collectives, local(): lax.all_to_all(wide, 'seq', 0, 0, axis_index_groups=along_z, tiled=True)  11 us
    ppermute x9, starting transfers between devices, around(): got = {d: lax.ppermute(value_of(d), axis, steps[d]) for d in order}  9.58 us
    ppermute x9, waiting for transfers between devices, around(): got = {d: lax.ppermute(value_of(d), axis, steps[d]) for d in order}  8.13 us
    ppermute x4, starting transfers between devices, exchange(): return (own, lax.ppermute(own, 'batch', cores))  6.32 us
    ppermute x1, starting transfers between devices, local(): one = lax.ppermute(one, axes, there[0])  6.04 us
    ppermute x1, starting transfers between devices, local(): other = lax.ppermute(part, 'batch', cores)  4.19 us
  transfers between devices with their start and end apart: 18, of which 14 were waited for; matrix products, arithmetic and copies ran while one was open for 0% of the time, Pallas kernels for 2%

profile of v7, /device:TPU:1, one launch (start us, length us, event | category | flops | bytes accessed | tf_op | source)
XLA Modules:
  0.0 128.9 jit_solution(10467688671148251241)
XLA Ops:
  0.7 0.1 pad_add_fusion.where_ref
  0.8 1.6 %shard_map.110 = (f32[168,128]{1,0:T(8,128)S(1)}, f32[168,128]{1,0:T(8,128)S(1)}) custom-call(s32[4]{0:T(128)S(1)} %pad_add_fusion.where_ref, bf16[2,64,256]{2,1,0:T(8,128)(2,1)} %x_hbm.1, f32[64,2,64]{2,1,0:T(2,128)} %cot_hbm.1, f32[2,64]{1,0:T(2,128)} %bitcast.20), custom_call_target="tpu_custom_call" | custom-call | tf_op jit(solution)/shard_map/pallas_call | solution.py:589
  2.4 6.0 %collective-permute-start = (f32[168,128]{1,0:T(8,128)S(1)}, f32[168,128]{1,0:T(8,128)S(1)}, u32[]{:S(2)}, u32[]{:S(2)}) collective-permute-start(f32[168,128]{1,0:T(8,128)S(1)} %get-tuple-element.45), channel_id=1, source_target_pairs={{0,0},{1,16},{2,2},{3,18},{4,4},{5,20},{6,6},{7,22},{8,8},{9,24},{... | collective-permute-start | bytes 258056 | tf_op jit(solution)/shard_map/ppermute | solution.py:634
  8.4 0.7 collective-permute-start.1
  9.1 1.2 shard_map.111
  10.3 0.3 collective-permute-done.a_ref
  10.6 3.1 %collective-permute-done.1.b_ref = f32[168,128]{1,0:T(8,128)S(1)} collective-permute-done((f32[168,128]{1,0:T(8,128)S(1)}, f32[168,128]{1,0:T(8,128)S(1)}, u32[]{:S(2)}, u32[]{:S(2)}) %collective-permute-start.1) | collective-permute-done | bytes 86048 | tf_op jit(solution)/shard_map/ppermute | solution.py:635
  13.6 3.4 %shard_map.112 = (f32[3,64,128]{2,1,0:T(8,128)S(1)}, bf16[128,256]{1,0:T(8,128)(2,1)S(1)}, f32[64,128]{1,0:T(8,128)S(1)}, f32[8,128]{1,0:T(8,128)S(1)}, f32[8,52...) custom-call(s32[4]{0:T(128)S(1)} %pad_add_fusion.where_ref, ...), custom_call_target="tpu_custom_call" | custom-call | tf_op jit(solution)/shard_map/pallas_call | solution.py:589
  17.1 12.7 %all_to_all.25.own_ref = f32[8,40,128]{2,1,0:T(8,128)S(1)} all-to-all(f32[8,40,128]{2,1,0:T(8,128)S(1)} %get-tuple-element.52), channel_id=1, replica_groups={{160,192,224,0,32,64,96,128},{168,200,232,8,40,72,104,136},{176,208,240..., dimensions={0} | all-to-all | bytes 327680 | tf_op jit(solution)/shard_map/all_to_all | solution.py:624
  29.8 0.0 collective-permute-start.2
  29.8 1.4 %collective-permute-done.2.other_ref = f32[8,40,128]{2,1,0:T(8,128)S(1)} collective-permute-done((f32[8,40,128]{2,1,0:T(8,128)S(1)}, f32[8,40,128]{2,1,0:T(8,128)S(1)}, u32[]{:S(2)}, u32[]{:S(2)}) %collective-permute-start.2) | collective-permute-done | bytes 163872 | tf_op jit(solution)/shard_map/ppermute | solution.py:625
  31.2 4.9 %shard_map.113 = (f32[8,520,128]{2,1,0:T(8,128)S(1)}, f32[8,64,128]{2,1,0:T(8,128)S(1)}, f32[8,128]{1,0:T(8,128)S(1)}, f32[72,128]{1,0:T(8,128)S(1)}, f32[8,40,128]{2,1,0:T(8,128)S(1)}) custom-call(s32[4]{0:T(128)S(1)} %pad_add_fusion.where_ref, f32[8,40,128]{2,1,0:T(8,128)S(1)} %all_to_all.25.own_ref, f32[8,40,128]{2,1,0:T(8,128)S(1)} %collective-permute-done.2.other_ref, ...), custom_call_target="tpu_custom_call" | custom-call | tf_op jit(solution)/shard_map/pallas_call | solution.py:589
  36.1 10.6 %all_to_all.26.own_ref = f32[8,40,128]{2,1,0:T(8,128)S(1)} all-to-all(f32[8,40,128]{2,1,0:T(8,128)S(1)} %get-tuple-element.59), channel_id=1, replica_groups={{160,192,224,0,32,64,96,128},{168,200,232,8,40,72,104,136},{176,208,240..., dimensions={0} | all-to-all | bytes 327680 | tf_op jit(solution)/shard_map/all_to_all | solution.py:624
  46.8 2.1 %collective-permute-start.3 = (f32[8,40,128]{2,1,0:T(8,128)S(1)}, f32[8,40,128]{2,1,0:T(8,128)S(1)}, u32[]{:S(2)}, u32[]{:S(2)}) collective-permute-start(f32[8,40,128]{2,1,0:T(8,128)S(1)} %all_to_all.26.own_ref), channel_id=1, source_target_pairs={{0,1},{1,0},{2,3},{3,2},{4,5},{5,4},{6,7},{7,6},{8,9},{9,8},{10,11... | collective-permute-start | bytes 491528 | tf_op jit(solution)/shard_map/ppermute | solution.py:625
  48.8 1.0 collective-permute-done.3.other_ref
  49.9 4.9 %shard_map.114 = (f32[8,520,128]{2,1,0:T(8,128)S(1)}, f32[8,64,128]{2,1,0:T(8,128)S(1)}, f32[8,128]{1,0:T(8,128)S(1)}, f32[72,128]{1,0:T(8,128)S(1)}, f32[8,40,128]{2,1,0:T(8,128)S(1)}) custom-call(s32[4]{0:T(128)S(1)} %pad_add_fusion.where_ref, f32[8,40,128]{2,1,0:T(8,128)S(1)} %all_to_all.26.own_ref, f32[8,40,128]{2,1,0:T(8,128)S(1)} %collective-permute-done.3.other_ref, ...), custom_call_target="tpu_custom_call" | custom-call | tf_op jit(solution)/shard_map/pallas_call | solution.py:589
  54.8 10.7 %all_to_all.27.own_ref = f32[8,40,128]{2,1,0:T(8,128)S(1)} all-to-all(f32[8,40,128]{2,1,0:T(8,128)S(1)} %get-tuple-element.64), channel_id=1, replica_groups={{160,192,224,0,32,64,96,128},{168,200,232,8,40,72,104,136},{176,208,240..., dimensions={0} | all-to-all | bytes 327680 | tf_op jit(solution)/shard_map/all_to_all | solution.py:624
  65.5 2.1 %collective-permute-start.4 = (f32[8,40,128]{2,1,0:T(8,128)S(1)}, f32[8,40,128]{2,1,0:T(8,128)S(1)}, u32[]{:S(2)}, u32[]{:S(2)}) collective-permute-start(f32[8,40,128]{2,1,0:T(8,128)S(1)} %all_to_all.27.own_ref), channel_id=1, source_target_pairs={{0,1},{1,0},{2,3},{3,2},{4,5},{5,4},{6,7},{7,6},{8,9},{9,8},{10,11... | collective-permute-start | bytes 491528 | tf_op jit(solution)/shard_map/ppermute | solution.py:625
  67.6 1.0 collective-permute-done.4.other_ref
  68.6 5.3 %shard_map.115 = (f32[64,128]{1,0:T(8,128)S(1)}, f32[6,64,128]{2,1,0:T(8,128)S(1)}, f32[8,64,128]{2,1,0:T(8,128)S(1)}, f32[8,128]{1,0:T(8,128)S(1)}, f32[72,128]{1,0:T(8,128)S(1)}, /*index=5*/f32[8,40,128]{2,1,0:T(8,128)S(1)}) custom-call(s32[4]{0:T(128)S(1)} %pad_add_fusion.where_ref, f32[8,40,128]{2,1,0:T(8,128)S(1)} %all_to_all.27.own_ref, ...), custom_call_target="tpu_custom_call" | custom-call | tf_op jit(solution)/shard_map/pallas_call | solution.py:589
  74.0 10.6 %all_to_all.28.own_ref = f32[8,40,128]{2,1,0:T(8,128)S(1)} all-to-all(f32[8,40,128]{2,1,0:T(8,128)S(1)} %get-tuple-element.70), channel_id=1, replica_groups={{160,192,224,0,32,64,96,128},{168,200,232,8,40,72,104,136},{176,208,240..., dimensions={0} | all-to-all | bytes 327680 | tf_op jit(solution)/shard_map/all_to_all | solution.py:624
  84.6 2.1 %collective-permute-start.5 = (f32[8,40,128]{2,1,0:T(8,128)S(1)}, f32[8,40,128]{2,1,0:T(8,128)S(1)}, u32[]{:S(2)}, u32[]{:S(2)}) collective-permute-start(f32[8,40,128]{2,1,0:T(8,128)S(1)} %all_to_all.28.own_ref), channel_id=1, source_target_pairs={{0,1},{1,0},{2,3},{3,2},{4,5},{5,4},{6,7},{7,6},{8,9},{9,8},{10,11... | collective-permute-start | bytes 491528 | tf_op jit(solution)/shard_map/ppermute | solution.py:625
  86.7 0.0 collective-permute-start.6
  86.7 1.2 collective-permute-done.6.across_ref
  87.9 0.0 collective-permute-done.5.other_ref
  87.9 3.0 %shard_map.116 = (f32[256,128]{1,0:T(8,128)S(1)}, f32[256,128]{1,0:T(8,128)S(1)}, f32[4,32,128]{2,1,0:T(8,128)S(1)}) custom-call(s32[4]{0:T(128)S(1)} %pad_add_fusion.where_ref, f32[8,40,128]{2,1,0:T(8,128)S(1)} %all_to_all.28.own_ref, f32[8,40,128]{2,1,0:T(8,128)S(1)} %collective-permute-done.5.other_ref, f32[6,64,128]{2,1,0:T(8,128)S(1)} %get-tuple-element.71.coef_ref, ...), custom_call_target="tpu_custom_call" | custom-call | tf_op jit(solution)/shard_map/pallas_call | solution.py:589
  90.9 0.3 collective-permute-start.7
  91.2 1.1 collective-permute-done.7
  92.4 1.2 collective-permute-start.8
  93.6 0.8 collective-permute-start.9
  94.4 0.7 collective-permute-start.10
  95.1 1.8 %collective-permute-done.8.two_ref = f32[96,128]{1,0:T(8,128)S(1)} collective-permute-done((f32[96,128]{1,0:T(8,128)S(1)}, f32[96,128]{1,0:T(8,128)S(1)}, u32[]{:S(2)}, u32[]{:S(2)}) %collective-permute-start.8) | collective-permute-done | bytes 49184 | tf_op jit(solution)/shard_map/ppermute | solution.py:682
  96.9 1.2 collective-permute-done.9.three_ref
  98.1 0.0 collective-permute-done.10.one_ref
  98.2 3.0 %collective-permute-start.13 = (f32[64,128]{1,0:T(8,128)S(1)}, f32[64,128]{1,0:T(8,128)S(1)}, u32[]{:S(2)}, u32[]{:S(2)}) collective-permute-start(f32[64,128]{1,0:T(8,128)S(1)} %fusion), channel_id=1, source_target_pairs={{0,4},{1,5},{2,6},{3,7},{4,0},{5,1},{6,2},{7,3},{8,12},{9,13},{10,... | collective-permute-start | bytes 98312 | tf_op jit(solution)/shard_map/ppermute | solution.py:682
  101.2 0.8 collective-permute-start.12
  101.9 0.0 collective-permute-start.11
  101.9 0.6 collective-permute-done.13
  102.5 2.6 %collective-permute-done.12 = f32[64,128]{1,0:T(8,128)S(1)} collective-permute-done((f32[64,128]{1,0:T(8,128)S(1)}, f32[64,128]{1,0:T(8,128)S(1)}, u32[]{:S(2)}, u32[]{:S(2)}) %collective-permute-start.12) | collective-permute-done | bytes 32800 | tf_op jit(solution)/shard_map/ppermute | solution.py:682
  105.1 0.0 collective-permute-done.11
  105.2 11.0 %all_to_all.29 = f32[8,64,128]{2,1,0:T(8,128)S(1)} all-to-all(f32[8,64,128]{2,1,0:T(8,128)S(1)} %broadcast_in_dim.10), channel_id=1, replica_groups={{160,192,224,0,32,64,96,128},{168,200,232,8,40,72,104,136},{176,208,240..., dimensions={0} | all-to-all | bytes 524288 | tf_op jit(solution)/shard_map/all_to_all | solution.py:690
  116.2 4.2 %collective-permute-start.14 = (f32[64,128]{1,0:T(8,128)S(1)}, f32[64,128]{1,0:T(8,128)S(1)}, u32[]{:S(2)}, u32[]{:S(2)}) collective-permute-start(f32[64,128]{1,0:T(8,128)S(1)} %reduce_sum.9), channel_id=1, source_target_pairs={{0,1},{1,0},{2,3},{3,2},{4,5},{5,4},{6,7},{7,6},{8,9},{9,8},{10,11... | collective-permute-start | bytes 98312 | tf_op jit(solution)/shard_map/ppermute | solution.py:691
  120.4 0.9 collective-permute-done.14
  121.2 2.0 %collective-permute-start.17 = (f32[2,64,128]{2,1,0:T(8,128)S(1)}, f32[2,64,128]{2,1,0:T(8,128)S(1)}, u32[]{:S(2)}, u32[]{:S(2)}) collective-permute-start(f32[2,64,128]{2,1,0:T(8,128)S(1)} %pad_maximum_fusion.both_ref), channel_id=1, source_target_pairs={{0,16},{8,24},{16,0},{24,8},{32,48},{40,56},{48,32},{56,40},{64,80... | collective-permute-start | bytes 196616 | tf_op jit(solution)/shard_map/ppermute | solution.py:682
  123.2 1.1 collective-permute-start.16
  124.3 0.0 collective-permute-start.15
  124.3 1.3 %shard_map.117 = f32[64,2,64]{2,1,0:T(2,128)} custom-call(s32[4]{0:T(128)S(1)} %pad_add_fusion.where_ref, f32[4,32,128]{2,1,0:T(8,128)S(1)} %get-tuple-element.78.home_ref, f32[96,128]{1,0:T(8,128)S(1)} %collective-permute-done.8.two_ref, f32[96,128]{1,0:T(8,128)S(1)} %collective-permute-done.9.three_ref, f32[96,128]{1,0:T(8,128)S(1)} %collective-permute-done.10.one_ref), custom_call_target="tpu_custom_call" | custom-call | tf_op jit(solution)/shard_map/pallas_call | solution.py:589
  125.6 0.3 collective-permute-done.17.two_ref
  126.0 1.6 %collective-permute-done.16.three_ref = f32[2,64,128]{2,1,0:T(8,128)S(1)} collective-permute-done((f32[2,64,128]{2,1,0:T(8,128)S(1)}, f32[2,64,128]{2,1,0:T(8,128)S(1)}, u32[]{:S(2)}, u32[]{:S(2)}) %collective-permute-start.16) | collective-permute-done | bytes 65568 | tf_op jit(solution)/shard_map/ppermute | solution.py:682
  127.6 0.0 collective-permute-done.15.one_ref
  127.6 1.3 %shard_map.118 = (f32[192,256]{1,0:T(8,128)}, f32[64,192]{1,0:T(8,128)}, f32[1,64]{1,0:T(1,128)}, f32[3,64]{1,0:T(4,128)}) custom-call(s32[4]{0:T(128)S(1)} %pad_add_fusion.where_ref, f32[2,64,128]{2,1,0:T(8,128)S(1)} %collective-permute-done.15.one_ref, f32[2,64,128]{2,1,0:T(8,128)S(1)} %collective-permute-done.16.three_ref, ...), custom_call_target="tpu_custom_call" | custom-call | tf_op jit(solution)/shard_map/pallas_call | solution.py:589
  (12 shorter events, 0.1 us)
Async XLA Ops:
  2.4 8.2 %collective-permute-start = (f32[168,128]{1,0:T(8,128)S(1)}, f32[168,128]{1,0:T(8,128)S(1)}, u32[]{:S(2)}, u32[]{:S(2)}) collective-permute-start(f32[168,128]{1,0:T(8,128)S(1)} %get-tuple-element.45), channel_id=1, source_target_pairs={{0,0},{1,16},{2,2},{3,18},{4,4},{5,20},{6,6},{7,22},{8,8},{9,24},{... | collective-permute-start | bytes 258056 | tf_op jit(solution)/shard_map/ppermute | solution.py:634
  8.4 5.2 %collective-permute-start.1 = (f32[168,128]{1,0:T(8,128)S(1)}, f32[168,128]{1,0:T(8,128)S(1)}, u32[]{:S(2)}, u32[]{:S(2)}) collective-permute-start(f32[168,128]{1,0:T(8,128)S(1)} %get-tuple-element.46), channel_id=1, source_target_pairs={{0,8},{1,24},{2,10},{3,26},{4,12},{5,28},{6,14},{7,30},{8,0},{9,16... | collective-permute-start | bytes 258056 | tf_op jit(solution)/shard_map/ppermute | solution.py:635
  29.8 1.4 %collective-permute-start.2 = (f32[8,40,128]{2,1,0:T(8,128)S(1)}, f32[8,40,128]{2,1,0:T(8,128)S(1)}, u32[]{:S(2)}, u32[]{:S(2)}) collective-permute-start(f32[8,40,128]{2,1,0:T(8,128)S(1)} %all_to_all.25.own_ref), channel_id=1, source_target_pairs={{0,1},{1,0},{2,3},{3,2},{4,5},{5,4},{6,7},{7,6},{8,9},{9,8},{10,11... | collective-permute-start | bytes 491528 | tf_op jit(solution)/shard_map/ppermute | solution.py:625
  46.8 3.1 %collective-permute-start.3 = (f32[8,40,128]{2,1,0:T(8,128)S(1)}, f32[8,40,128]{2,1,0:T(8,128)S(1)}, u32[]{:S(2)}, u32[]{:S(2)}) collective-permute-start(f32[8,40,128]{2,1,0:T(8,128)S(1)} %all_to_all.26.own_ref), channel_id=1, source_target_pairs={{0,1},{1,0},{2,3},{3,2},{4,5},{5,4},{6,7},{7,6},{8,9},{9,8},{10,11... | collective-permute-start | bytes 491528 | tf_op jit(solution)/shard_map/ppermute | solution.py:625
  65.5 3.2 %collective-permute-start.4 = (f32[8,40,128]{2,1,0:T(8,128)S(1)}, f32[8,40,128]{2,1,0:T(8,128)S(1)}, u32[]{:S(2)}, u32[]{:S(2)}) collective-permute-start(f32[8,40,128]{2,1,0:T(8,128)S(1)} %all_to_all.27.own_ref), channel_id=1, source_target_pairs={{0,1},{1,0},{2,3},{3,2},{4,5},{5,4},{6,7},{7,6},{8,9},{9,8},{10,11... | collective-permute-start | bytes 491528 | tf_op jit(solution)/shard_map/ppermute | solution.py:625
  84.6 3.3 %collective-permute-start.5 = (f32[8,40,128]{2,1,0:T(8,128)S(1)}, f32[8,40,128]{2,1,0:T(8,128)S(1)}, u32[]{:S(2)}, u32[]{:S(2)}) collective-permute-start(f32[8,40,128]{2,1,0:T(8,128)S(1)} %all_to_all.28.own_ref), channel_id=1, source_target_pairs={{0,1},{1,0},{2,3},{3,2},{4,5},{5,4},{6,7},{7,6},{8,9},{9,8},{10,11... | collective-permute-start | bytes 491528 | tf_op jit(solution)/shard_map/ppermute | solution.py:625
  86.7 1.2 collective-permute-start.6
  90.9 1.4 %collective-permute-start.7 = (f32[256,128]{1,0:T(8,128)S(1)}, f32[256,128]{1,0:T(8,128)S(1)}, u32[]{:S(2)}, u32[]{:S(2)}) collective-permute-start(f32[256,128]{1,0:T(8,128)S(1)} %get-tuple-element.80), channel_id=1, source_target_pairs={{0,1},{1,0},{2,3},{3,2},{4,5},{5,4},{6,7},{7,6},{8,9},{9,8},{10,11... | collective-permute-start | bytes 393224 | tf_op jit(solution)/shard_map/ppermute | solution.py:685
  92.4 4.5 %collective-permute-start.8 = (f32[96,128]{1,0:T(8,128)S(1)}, f32[96,128]{1,0:T(8,128)S(1)}, u32[]{:S(2)}, u32[]{:S(2)}) collective-permute-start(f32[96,128]{1,0:T(8,128)S(1)} %pad_maximum_fusion.1), channel_id=1, source_target_pairs={{0,16},{8,24},{16,0},{24,8},{32,48},{40,56},{48,32},{56,40},{64,80... | collective-permute-start | bytes 147464 | tf_op jit(solution)/shard_map/ppermute | solution.py:682
  93.6 4.5 %collective-permute-start.9 = (f32[96,128]{1,0:T(8,128)S(1)}, f32[96,128]{1,0:T(8,128)S(1)}, u32[]{:S(2)}, u32[]{:S(2)}) collective-permute-start(f32[96,128]{1,0:T(8,128)S(1)} %pad_maximum_fusion.2), channel_id=1, source_target_pairs={{0,24},{8,16},{16,8},{24,0},{32,56},{40,48},{48,40},{56,32},{64,88... | collective-permute-start | bytes 147464 | tf_op jit(solution)/shard_map/ppermute | solution.py:682
  94.4 3.7 %collective-permute-start.10 = (f32[96,128]{1,0:T(8,128)S(1)}, f32[96,128]{1,0:T(8,128)S(1)}, u32[]{:S(2)}, u32[]{:S(2)}) collective-permute-start(f32[96,128]{1,0:T(8,128)S(1)} %pad_maximum_fusion.3), channel_id=1, source_target_pairs={{0,8},{8,0},{16,24},{24,16},{32,40},{40,32},{48,56},{56,48},{64,72... | collective-permute-start | bytes 147464 | tf_op jit(solution)/shard_map/ppermute | solution.py:682
  98.2 4.4 %collective-permute-start.13 = (f32[64,128]{1,0:T(8,128)S(1)}, f32[64,128]{1,0:T(8,128)S(1)}, u32[]{:S(2)}, u32[]{:S(2)}) collective-permute-start(f32[64,128]{1,0:T(8,128)S(1)} %fusion), channel_id=1, source_target_pairs={{0,4},{1,5},{2,6},{3,7},{4,0},{5,1},{6,2},{7,3},{8,12},{9,13},{10,... | collective-permute-start | bytes 98312 | tf_op jit(solution)/shard_map/ppermute | solution.py:682
  101.2 4.0 %collective-permute-start.12 = (f32[64,128]{1,0:T(8,128)S(1)}, f32[64,128]{1,0:T(8,128)S(1)}, u32[]{:S(2)}, u32[]{:S(2)}) collective-permute-start(f32[64,128]{1,0:T(8,128)S(1)} %fusion), channel_id=1, source_target_pairs={{0,6},{1,7},{2,4},{3,5},{4,2},{5,3},{6,0},{7,1},{8,14},{9,15},{10,... | collective-permute-start | bytes 98312 | tf_op jit(solution)/shard_map/ppermute | solution.py:682
  101.9 3.2 %collective-permute-start.11 = (f32[64,128]{1,0:T(8,128)S(1)}, f32[64,128]{1,0:T(8,128)S(1)}, u32[]{:S(2)}, u32[]{:S(2)}) collective-permute-start(f32[64,128]{1,0:T(8,128)S(1)} %fusion), channel_id=1, source_target_pairs={{0,2},{1,3},{2,0},{3,1},{4,6},{5,7},{6,4},{7,5},{8,10},{9,11},{10,... | collective-permute-start | bytes 98312 | tf_op jit(solution)/shard_map/ppermute | solution.py:682
  116.2 5.0 %collective-permute-start.14 = (f32[64,128]{1,0:T(8,128)S(1)}, f32[64,128]{1,0:T(8,128)S(1)}, u32[]{:S(2)}, u32[]{:S(2)}) collective-permute-start(f32[64,128]{1,0:T(8,128)S(1)} %reduce_sum.9), channel_id=1, source_target_pairs={{0,1},{1,0},{2,3},{3,2},{4,5},{5,4},{6,7},{7,6},{8,9},{9,8},{10,11... | collective-permute-start | bytes 98312 | tf_op jit(solution)/shard_map/ppermute | solution.py:691
  121.2 4.7 %collective-permute-start.17 = (f32[2,64,128]{2,1,0:T(8,128)S(1)}, f32[2,64,128]{2,1,0:T(8,128)S(1)}, u32[]{:S(2)}, u32[]{:S(2)}) collective-permute-start(f32[2,64,128]{2,1,0:T(8,128)S(1)} %pad_maximum_fusion.both_ref), channel_id=1, source_target_pairs={{0,16},{8,24},{16,0},{24,8},{32,48},{40,56},{48,32},{56,40},{64,80... | collective-permute-start | bytes 196616 | tf_op jit(solution)/shard_map/ppermute | solution.py:682
  123.2 4.3 %collective-permute-start.16 = (f32[2,64,128]{2,1,0:T(8,128)S(1)}, f32[2,64,128]{2,1,0:T(8,128)S(1)}, u32[]{:S(2)}, u32[]{:S(2)}) collective-permute-start(f32[2,64,128]{2,1,0:T(8,128)S(1)} %pad_maximum_fusion.both_ref), channel_id=1, source_target_pairs={{0,24},{8,16},{16,8},{24,0},{32,56},{40,48},{48,40},{56,32},{64,88... | collective-permute-start | bytes 196616 | tf_op jit(solution)/shard_map/ppermute | solution.py:682
  124.3 3.3 %collective-permute-start.15 = (f32[2,64,128]{2,1,0:T(8,128)S(1)}, f32[2,64,128]{2,1,0:T(8,128)S(1)}, u32[]{:S(2)}, u32[]{:S(2)}) collective-permute-start(f32[2,64,128]{2,1,0:T(8,128)S(1)} %pad_maximum_fusion.both_ref), channel_id=1, source_target_pairs={{0,8},{8,0},{16,24},{24,16},{32,40},{40,32},{48,56},{56,48},{64,72... | collective-permute-start | bytes 196616 | tf_op jit(solution)/shard_map/ppermute | solution.py:682

commit v8 on v7

--- a/solution.py
+++ b/solution.py
@@ -17,6 +17,7 @@
 BLOCKS = (0, 22, 44, 65)
 MAP = 40
 PART = 168
+ORDER = (5, 4, 6, 7, 3, 2, 1, 0)
 F32 = jnp.float32
 BF16 = jnp.bfloat16
 VMEM = pltpu.VMEM
@@ -302,7 +303,7 @@
     for n in reversed(order) if reverse else order:
         z, kappa = n // 2, n % 2
         reached = (mine < n) if reverse else (mine > n)
-        at = (z + 3) % planes
+        at = ORDER.index(z)
         packed = jnp.where(core == kappa, own_ref[at], other_ref[at])
         to_column = kappa == (1 if reverse else 0)
         matrix, vector = unpack_map(packed, not to_column)
@@ -615,7 +616,7 @@
         d: [(z * width + x, z * width + (x ^ d)) for z in range(planes) for x in range(width)]
         for d in range(1, width)
     }
-    along_z = [[(z + 5) % planes * width + x for z in range(planes)] for x in range(width)]
+    along_z = [[z * width + x for z in ORDER] for x in range(width)]
     step_y = {d: [(b, b ^ (2 * d)) for b in range(2 * ys)] for d in range(1, ys)}
     cores = [(b, b ^ 1) for b in range(2 * ys)]
     axes = ("seq", "batch")

time: 129 us -> 127 us (0.984)
  starting transfers between devices: 27.1 us -> 24.2 us
    ppermute x4, starting transfers between devices: 6.32 us -> 3.65 us  [exchange(): return (own, lax.ppermute(own, 'batch', cores))]
where the time goes in v8:
time: 127 us
  blocking collectives  56.4 us (44%)
  Pallas kernels  27.1 us (21%)
  starting transfers between devices  24.2 us (19%)
  waiting for transfers between devices  18.1 us (14%)
    all_to_all x4, blocking collectives, exchange(): lax.all_to_all(value, 'seq', 0, 0, axis_index_groups=along_z, tiled=True)  45.6 us
    pallas_call x9, Pallas kernels, call(): pl.pallas_call(kernel, out_shape=[jax.ShapeDtypeStruct(*out) for out in o...  27.1 us
    all_to_all x1, blocking collectives, local(): lax.all_to_all(wide, 'seq', 0, 0, axis_index_groups=along_z, tiled=True)  10.9 us
    ppermute x9, starting transfers between devices, around(): got = {d: lax.ppermute(value_of(d), axis, steps[d]) for d in order}  9.53 us
    ppermute x9, waiting for transfers between devices, around(): got = {d: lax.ppermute(value_of(d), axis, steps[d]) for d in order}  8.18 us
    ppermute x1, starting transfers between devices, local(): one = lax.ppermute(one, axes, there[0])  6.04 us
    ppermute x1, starting transfers between devices, local(): other = lax.ppermute(part, 'batch', cores)  3.99 us
    ppermute x4, starting transfers between devices, exchange(): return (own, lax.ppermute(own, 'batch', cores))  3.65 us
  transfers between devices with their start and end apart: 18, of which 14 were waited for; matrix products, arithmetic and copies ran while one was open for 0% of the time, Pallas kernels for 2%

profile of v8, /device:TPU:1, one launch (start us, length us, event | category | flops | bytes accessed | tf_op | source)
XLA Modules:
  0.0 126.9 jit_solution(9489295109719913984)
XLA Ops:
  0.7 0.1 pad_add_fusion.where_ref
  0.8 1.6 %shard_map.110 = (f32[168,128]{1,0:T(8,128)S(1)}, f32[168,128]{1,0:T(8,128)S(1)}) custom-call(s32[4]{0:T(128)S(1)} %pad_add_fusion.where_ref, bf16[2,64,256]{2,1,0:T(8,128)(2,1)} %x_hbm.1, f32[64,2,64]{2,1,0:T(2,128)} %cot_hbm.1, f32[2,64]{1,0:T(2,128)} %bitcast.20), custom_call_target="tpu_custom_call" | custom-call | tf_op jit(solution)/shard_map/pallas_call | solution.py:590
  2.4 6.0 %collective-permute-start = (f32[168,128]{1,0:T(8,128)S(1)}, f32[168,128]{1,0:T(8,128)S(1)}, u32[]{:S(2)}, u32[]{:S(2)}) collective-permute-start(f32[168,128]{1,0:T(8,128)S(1)} %get-tuple-element.45), channel_id=1, source_target_pairs={{0,0},{1,16},{2,2},{3,18},{4,4},{5,20},{6,6},{7,22},{8,8},{9,24},{... | collective-permute-start | bytes 258056 | tf_op jit(solution)/shard_map/ppermute | solution.py:635
  8.4 0.7 collective-permute-start.1
  9.1 1.2 shard_map.111
  10.3 0.3 collective-permute-done.a_ref
  10.6 3.1 %collective-permute-done.1.b_ref = f32[168,128]{1,0:T(8,128)S(1)} collective-permute-done((f32[168,128]{1,0:T(8,128)S(1)}, f32[168,128]{1,0:T(8,128)S(1)}, u32[]{:S(2)}, u32[]{:S(2)}) %collective-permute-start.1) | collective-permute-done | bytes 86048 | tf_op jit(solution)/shard_map/ppermute | solution.py:636
  13.6 3.4 %shard_map.112 = (f32[3,64,128]{2,1,0:T(8,128)S(1)}, bf16[128,256]{1,0:T(8,128)(2,1)S(1)}, f32[64,128]{1,0:T(8,128)S(1)}, f32[8,128]{1,0:T(8,128)S(1)}, f32[8,52...) custom-call(s32[4]{0:T(128)S(1)} %pad_add_fusion.where_ref, ...), custom_call_target="tpu_custom_call" | custom-call | tf_op jit(solution)/shard_map/pallas_call | solution.py:590
  17.1 12.7 %all_to_all.25.own_ref = f32[8,40,128]{2,1,0:T(8,128)S(1)} all-to-all(f32[8,40,128]{2,1,0:T(8,128)S(1)} %get-tuple-element.52), channel_id=1, replica_groups={{160,128,192,224,96,64,32,0},{168,136,200,232,104,72,40,8},{176,144,208..., dimensions={0} | all-to-all | bytes 327680 | tf_op jit(solution)/shard_map/all_to_all | solution.py:625
  29.8 0.0 collective-permute-start.2
  29.8 1.4 %collective-permute-done.2.other_ref = f32[8,40,128]{2,1,0:T(8,128)S(1)} collective-permute-done((f32[8,40,128]{2,1,0:T(8,128)S(1)}, f32[8,40,128]{2,1,0:T(8,128)S(1)}, u32[]{:S(2)}, u32[]{:S(2)}) %collective-permute-start.2) | collective-permute-done | bytes 163872 | tf_op jit(solution)/shard_map/ppermute | solution.py:626
  31.2 4.9 %shard_map.113 = (f32[8,520,128]{2,1,0:T(8,128)S(1)}, f32[8,64,128]{2,1,0:T(8,128)S(1)}, f32[8,128]{1,0:T(8,128)S(1)}, f32[72,128]{1,0:T(8,128)S(1)}, f32[8,40,128]{2,1,0:T(8,128)S(1)}) custom-call(s32[4]{0:T(128)S(1)} %pad_add_fusion.where_ref, f32[8,40,128]{2,1,0:T(8,128)S(1)} %all_to_all.25.own_ref, f32[8,40,128]{2,1,0:T(8,128)S(1)} %collective-permute-done.2.other_ref, ...), custom_call_target="tpu_custom_call" | custom-call | tf_op jit(solution)/shard_map/pallas_call | solution.py:590
  36.1 11.3 %all_to_all.26.own_ref = f32[8,40,128]{2,1,0:T(8,128)S(1)} all-to-all(f32[8,40,128]{2,1,0:T(8,128)S(1)} %get-tuple-element.59), channel_id=1, replica_groups={{160,128,192,224,96,64,32,0},{168,136,200,232,104,72,40,8},{176,144,208..., dimensions={0} | all-to-all | bytes 327680 | tf_op jit(solution)/shard_map/all_to_all | solution.py:625
  47.4 1.0 collective-permute-start.3
  48.5 1.0 collective-permute-done.3.other_ref
  49.5 4.9 %shard_map.114 = (f32[8,520,128]{2,1,0:T(8,128)S(1)}, f32[8,64,128]{2,1,0:T(8,128)S(1)}, f32[8,128]{1,0:T(8,128)S(1)}, f32[72,128]{1,0:T(8,128)S(1)}, f32[8,40,128]{2,1,0:T(8,128)S(1)}) custom-call(s32[4]{0:T(128)S(1)} %pad_add_fusion.where_ref, f32[8,40,128]{2,1,0:T(8,128)S(1)} %all_to_all.26.own_ref, f32[8,40,128]{2,1,0:T(8,128)S(1)} %collective-permute-done.3.other_ref, ...), custom_call_target="tpu_custom_call" | custom-call | tf_op jit(solution)/shard_map/pallas_call | solution.py:590
  54.4 10.8 %all_to_all.27.own_ref = f32[8,40,128]{2,1,0:T(8,128)S(1)} all-to-all(f32[8,40,128]{2,1,0:T(8,128)S(1)} %get-tuple-element.64), channel_id=1, replica_groups={{160,128,192,224,96,64,32,0},{168,136,200,232,104,72,40,8},{176,144,208..., dimensions={0} | all-to-all | bytes 327680 | tf_op jit(solution)/shard_map/all_to_all | solution.py:625
  65.2 1.3 %collective-permute-start.4 = (f32[8,40,128]{2,1,0:T(8,128)S(1)}, f32[8,40,128]{2,1,0:T(8,128)S(1)}, u32[]{:S(2)}, u32[]{:S(2)}) collective-permute-start(f32[8,40,128]{2,1,0:T(8,128)S(1)} %all_to_all.27.own_ref), channel_id=1, source_target_pairs={{0,1},{1,0},{2,3},{3,2},{4,5},{5,4},{6,7},{7,6},{8,9},{9,8},{10,11... | collective-permute-start | bytes 491528 | tf_op jit(solution)/shard_map/ppermute | solution.py:626
  66.5 1.0 collective-permute-done.4.other_ref
  67.5 5.3 %shard_map.115 = (f32[64,128]{1,0:T(8,128)S(1)}, f32[6,64,128]{2,1,0:T(8,128)S(1)}, f32[8,64,128]{2,1,0:T(8,128)S(1)}, f32[8,128]{1,0:T(8,128)S(1)}, f32[72,128]{1,0:T(8,128)S(1)}, /*index=5*/f32[8,40,128]{2,1,0:T(8,128)S(1)}) custom-call(s32[4]{0:T(128)S(1)} %pad_add_fusion.where_ref, f32[8,40,128]{2,1,0:T(8,128)S(1)} %all_to_all.27.own_ref, ...), custom_call_target="tpu_custom_call" | custom-call | tf_op jit(solution)/shard_map/pallas_call | solution.py:590
  72.8 10.8 %all_to_all.28.own_ref = f32[8,40,128]{2,1,0:T(8,128)S(1)} all-to-all(f32[8,40,128]{2,1,0:T(8,128)S(1)} %get-tuple-element.70), channel_id=1, replica_groups={{160,128,192,224,96,64,32,0},{168,136,200,232,104,72,40,8},{176,144,208..., dimensions={0} | all-to-all | bytes 327680 | tf_op jit(solution)/shard_map/all_to_all | solution.py:625
  83.6 1.3 %collective-permute-start.5 = (f32[8,40,128]{2,1,0:T(8,128)S(1)}, f32[8,40,128]{2,1,0:T(8,128)S(1)}, u32[]{:S(2)}, u32[]{:S(2)}) collective-permute-start(f32[8,40,128]{2,1,0:T(8,128)S(1)} %all_to_all.28.own_ref), channel_id=1, source_target_pairs={{0,1},{1,0},{2,3},{3,2},{4,5},{5,4},{6,7},{7,6},{8,9},{9,8},{10,11... | collective-permute-start | bytes 491528 | tf_op jit(solution)/shard_map/ppermute | solution.py:626
  84.9 0.0 collective-permute-start.6
  84.9 1.2 collective-permute-done.6.across_ref
  86.1 0.0 collective-permute-done.5.other_ref
  86.1 3.0 %shard_map.116 = (f32[256,128]{1,0:T(8,128)S(1)}, f32[256,128]{1,0:T(8,128)S(1)}, f32[4,32,128]{2,1,0:T(8,128)S(1)}) custom-call(s32[4]{0:T(128)S(1)} %pad_add_fusion.where_ref, f32[8,40,128]{2,1,0:T(8,128)S(1)} %all_to_all.28.own_ref, f32[8,40,128]{2,1,0:T(8,128)S(1)} %collective-permute-done.5.other_ref, f32[6,64,128]{2,1,0:T(8,128)S(1)} %get-tuple-element.71.coef_ref, ...), custom_call_target="tpu_custom_call" | custom-call | tf_op jit(solution)/shard_map/pallas_call | solution.py:590
  89.2 0.3 collective-permute-start.7
  89.5 1.1 collective-permute-done.7
  90.6 1.3 collective-permute-start.8
  91.9 0.6 collective-permute-start.9
  92.5 0.9 collective-permute-start.10
  93.4 1.8 %collective-permute-done.8.two_ref = f32[96,128]{1,0:T(8,128)S(1)} collective-permute-done((f32[96,128]{1,0:T(8,128)S(1)}, f32[96,128]{1,0:T(8,128)S(1)}, u32[]{:S(2)}, u32[]{:S(2)}) %collective-permute-start.8) | collective-permute-done | bytes 49184 | tf_op jit(solution)/shard_map/ppermute | solution.py:683
  95.2 1.2 collective-permute-done.9.three_ref
  96.4 0.0 collective-permute-done.10.one_ref
  96.4 3.0 %collective-permute-start.13 = (f32[64,128]{1,0:T(8,128)S(1)}, f32[64,128]{1,0:T(8,128)S(1)}, u32[]{:S(2)}, u32[]{:S(2)}) collective-permute-start(f32[64,128]{1,0:T(8,128)S(1)} %fusion), channel_id=1, source_target_pairs={{0,4},{1,5},{2,6},{3,7},{4,0},{5,1},{6,2},{7,3},{8,12},{9,13},{10,... | collective-permute-start | bytes 98312 | tf_op jit(solution)/shard_map/ppermute | solution.py:683
  99.4 0.8 collective-permute-start.12
  100.2 0.0 collective-permute-start.11
  100.2 0.6 collective-permute-done.13
  100.8 2.6 %collective-permute-done.12 = f32[64,128]{1,0:T(8,128)S(1)} collective-permute-done((f32[64,128]{1,0:T(8,128)S(1)}, f32[64,128]{1,0:T(8,128)S(1)}, u32[]{:S(2)}, u32[]{:S(2)}) %collective-permute-start.12) | collective-permute-done | bytes 32800 | tf_op jit(solution)/shard_map/ppermute | solution.py:683
  103.4 0.0 collective-permute-done.11
  103.4 10.9 %all_to_all.29 = f32[8,64,128]{2,1,0:T(8,128)S(1)} all-to-all(f32[8,64,128]{2,1,0:T(8,128)S(1)} %broadcast_in_dim.10), channel_id=1, replica_groups={{160,128,192,224,96,64,32,0},{168,136,200,232,104,72,40,8},{176,144,208..., dimensions={0} | all-to-all | bytes 524288 | tf_op jit(solution)/shard_map/all_to_all | solution.py:691
  114.3 4.0 %collective-permute-start.14 = (f32[64,128]{1,0:T(8,128)S(1)}, f32[64,128]{1,0:T(8,128)S(1)}, u32[]{:S(2)}, u32[]{:S(2)}) collective-permute-start(f32[64,128]{1,0:T(8,128)S(1)} %reduce_sum.9), channel_id=1, source_target_pairs={{0,1},{1,0},{2,3},{3,2},{4,5},{5,4},{6,7},{7,6},{8,9},{9,8},{10,11... | collective-permute-start | bytes 98312 | tf_op jit(solution)/shard_map/ppermute | solution.py:692
  118.3 0.9 collective-permute-done.14
  119.2 2.0 %collective-permute-start.17 = (f32[2,64,128]{2,1,0:T(8,128)S(1)}, f32[2,64,128]{2,1,0:T(8,128)S(1)}, u32[]{:S(2)}, u32[]{:S(2)}) collective-permute-start(f32[2,64,128]{2,1,0:T(8,128)S(1)} %pad_maximum_fusion.both_ref), channel_id=1, source_target_pairs={{0,16},{8,24},{16,0},{24,8},{32,48},{40,56},{48,32},{56,40},{64,80... | collective-permute-start | bytes 196616 | tf_op jit(solution)/shard_map/ppermute | solution.py:683
  121.2 1.0 collective-permute-start.16
  122.2 0.0 collective-permute-start.15
  122.2 1.3 %shard_map.117 = f32[64,2,64]{2,1,0:T(2,128)} custom-call(s32[4]{0:T(128)S(1)} %pad_add_fusion.where_ref, f32[4,32,128]{2,1,0:T(8,128)S(1)} %get-tuple-element.78.home_ref, f32[96,128]{1,0:T(8,128)S(1)} %collective-permute-done.8.two_ref, f32[96,128]{1,0:T(8,128)S(1)} %collective-permute-done.9.three_ref, f32[96,128]{1,0:T(8,128)S(1)} %collective-permute-done.10.one_ref), custom_call_target="tpu_custom_call" | custom-call | tf_op jit(solution)/shard_map/pallas_call | solution.py:590
  123.5 0.3 collective-permute-done.17.two_ref
  123.9 1.6 %collective-permute-done.16.three_ref = f32[2,64,128]{2,1,0:T(8,128)S(1)} collective-permute-done((f32[2,64,128]{2,1,0:T(8,128)S(1)}, f32[2,64,128]{2,1,0:T(8,128)S(1)}, u32[]{:S(2)}, u32[]{:S(2)}) %collective-permute-start.16) | collective-permute-done | bytes 65568 | tf_op jit(solution)/shard_map/ppermute | solution.py:683
  125.5 0.0 collective-permute-done.15.one_ref
  125.5 1.3 %shard_map.118 = (f32[192,256]{1,0:T(8,128)}, f32[64,192]{1,0:T(8,128)}, f32[1,64]{1,0:T(1,128)}, f32[3,64]{1,0:T(4,128)}) custom-call(s32[4]{0:T(128)S(1)} %pad_add_fusion.where_ref, f32[2,64,128]{2,1,0:T(8,128)S(1)} %collective-permute-done.15.one_ref, f32[2,64,128]{2,1,0:T(8,128)S(1)} %collective-permute-done.16.three_ref, ...), custom_call_target="tpu_custom_call" | custom-call | tf_op jit(solution)/shard_map/pallas_call | solution.py:590
  (12 shorter events, 0.1 us)
Async XLA Ops:
  2.4 8.2 %collective-permute-start = (f32[168,128]{1,0:T(8,128)S(1)}, f32[168,128]{1,0:T(8,128)S(1)}, u32[]{:S(2)}, u32[]{:S(2)}) collective-permute-start(f32[168,128]{1,0:T(8,128)S(1)} %get-tuple-element.45), channel_id=1, source_target_pairs={{0,0},{1,16},{2,2},{3,18},{4,4},{5,20},{6,6},{7,22},{8,8},{9,24},{... | collective-permute-start | bytes 258056 | tf_op jit(solution)/shard_map/ppermute | solution.py:635
  8.4 5.2 %collective-permute-start.1 = (f32[168,128]{1,0:T(8,128)S(1)}, f32[168,128]{1,0:T(8,128)S(1)}, u32[]{:S(2)}, u32[]{:S(2)}) collective-permute-start(f32[168,128]{1,0:T(8,128)S(1)} %get-tuple-element.46), channel_id=1, source_target_pairs={{0,8},{1,24},{2,10},{3,26},{4,12},{5,28},{6,14},{7,30},{8,0},{9,16... | collective-permute-start | bytes 258056 | tf_op jit(solution)/shard_map/ppermute | solution.py:636
  29.8 1.4 %collective-permute-start.2 = (f32[8,40,128]{2,1,0:T(8,128)S(1)}, f32[8,40,128]{2,1,0:T(8,128)S(1)}, u32[]{:S(2)}, u32[]{:S(2)}) collective-permute-start(f32[8,40,128]{2,1,0:T(8,128)S(1)} %all_to_all.25.own_ref), channel_id=1, source_target_pairs={{0,1},{1,0},{2,3},{3,2},{4,5},{5,4},{6,7},{7,6},{8,9},{9,8},{10,11... | collective-permute-start | bytes 491528 | tf_op jit(solution)/shard_map/ppermute | solution.py:626
  47.4 2.1 %collective-permute-start.3 = (f32[8,40,128]{2,1,0:T(8,128)S(1)}, f32[8,40,128]{2,1,0:T(8,128)S(1)}, u32[]{:S(2)}, u32[]{:S(2)}) collective-permute-start(f32[8,40,128]{2,1,0:T(8,128)S(1)} %all_to_all.26.own_ref), channel_id=1, source_target_pairs={{0,1},{1,0},{2,3},{3,2},{4,5},{5,4},{6,7},{7,6},{8,9},{9,8},{10,11... | collective-permute-start | bytes 491528 | tf_op jit(solution)/shard_map/ppermute | solution.py:626
  65.2 2.3 %collective-permute-start.4 = (f32[8,40,128]{2,1,0:T(8,128)S(1)}, f32[8,40,128]{2,1,0:T(8,128)S(1)}, u32[]{:S(2)}, u32[]{:S(2)}) collective-permute-start(f32[8,40,128]{2,1,0:T(8,128)S(1)} %all_to_all.27.own_ref), channel_id=1, source_target_pairs={{0,1},{1,0},{2,3},{3,2},{4,5},{5,4},{6,7},{7,6},{8,9},{9,8},{10,11... | collective-permute-start | bytes 491528 | tf_op jit(solution)/shard_map/ppermute | solution.py:626
  83.6 2.5 %collective-permute-start.5 = (f32[8,40,128]{2,1,0:T(8,128)S(1)}, f32[8,40,128]{2,1,0:T(8,128)S(1)}, u32[]{:S(2)}, u32[]{:S(2)}) collective-permute-start(f32[8,40,128]{2,1,0:T(8,128)S(1)} %all_to_all.28.own_ref), channel_id=1, source_target_pairs={{0,1},{1,0},{2,3},{3,2},{4,5},{5,4},{6,7},{7,6},{8,9},{9,8},{10,11... | collective-permute-start | bytes 491528 | tf_op jit(solution)/shard_map/ppermute | solution.py:626
  84.9 1.2 collective-permute-start.6
  89.2 1.4 %collective-permute-start.7 = (f32[256,128]{1,0:T(8,128)S(1)}, f32[256,128]{1,0:T(8,128)S(1)}, u32[]{:S(2)}, u32[]{:S(2)}) collective-permute-start(f32[256,128]{1,0:T(8,128)S(1)} %get-tuple-element.80), channel_id=1, source_target_pairs={{0,1},{1,0},{2,3},{3,2},{4,5},{5,4},{6,7},{7,6},{8,9},{9,8},{10,11... | collective-permute-start | bytes 393224 | tf_op jit(solution)/shard_map/ppermute | solution.py:686
  90.6 4.5 %collective-permute-start.8 = (f32[96,128]{1,0:T(8,128)S(1)}, f32[96,128]{1,0:T(8,128)S(1)}, u32[]{:S(2)}, u32[]{:S(2)}) collective-permute-start(f32[96,128]{1,0:T(8,128)S(1)} %pad_maximum_fusion.1), channel_id=1, source_target_pairs={{0,16},{8,24},{16,0},{24,8},{32,48},{40,56},{48,32},{56,40},{64,80... | collective-permute-start | bytes 147464 | tf_op jit(solution)/shard_map/ppermute | solution.py:683
  91.9 4.5 %collective-permute-start.9 = (f32[96,128]{1,0:T(8,128)S(1)}, f32[96,128]{1,0:T(8,128)S(1)}, u32[]{:S(2)}, u32[]{:S(2)}) collective-permute-start(f32[96,128]{1,0:T(8,128)S(1)} %pad_maximum_fusion.2), channel_id=1, source_target_pairs={{0,24},{8,16},{16,8},{24,0},{32,56},{40,48},{48,40},{56,32},{64,88... | collective-permute-start | bytes 147464 | tf_op jit(solution)/shard_map/ppermute | solution.py:683
  92.5 3.9 %collective-permute-start.10 = (f32[96,128]{1,0:T(8,128)S(1)}, f32[96,128]{1,0:T(8,128)S(1)}, u32[]{:S(2)}, u32[]{:S(2)}) collective-permute-start(f32[96,128]{1,0:T(8,128)S(1)} %pad_maximum_fusion.3), channel_id=1, source_target_pairs={{0,8},{8,0},{16,24},{24,16},{32,40},{40,32},{48,56},{56,48},{64,72... | collective-permute-start | bytes 147464 | tf_op jit(solution)/shard_map/ppermute | solution.py:683
  96.4 4.4 %collective-permute-start.13 = (f32[64,128]{1,0:T(8,128)S(1)}, f32[64,128]{1,0:T(8,128)S(1)}, u32[]{:S(2)}, u32[]{:S(2)}) collective-permute-start(f32[64,128]{1,0:T(8,128)S(1)} %fusion), channel_id=1, source_target_pairs={{0,4},{1,5},{2,6},{3,7},{4,0},{5,1},{6,2},{7,3},{8,12},{9,13},{10,... | collective-permute-start | bytes 98312 | tf_op jit(solution)/shard_map/ppermute | solution.py:683
  99.4 4.0 %collective-permute-start.12 = (f32[64,128]{1,0:T(8,128)S(1)}, f32[64,128]{1,0:T(8,128)S(1)}, u32[]{:S(2)}, u32[]{:S(2)}) collective-permute-start(f32[64,128]{1,0:T(8,128)S(1)} %fusion), channel_id=1, source_target_pairs={{0,6},{1,7},{2,4},{3,5},{4,2},{5,3},{6,0},{7,1},{8,14},{9,15},{10,... | collective-permute-start | bytes 98312 | tf_op jit(solution)/shard_map/ppermute | solution.py:683
  100.2 3.2 %collective-permute-start.11 = (f32[64,128]{1,0:T(8,128)S(1)}, f32[64,128]{1,0:T(8,128)S(1)}, u32[]{:S(2)}, u32[]{:S(2)}) collective-permute-start(f32[64,128]{1,0:T(8,128)S(1)} %fusion), channel_id=1, source_target_pairs={{0,2},{1,3},{2,0},{3,1},{4,6},{5,7},{6,4},{7,5},{8,10},{9,11},{10,... | collective-permute-start | bytes 98312 | tf_op jit(solution)/shard_map/ppermute | solution.py:683
  114.3 4.8 %collective-permute-start.14 = (f32[64,128]{1,0:T(8,128)S(1)}, f32[64,128]{1,0:T(8,128)S(1)}, u32[]{:S(2)}, u32[]{:S(2)}) collective-permute-start(f32[64,128]{1,0:T(8,128)S(1)} %reduce_sum.9), channel_id=1, source_target_pairs={{0,1},{1,0},{2,3},{3,2},{4,5},{5,4},{6,7},{7,6},{8,9},{9,8},{10,11... | collective-permute-start | bytes 98312 | tf_op jit(solution)/shard_map/ppermute | solution.py:692
  119.2 4.7 %collective-permute-start.17 = (f32[2,64,128]{2,1,0:T(8,128)S(1)}, f32[2,64,128]{2,1,0:T(8,128)S(1)}, u32[]{:S(2)}, u32[]{:S(2)}) collective-permute-start(f32[2,64,128]{2,1,0:T(8,128)S(1)} %pad_maximum_fusion.both_ref), channel_id=1, source_target_pairs={{0,16},{8,24},{16,0},{24,8},{32,48},{40,56},{48,32},{56,40},{64,80... | collective-permute-start | bytes 196616 | tf_op jit(solution)/shard_map/ppermute | solution.py:683
  121.2 4.3 %collective-permute-start.16 = (f32[2,64,128]{2,1,0:T(8,128)S(1)}, f32[2,64,128]{2,1,0:T(8,128)S(1)}, u32[]{:S(2)}, u32[]{:S(2)}) collective-permute-start(f32[2,64,128]{2,1,0:T(8,128)S(1)} %pad_maximum_fusion.both_ref), channel_id=1, source_target_pairs={{0,24},{8,16},{16,8},{24,0},{32,56},{40,48},{48,40},{56,32},{64,88... | collective-permute-start | bytes 196616 | tf_op jit(solution)/shard_map/ppermute | solution.py:683
  122.2 3.3 %collective-permute-start.15 = (f32[2,64,128]{2,1,0:T(8,128)S(1)}, f32[2,64,128]{2,1,0:T(8,128)S(1)}, u32[]{:S(2)}, u32[]{:S(2)}) collective-permute-start(f32[2,64,128]{2,1,0:T(8,128)S(1)} %pad_maximum_fusion.both_ref), channel_id=1, source_target_pairs={{0,8},{8,0},{16,24},{24,16},{32,40},{40,32},{48,56},{56,48},{64,72... | collective-permute-start | bytes 196616 | tf_op jit(solution)/shard_map/ppermute | solution.py:683
